TPU v7x, 512 devices: a whole 4x8x8 slice. The times are simulated.
512 devices in a mesh: gx: 4 (over z_hi, core), gy: 8 (over y), gz: 16 (over x, z_lo).
Axes of the slice: x: 4, y: 8, z: 8 (z_hi: 2, z_lo: 4; z = z_hi * 4 + z_lo), core: 2. Of those that a mesh axis runs over, the one named last changes fastest.
Arguments:
- features: bfloat16 [32, 64, 2048, 128], P('gx', 'gy', 'gz'), may hold values from -6 to 6
- positions: float32 [3, 32, 64, 2048], P(None, 'gx', 'gy', 'gz'), may hold values from 0 to 1
- box_counts: int32 [32, 64, 64], P('gx', 'gy', 'gz'), may hold values from 1 to 32, as said below
- w_hidden: bfloat16 [128, 128], replicated, may hold values from -0.5 to 0.5
- w_charge: bfloat16 [128], replicated, may hold values from -0.5 to 0.5
- wave_numbers: float32 [3, 128], replicated, may hold values from -24 to 24
- phases: float32 [128], replicated, may hold values from -3.140625 to 3.140625
- upward: bfloat16 [2, 8, 128, 128], replicated, may hold values from -0.1875 to 0.1875
- downward: bfloat16 [2, 8, 128, 128], replicated, may hold values from -0.5 to 0.5
- transfer: bfloat16 [3, 128, 128], replicated, may hold values from -0.5 to 0.5
- out_scale: float32 [3, 343, 128], replicated, may hold values from -0.018 to 0.018
- in_scale: float32 [3, 343, 128], replicated, may hold values from 0.5 to 2
Outputs:
- forces: float32 [3, 32, 64, 2048], P(None, 'gx', 'gy', 'gz')
- virial: float32 [3, 3], replicated
Inputs may be any that keep to these rules, and one draw needn't show every extreme that they name: `box_counts`: the live atoms of a box fill its first slots; some box holds 32 atoms.
All inputs are finite; a program needn't handle non-finite values.
Results may differ from a plain program's by a relative error of at most 0.012.
Values sent between devices are 32-bit elements; how exact they have to be, the bound alone decides.
No kernel may reach another device: no remote copies, remote signals or barrier semaphores. Data moves between devices by JAX's collectives and lax.ppermute only.
A program may use at most 64 MiB of HBM per device.

v0:
```python
import math

import jax
import jax.numpy as jnp
import numpy as np
from jax import lax
from jax.sharding import PartitionSpec as P


def padded_2(block, sides, width):
    for axis, dim in sides:
        count = lax.axis_size(axis)
        forward = [(i, i + 1) for i in range(count - 1)]
        forward.append((count - 1, 0))
        backward = [(target, source) for source, target in forward]
        low = lax.ppermute(
            lax.slice_in_dim(block, block.shape[dim] - width, None, axis=dim), axis, forward
        )
        high = lax.ppermute(lax.slice_in_dim(block, 0, width, axis=dim), axis, backward)
        block = jnp.concatenate([low, block, high], axis=dim)
    return block


def shifted(value, axis, steps):
    count = lax.axis_size(axis)
    pairs = [(source, (source + steps) % count) for source in range(count)]
    return lax.ppermute(value, axis, pairs)


def offset_tables():
    index_rows = np.zeros((216, 8), np.int32)
    keep_rows = np.zeros((216, 8), np.float32)
    for along_x in range(6):
        for along_y in range(6):
            for along_z in range(6):
                row = (along_x * 6 + along_y) * 6 + along_z
                for child in range(8):
                    delta_x = along_x - 2 - child // 4
                    delta_y = along_y - 2 - child // 2 % 2
                    delta_z = along_z - 2 - child % 2
                    index_rows[row, child] = (delta_x + 3) * 49 + (delta_y + 3) * 7 + delta_z + 3
                    near = abs(delta_x) <= 1 and abs(delta_y) <= 1 and (abs(delta_z) <= 1)
                    keep_rows[row, child] = 0.0 if near else 1.0
    return (index_rows, keep_rows)


def translate(padded, out_table, in_table, transfer_level):
    width_x = padded.shape[0] - 4
    width_y = padded.shape[1] - 4
    width_z = padded.shape[2] - 4
    coeffs = padded.shape[3]
    half_x, half_y, half_z = (width_x // 2, width_y // 2, width_z // 2)
    parents = half_x * half_y * half_z
    parity = padded.reshape(half_x + 2, 2, half_y + 2, 2, half_z + 2, 2, coeffs)
    parity = parity.transpose(1, 3, 5, 0, 2, 4, 6)
    index_rows, keep_rows = offset_tables()
    flat = index_rows.reshape(-1)
    in_rows = jnp.take(in_table, flat, axis=0).reshape(6, 36, 8, coeffs) * jnp.asarray(
        keep_rows
    ).reshape(6, 36, 8, 1)
    out_rows = jnp.take(out_table, flat, axis=0).reshape(6, 36, 8, coeffs)

    def add_plane(along_x, total):
        plane = lax.dynamic_index_in_dim(parity, along_x % 2, 0, keepdims=False)
        plane = lax.dynamic_slice_in_dim(plane, along_x // 2, half_x, 2)
        pieces = []
        for along_y in range(6):
            for along_z in range(6):
                grid = plane[along_y % 2, along_z % 2]
                grid = lax.slice(
                    grid,
                    (0, along_y // 2, along_z // 2, 0),
                    (half_x, along_y // 2 + half_y, along_z // 2 + half_z, coeffs),
                )
                pieces.append(grid.reshape(parents, coeffs))
        sources = jnp.stack(pieces)
        scaled = lax.dynamic_index_in_dim(in_rows, along_x, 0, keepdims=False)
        outer = lax.dynamic_index_in_dim(out_rows, along_x, 0, keepdims=False)
        operand = (sources[:, None] * scaled[:, :, None, :]).astype(jnp.bfloat16)
        image = jnp.dot(
            operand.reshape(-1, coeffs), transfer_level, preferred_element_type=jnp.float32
        )
        image = image.reshape(36, 8, parents, coeffs) * outer[:, :, None, :]
        return total + jnp.sum(image, axis=0)

    total = lax.fori_loop(0, 6, add_plane, jnp.zeros((8, parents, coeffs), jnp.float32))
    total = total.reshape(2, 2, 2, half_x, half_y, half_z, coeffs)
    return total.transpose(3, 0, 4, 1, 5, 2, 6).reshape(width_x, width_y, width_z, coeffs)


def phase_terms(place, wave_numbers, phases):
    centered = place - 0.5
    return (
        phases
        + centered[0][..., None] * wave_numbers[0]
        + centered[1][..., None] * wave_numbers[1]
        + centered[2][..., None] * wave_numbers[2]
    )


def lift(moments, upward_level):
    grid_x, grid_y, grid_z, coeffs = moments.shape
    children = moments.astype(jnp.bfloat16).reshape(
        grid_x // 2, 2, grid_y // 2, 2, grid_z // 2, 2, coeffs
    )
    children = children.transpose(0, 2, 4, 1, 3, 5, 6).reshape(-1, 8 * coeffs)
    parent = jnp.dot(
        children, upward_level.reshape(8 * coeffs, coeffs), preferred_element_type=jnp.float32
    )
    return parent.reshape(grid_x // 2, grid_y // 2, grid_z // 2, coeffs)


def descend(local, downward_level):
    grid_x, grid_y, grid_z, coeffs = local.shape
    table = downward_level.transpose(1, 0, 2).reshape(coeffs, 8 * coeffs)
    spread = jnp.dot(local.reshape(-1, coeffs), table, preferred_element_type=jnp.float32)
    spread = spread.reshape(grid_x, grid_y, grid_z, 2, 2, 2, coeffs).transpose(0, 3, 1, 4, 2, 5, 6)
    return spread.reshape(2 * grid_x, 2 * grid_y, 2 * grid_z, coeffs)


def grow(brick, dim, width, mover):
    size = brick.shape[dim]
    reach = -(-width // size)
    lower = jnp.concatenate([mover(brick, hop) for hop in range(reach, 0, -1)], axis=dim)
    upper = jnp.concatenate([mover(brick, -hop) for hop in range(1, reach + 1)], axis=dim)
    lower = lax.slice_in_dim(lower, lower.shape[dim] - width, lower.shape[dim], 1, dim)
    upper = lax.slice_in_dim(upper, 0, width, 1, dim)
    return jnp.concatenate([lower, brick, upper], axis=dim)


def shards(
    features,
    positions,
    box_counts,
    w_hidden,
    w_charge,
    wave_numbers,
    phases,
    upward,
    downward,
    transfer,
    out_scale,
    in_scale,
):
    side_x, side_y, side_z = box_counts.shape
    slots = features.shape[2] // side_z
    coeffs = wave_numbers.shape[1]
    rows = features.reshape(-1, features.shape[3])
    hidden = jax.nn.silu(jnp.dot(rows, w_hidden, preferred_element_type=jnp.float32)).astype(
        jnp.bfloat16
    )
    charge = jnp.dot(hidden, w_charge, preferred_element_type=jnp.float32).reshape(
        side_x, side_y, side_z * slots
    )
    slot_index = jnp.arange(side_z * slots, dtype=jnp.int32) % slots
    live = (slot_index < jnp.repeat(box_counts, slots, axis=2)).astype(jnp.float32)
    charge = charge * live
    angle = phase_terms(positions, wave_numbers, phases)
    moments = (
        (charge[..., None] * jnp.cos(angle))
        .reshape(side_x, side_y, side_z, slots, coeffs)
        .sum(axis=3)
    )
    middle = lift(moments, upward[0])
    padded = padded_2(moments, (("gx", 0), ("gy", 1), ("gz", 2)), 2)
    padded_mid = padded_2(middle, (("gx", 0), ("gy", 1), ("gz", 2)), 2)
    top = lift(middle, upward[1])
    size_x, size_y, size_z = (top.shape[0], top.shape[1], top.shape[2])
    start_x = lax.axis_index("gx") * size_x
    start_y = lax.axis_index("gy") * size_y
    start_z = lax.axis_index("gz") * size_z
    parity_x = start_x % 2
    parity_y = start_y % 2
    parity_z = start_z % 2
    span_x = size_x + size_x % 2 + 4
    span_y = size_y + size_y % 2 + 4
    span_z = size_z + size_z % 2 + 4
    window = grow(top, 0, 3, lambda piece, hop: shifted(piece, "gx", hop))
    window = grow(window, 1, 3, lambda piece, hop: shifted(piece, "gy", hop))
    window = grow(window, 2, 3, lambda piece, hop: shifted(piece, "gz", hop))
    window = lax.dynamic_slice(
        window, (1 - parity_x, 1 - parity_y, 1 - parity_z, 0), (span_x, span_y, span_z, coeffs)
    )
    far_top = translate(window, out_scale[2], in_scale[2], transfer[2])
    local_top = lax.dynamic_slice(
        far_top, (parity_x, parity_y, parity_z, 0), (size_x, size_y, size_z, coeffs)
    ).astype(jnp.bfloat16)
    local_mid = (
        translate(padded_mid, out_scale[1], in_scale[1], transfer[1])
        + descend(local_top, downward[1])
    ).astype(jnp.bfloat16)
    local_leaf = translate(padded, out_scale[0], in_scale[0], transfer[0]) + descend(
        local_mid, downward[0]
    )
    weight = (charge[..., None] * jnp.sin(angle)).reshape(
        side_x, side_y, side_z, slots, coeffs
    ) * local_leaf[:, :, :, None, :]
    forces = jnp.einsum("xyzsk,dk->dxyzs", weight, wave_numbers, precision=lax.Precision.HIGHEST)
    forces = forces.reshape(3, side_x, side_y, side_z * slots)
    total_x = side_x * lax.axis_size("gx")
    total_y = side_y * lax.axis_size("gy")
    total_z = side_z * lax.axis_size("gz")
    box_x = (lax.axis_index("gx") * side_x + jnp.arange(side_x, dtype=jnp.int32)).astype(
        jnp.float32
    )
    box_y = (lax.axis_index("gy") * side_y + jnp.arange(side_y, dtype=jnp.int32)).astype(
        jnp.float32
    )
    box_z = (
        lax.axis_index("gz") * side_z + jnp.arange(side_z * slots, dtype=jnp.int32) // slots
    ).astype(jnp.float32)
    place_x = (box_x[:, None, None] + positions[0]) / total_x
    place_y = (box_y[None, :, None] + positions[1]) / total_y
    place_z = (box_z[None, None, :] + positions[2]) / total_z
    place = jnp.stack([place_x, place_y, place_z])
    partial_virial = jnp.einsum("dxyn,exyn->de", place, forces, precision=lax.Precision.HIGHEST)
    atom_total = total_x * total_y * total_z * slots
    virial = lax.psum(partial_virial, ("gx", "gy", "gz")) * (1.0 / math.sqrt(atom_total))
    return (forces, virial)


def solution(mesh):
    in_specs = (
        P("gx", "gy", "gz", None),
        P(None, "gx", "gy", "gz"),
        P("gx", "gy", "gz"),
        P(),
        P(),
        P(),
        P(),
        P(),
        P(),
        P(),
        P(),
        P(),
    )
    out_specs = (P(None, "gx", "gy", "gz"), P())
    return jax.shard_map(shards, mesh=mesh, in_specs=in_specs, out_specs=out_specs, check_vma=False)
```

profile of v0, /device:TPU:1, one launch (start us, length us, event | category | flops | bytes accessed | tf_op | source)
XLA Modules:
  0.0 361.5 jit_solution(3201141669808662308)
XLA Ops:
  5.6 30.8 %multiply_reduce_fusion.1 = f32[8,8,4,128]{3,2,1,0:T(4,128)S(1)} fusion(f32[128]{0:T(128)S(1)} %get-tuple-element.871, f32[8,8,4,32]{3,2,1,0:T(4,128)S(1)} %mul.347, f32[128]{0:T(128)S(1)} %get-tuple-element.870, f32[8,8,4,32]{3,2,1,0:T(4,128)S(1)} %mul.342, f32[128]{0:T(128)S(1)} %get-tuple-element.869, f32[8,8,4,32]{3,2,1,0:T(4,128)S(1)} %mul.337, ...), kind=kLoop, calls=%fused_computation.198 | loop fusion | flops 8355840 | bytes 264192 | tf_op jit(solution)/shard_map/reduce_sum | solution.py:162
  38.6 11.5 %collective-permute-start.12 = (f32[2,2,1,128]{3,1,0,2:T(2,128)}, f32[2,2,1,128]{3,1,0,2:T(2,128)}, u32[]{:S(2)}, u32[]{:S(2)}) collective-permute-start(f32[2,2,1,128]{3,1,0,2:T(2,128)} %convolution_bitcast_fusion.3), channel_id=1, source_target_pairs={{0,256},{128,384},{256,0},{384,128},{1,257},{129,385},{257,1},{385... | collective-permute-start | bytes 6152 | tf_op jit(solution)/shard_map/ppermute | solution.py:27
  50.0 4.8 %collective-permute-start.13 = (f32[2,2,1,128]{3,1,0,2:T(2,128)}, f32[2,2,1,128]{3,1,0,2:T(2,128)}, u32[]{:S(2)}, u32[]{:S(2)}) collective-permute-start(f32[2,2,1,128]{3,1,0,2:T(2,128)} %convolution_bitcast_fusion.3), channel_id=1, source_target_pairs={{0,128},{128,256},{256,384},{384,0},{1,129},{129,257},{257,385},{3... | collective-permute-start | bytes 6152 | tf_op jit(solution)/shard_map/ppermute | solution.py:27
  57.4 7.5 %collective-permute-start.6 = (f32[2,4,2,128]{3,1,2,0:T(4,128)}, f32[2,4,2,128]{3,1,2,0:T(4,128)}, u32[]{:S(2)}, u32[]{:S(2)}) collective-permute-start(f32[2,4,2,128]{3,1,2,0:T(4,128)} %copy.97), channel_id=1, source_target_pairs={{0,128},{128,256},{256,384},{384,0},{1,129},{129,257},{257,385},{3... | collective-permute-start | bytes 24584 | tf_op jit(solution)/shard_map/ppermute | solution.py:16
  68.2 3.3 gather_fusion.2
  71.4 4.2 %gather_fusion.4 = f32[1728,128]{1,0:T(8,128)} fusion(f32[343,128]{1,0:T(8,128)S(1)} %get-tuple-element.838, s32[2048]{0:T(1024)S(1)} %pad_clamp_fusion), kind=kCustom, calls=%fused_computation.4.clone | custom fusion | bytes 1776384 | tf_op jit(solution)/shard_map/jit(_take)/gather | solution.py:58
  75.7 4.2 %gather_fusion = f32[1728,128]{1,0:T(8,128)} fusion(f32[343,128]{1,0:T(8,128)S(1)} %get-tuple-element.839, s32[2048]{0:T(1024)S(1)} %pad_clamp_fusion), kind=kCustom, calls=%fused_computation.clone | custom fusion | bytes 1776384 | tf_op jit(solution)/shard_map/jit(_take)/gather | solution.py:58
  85.9 3.4 broadcast_multiply_fusion
  89.3 4.2 %gather_fusion.5 = f32[1728,128]{1,0:T(8,128)} fusion(f32[343,128]{1,0:T(8,128)S(1)} %get-tuple-element.835, s32[2048]{0:T(1024)S(1)} %pad_clamp_fusion), kind=kCustom, calls=%fused_computation.5.clone | custom fusion | bytes 1776384 | tf_op jit(solution)/shard_map/jit(_take)/gather | solution.py:61
  93.5 4.2 %gather_fusion.3 = f32[1728,128]{1,0:T(8,128)} fusion(f32[343,128]{1,0:T(8,128)S(1)} %get-tuple-element.837, s32[2048]{0:T(1024)S(1)} %pad_clamp_fusion), kind=kCustom, calls=%fused_computation.3.clone | custom fusion | bytes 1776384 | tf_op jit(solution)/shard_map/jit(_take)/gather | solution.py:61
  98.0 4.2 %gather_fusion.1 = f32[1728,128]{1,0:T(8,128)} fusion(f32[343,128]{1,0:T(8,128)S(1)} %get-tuple-element.836, s32[2048]{0:T(1024)S(1)} %pad_clamp_fusion), kind=kCustom, calls=%fused_computation.1.clone | custom fusion | bytes 1776384 | tf_op jit(solution)/shard_map/jit(_take)/gather | solution.py:61
  103.0 7.5 %collective-permute-start = (f32[2,8,4,128]{3,2,1,0:T(4,128)S(1)}, f32[2,8,4,128]{3,2,1,0:T(4,128)S(1)}, u32[]{:S(2)}, u32[]{:S(2)}) collective-permute-start(f32[2,8,4,128]{3,2,1,0:T(4,128)S(1)} %copy-done.22), channel_id=1, source_target_pairs={{0,128},{128,256},{256,384},{384,0},{1,129},{129,257},{257,385},{3... | collective-permute-start | bytes 98312 | tf_op jit(solution)/shard_map/ppermute | solution.py:16
  113.9 3.2 collective-permute-start.16
  117.1 3.3 collective-permute-start.17
  121.2 4.3 %collective-permute-start.18 = (f32[8,2,1,128]{3,1,0,2:T(2,128)S(1)}, f32[8,2,1,128]{3,1,0,2:T(2,128)S(1)}, u32[]{:S(2)}, u32[]{:S(2)}) collective-permute-start(f32[8,2,1,128]{3,1,0,2:T(2,128)S(1)} %pad_maximum_fusion.10), channel_id=1, source_target_pairs={{0,96},{16,112},{32,0},{48,16},{64,32},{80,48},{96,64},{112,80},{1... | collective-permute-start | bytes 24584 | tf_op jit(solution)/shard_map/ppermute | solution.py:27
  128.1 2.4 collective-permute-start.8
  130.5 4.1 %collective-permute-start.9 = (f32[8,2,2,128]{3,1,2,0:T(2,128)S(1)}, f32[8,2,2,128]{3,1,2,0:T(2,128)S(1)}, u32[]{:S(2)}, u32[]{:S(2)}) collective-permute-start(f32[8,2,2,128]{3,1,2,0:T(2,128)S(1)} %get-tuple-element.864), channel_id=1, source_target_pairs={{16,0},{32,16},{48,32},{64,48},{80,64},{96,80},{112,96},{0,112},{1... | collective-permute-start | bytes 49160 | tf_op jit(solution)/shard_map/ppermute | solution.py:19
  135.3 4.4 %collective-permute-start.19 = (f32[8,8,1,128]{3,1,0,2:T(8,128)S(1)}, f32[8,8,1,128]{3,1,0,2:T(8,128)S(1)}, u32[]{:S(2)}, u32[]{:S(2)}) collective-permute-start(f32[8,8,1,128]{3,1,0,2:T(8,128)S(1)} %fusion.37), channel_id=1, source_target_pairs={{0,3},{1,4},{2,5},{3,6},{4,7},{5,8},{6,9},{7,10},{8,11},{9,12},{10... | collective-permute-start | bytes 98312 | tf_op jit(solution)/shard_map/ppermute | solution.py:27
  139.7 2.2 collective-permute-start.20
  142.0 3.1 collective-permute-start.21
  145.7 6.1 %collective-permute-start.22 = (f32[8,8,1,128]{3,1,0,2:T(8,128)S(1)}, f32[8,8,1,128]{3,1,0,2:T(8,128)S(1)}, u32[]{:S(2)}, u32[]{:S(2)}) collective-permute-start(f32[8,8,1,128]{3,1,0,2:T(8,128)S(1)} %fusion.37), channel_id=1, source_target_pairs={{0,15},{1,0},{2,1},{3,2},{4,3},{5,4},{6,5},{7,6},{8,7},{9,8},{10,9... | collective-permute-start | bytes 98312 | tf_op jit(solution)/shard_map/ppermute | solution.py:27
  151.8 2.2 collective-permute-start.23
  154.7 2.9 collective-permute-start.24
  157.6 4.0 %collective-permute-start.10 = (f32[8,8,2,128]{3,1,2,0:T(8,128)}, f32[8,8,2,128]{3,1,2,0:T(8,128)}, u32[]{:S(2)}, u32[]{:S(2)}) collective-permute-start(f32[8,8,2,128]{3,1,2,0:T(8,128)} %pad_maximum_fusion.4), channel_id=1, source_target_pairs={{0,1},{1,2},{2,3},{3,4},{4,5},{5,6},{6,7},{7,8},{8,9},{9,10},{10,1... | collective-permute-start | bytes 196616 | tf_op jit(solution)/shard_map/ppermute | solution.py:16
  161.6 5.2 %collective-permute-start.11 = (f32[8,8,2,128]{3,1,2,0:T(8,128)}, f32[8,8,2,128]{3,1,2,0:T(8,128)}, u32[]{:S(2)}, u32[]{:S(2)}) collective-permute-start(f32[8,8,2,128]{3,1,2,0:T(8,128)} %pad_maximum_fusion.4), channel_id=1, source_target_pairs={{1,0},{2,1},{3,2},{4,3},{5,4},{6,5},{7,6},{8,7},{9,8},{10,9},{11,1... | collective-permute-start | bytes 196616 | tf_op jit(solution)/shard_map/ppermute | solution.py:19
  168.8 4.6 %collective-permute-start.3 = (f32[12,2,4,128]{3,2,1,0:T(4,128)S(1)}, f32[12,2,4,128]{3,2,1,0:T(4,128)S(1)}, u32[]{:S(2)}, u32[]{:S(2)}) collective-permute-start(f32[12,2,4,128]{3,2,1,0:T(4,128)S(1)} %get-tuple-element.848), channel_id=1, source_target_pairs={{16,0},{32,16},{48,32},{64,48},{80,64},{96,80},{112,96},{0,112},{1... | collective-permute-start | bytes 147464 | tf_op jit(solution)/shard_map/ppermute | solution.py:19
  173.6 10.5 %while.53 = (s32[]{:T(128)}, f32[8,1,128]{2,1,0:T(1,128)S(1)}, f32[2,2,2,3,3,3,128]{6,1,4,0,3,2,5:T(2,128)S(1)}, f32[6,36,8,128]{3,2,1,0:T(8,128)}, bf16[128,128...) while((s32[]{:T(128)}, f32[8,1,128]{2,1,0:T(1,128)S(1)}, ...), condition=%wide.region_9.11_spmd.clone, body=%wide.region_7.10_spmd.clone.sunk | while | flops 9585687 | bytes 548182 | solution.py:86
  186.9 7.5 %collective-permute-start.5 = (f32[12,12,2,128]{3,2,1,0:T(2,128)}, f32[12,12,2,128]{3,2,1,0:T(2,128)}, u32[]{:S(2)}, u32[]{:S(2)}) collective-permute-start(f32[12,12,2,128]{3,2,1,0:T(2,128)} %get-tuple-element.846), channel_id=1, source_target_pairs={{1,0},{2,1},{3,2},{4,3},{5,4},{6,5},{7,6},{8,7},{9,8},{10,9},{11,1... | collective-permute-start | bytes 442376 | tf_op jit(solution)/shard_map/ppermute | solution.py:19
  195.4 11.2 %while.52 = (s32[]{:T(128)}, f32[8,4,128]{2,0,1:T(8,128)S(1)}, f32[2,2,2,4,4,3,128]{6,1,4,2,5,0,3:T(2,128)S(1)}, f32[6,36,8,128]{3,2,1,0:T(8,128)}, bf16[128,128...) while((s32[]{:T(128)}, f32[8,4,128]{2,0,1:T(8,128)S(1)}, ...), condition=%wide.region_6.8_spmd.clone, body=%wide.region_4.7_spmd.clone.sunk | while | flops 38342676 | bytes 1646938 | solution.py:86
  208.1 16.4 %while.51 = (s32[]{:T(128)}, f32[8,32,128]{2,1,0:T(8,128)S(1)}, f32[2,2,2,6,6,4,128]{6,2,5,1,4,0,3:T(2,128)S(1)}, f32[6,36,8,128]{3,2,1,0:T(8,128)}, bf16[128,12...) while((s32[]{:T(128)}, f32[8,32,128]{2,1,0:T(8,128)S(1)}, ...), condition=%wide.region_3.5_spmd.clone, body=%wide.region_1.4_spmd.clone.sunk | while | flops 306741280 | bytes 5570906 | solution.py:86
  225.8 33.5 %fusion.29 = f32[3,8,8,4,32]{4,0,3,2,1:T(4,128)S(1)} fusion(f32[8,8,4,128]{3,2,1,0:T(4,128)S(1)} %copy.111, f32[128]{0:T(128)S(1)} %copy-done.31, f32[8,8,4,32]{3,2,1,0:T(4,128)} %copy-done.17, f32[128]{0:T(128)S(1)} %copy-done.29, f32[8,8,4,32]{3,2,1,0:T(4,128)} %copy-done.16, f32[128]{0:T(128)S(1)} %copy-done.27, f32[8,8,4,32]{3,2,1,0:T(4,128)S(1)} %copy-done.15, ...), kind=kOutput, calls=%fused_computation.213 | convolution fusion | flops 46137344 | bytes 364032 | tf_op jit(solution)/shard_map/xyzsk,dk->dxyzs/dot_general | solution.py:198
  260.4 100.5 %psum.7 = f32[3,3]{1,0:T(4,128)S(1)} all-reduce(f32[3,3]{1,0:T(4,128)S(1)} %convolution_bitcast_fusion.2), channel_id=1, replica_groups=mesh['gx'=4,'gy'=8,'gz'=16] {'gx','gy','gz'}, use_global_device_ids=true, to_apply=%region_10.12 | all-reduce | flops 9 | bytes 72 | tf_op jit(solution)/shard_map/psum | solution.py:218
  (948 shorter events, 71.9 us)
Async XLA Ops:
  5.5 31.0 %copy-start.18 = (f32[8,8,4,32]{3,2,1,0:T(4,128)}, f32[8,8,4,32]{3,2,1,0:T(4,128)S(1)}, u32[]{:S(2)}) copy-start(f32[8,8,4,32]{3,2,1,0:T(4,128)S(1)} %compare_select_fusion) | copy-start | bytes 98308
  5.6 62.5 %copy-start.24 = (s32[1728]{0:T(1024)S(1)}, s32[1728]{0:T(1024)}, u32[]{:S(2)}) copy-start(s32[1728]{0:T(1024)} %constant.693) | copy-start | bytes 20740
  5.6 62.5 %copy-start.7 = (f32[3,343,128]{2,1,0:T(8,128)S(1)}, f32[3,343,128]{2,1,0:T(8,128)}, u32[]{:S(2)}) copy-start(f32[3,343,128]{2,1,0:T(8,128)} %param.37) | copy-start | bytes 1580548
  36.4 31.7 %copy-start.1 = (f32[8,8,4,128]{3,2,1,0:T(4,128)}, f32[8,8,4,128]{3,2,1,0:T(4,128)S(1)}, u32[]{:S(2)}) copy-start(f32[8,8,4,128]{3,2,1,0:T(4,128)S(1)} %multiply_reduce_fusion.1) | copy-start | bytes 393220
  38.6 64.5 %collective-permute-start.12 = (f32[2,2,1,128]{3,1,0,2:T(2,128)}, f32[2,2,1,128]{3,1,0,2:T(2,128)}, u32[]{:S(2)}, u32[]{:S(2)}) collective-permute-start(f32[2,2,1,128]{3,1,0,2:T(2,128)} %convolution_bitcast_fusion.3), channel_id=1, source_target_pairs={{0,256},{128,384},{256,0},{384,128},{1,257},{129,385},{257,1},{385... | collective-permute-start | bytes 6152 | tf_op jit(solution)/shard_map/ppermute | solution.py:27
  50.0 60.5 %collective-permute-start.13 = (f32[2,2,1,128]{3,1,0,2:T(2,128)}, f32[2,2,1,128]{3,1,0,2:T(2,128)}, u32[]{:S(2)}, u32[]{:S(2)}) collective-permute-start(f32[2,2,1,128]{3,1,0,2:T(2,128)} %convolution_bitcast_fusion.3), channel_id=1, source_target_pairs={{0,128},{128,256},{256,384},{384,0},{1,129},{129,257},{257,385},{3... | collective-permute-start | bytes 6152 | tf_op jit(solution)/shard_map/ppermute | solution.py:27
  54.8 55.8 %collective-permute-start.14 = (f32[2,2,1,128]{3,1,0,2:T(2,128)}, f32[2,2,1,128]{3,1,0,2:T(2,128)}, u32[]{:S(2)}, u32[]{:S(2)}) collective-permute-start(f32[2,2,1,128]{3,1,0,2:T(2,128)} %convolution_bitcast_fusion.3), channel_id=1, source_target_pairs={{0,384},{128,0},{256,128},{384,256},{1,385},{129,1},{257,129},{385... | collective-permute-start | bytes 6152 | tf_op jit(solution)/shard_map/ppermute | solution.py:27
  57.4 59.8 %collective-permute-start.6 = (f32[2,4,2,128]{3,1,2,0:T(4,128)}, f32[2,4,2,128]{3,1,2,0:T(4,128)}, u32[]{:S(2)}, u32[]{:S(2)}) collective-permute-start(f32[2,4,2,128]{3,1,2,0:T(4,128)} %copy.97), channel_id=1, source_target_pairs={{0,128},{128,256},{256,384},{384,0},{1,129},{129,257},{257,385},{3... | collective-permute-start | bytes 24584 | tf_op jit(solution)/shard_map/ppermute | solution.py:16
  65.5 55.6 %collective-permute-start.7 = (f32[2,4,2,128]{3,1,2,0:T(4,128)}, f32[2,4,2,128]{3,1,2,0:T(4,128)}, u32[]{:S(2)}, u32[]{:S(2)}) collective-permute-start(f32[2,4,2,128]{3,1,2,0:T(4,128)} %copy.98), channel_id=1, source_target_pairs={{128,0},{256,128},{384,256},{0,384},{129,1},{257,129},{385,257},{1... | collective-permute-start | bytes 24584 | tf_op jit(solution)/shard_map/ppermute | solution.py:19
  97.9 56.1 %copy-start.2 = (f32[8,8,4,128]{3,2,1,0:T(4,128)S(1)}, f32[8,8,4,128]{3,2,1,0:T(4,128)}, u32[]{:S(2)}) copy-start(f32[8,8,4,128]{3,2,1,0:T(4,128)} %copy-done.1) | copy-start | bytes 393220
  103.0 42.7 %collective-permute-start = (f32[2,8,4,128]{3,2,1,0:T(4,128)S(1)}, f32[2,8,4,128]{3,2,1,0:T(4,128)S(1)}, u32[]{:S(2)}, u32[]{:S(2)}) collective-permute-start(f32[2,8,4,128]{3,2,1,0:T(4,128)S(1)} %copy-done.22), channel_id=1, source_target_pairs={{0,128},{128,256},{256,384},{384,0},{1,129},{129,257},{257,385},{3... | collective-permute-start | bytes 98312 | tf_op jit(solution)/shard_map/ppermute | solution.py:16
  112.0 14.2 %collective-permute-start.15 = (f32[8,2,1,128]{3,1,0,2:T(2,128)S(1)}, f32[8,2,1,128]{3,1,0,2:T(2,128)S(1)}, u32[]{:S(2)}, u32[]{:S(2)}) collective-permute-start(f32[8,2,1,128]{3,1,0,2:T(2,128)S(1)} %pad_maximum_fusion.10), channel_id=1, source_target_pairs={{0,32},{16,48},{32,64},{48,80},{64,96},{80,112},{96,0},{112,16},{1... | collective-permute-start | bytes 24584 | tf_op jit(solution)/shard_map/ppermute | solution.py:27
  113.9 14.2 %collective-permute-start.16 = (f32[8,2,1,128]{3,1,0,2:T(2,128)S(1)}, f32[8,2,1,128]{3,1,0,2:T(2,128)S(1)}, u32[]{:S(2)}, u32[]{:S(2)}) collective-permute-start(f32[8,2,1,128]{3,1,0,2:T(2,128)S(1)} %pad_maximum_fusion.10), channel_id=1, source_target_pairs={{0,16},{16,32},{32,48},{48,64},{64,80},{80,96},{96,112},{112,0},{1... | collective-permute-start | bytes 24584 | tf_op jit(solution)/shard_map/ppermute | solution.py:27
  117.1 13.4 %collective-permute-start.17 = (f32[8,2,1,128]{3,1,0,2:T(2,128)S(1)}, f32[8,2,1,128]{3,1,0,2:T(2,128)S(1)}, u32[]{:S(2)}, u32[]{:S(2)}) collective-permute-start(f32[8,2,1,128]{3,1,0,2:T(2,128)S(1)} %pad_maximum_fusion.10), channel_id=1, source_target_pairs={{0,112},{16,0},{32,16},{48,32},{64,48},{80,64},{96,80},{112,96},{1... | collective-permute-start | bytes 24584 | tf_op jit(solution)/shard_map/ppermute | solution.py:27
  121.2 13.5 %collective-permute-start.18 = (f32[8,2,1,128]{3,1,0,2:T(2,128)S(1)}, f32[8,2,1,128]{3,1,0,2:T(2,128)S(1)}, u32[]{:S(2)}, u32[]{:S(2)}) collective-permute-start(f32[8,2,1,128]{3,1,0,2:T(2,128)S(1)} %pad_maximum_fusion.10), channel_id=1, source_target_pairs={{0,96},{16,112},{32,0},{48,16},{64,32},{80,48},{96,64},{112,80},{1... | collective-permute-start | bytes 24584 | tf_op jit(solution)/shard_map/ppermute | solution.py:27
  126.2 25.7 %collective-permute-start.1 = (f32[2,8,4,128]{3,2,1,0:T(4,128)S(1)}, f32[2,8,4,128]{3,2,1,0:T(4,128)S(1)}, u32[]{:S(2)}, u32[]{:S(2)}) collective-permute-start(f32[2,8,4,128]{3,2,1,0:T(4,128)S(1)} %copy-done.21), channel_id=1, source_target_pairs={{128,0},{256,128},{384,256},{0,384},{129,1},{257,129},{385,257},{1... | collective-permute-start | bytes 98312 | tf_op jit(solution)/shard_map/ppermute | solution.py:19
  128.1 11.6 %collective-permute-start.8 = (f32[8,2,2,128]{3,1,2,0:T(2,128)S(1)}, f32[8,2,2,128]{3,1,2,0:T(2,128)S(1)}, u32[]{:S(2)}, u32[]{:S(2)}) collective-permute-start(f32[8,2,2,128]{3,1,2,0:T(2,128)S(1)} %get-tuple-element.863), channel_id=1, source_target_pairs={{0,16},{16,32},{32,48},{48,64},{64,80},{80,96},{96,112},{112,0},{1... | collective-permute-start | bytes 49160 | tf_op jit(solution)/shard_map/ppermute | solution.py:16
  130.5 11.4 %collective-permute-start.9 = (f32[8,2,2,128]{3,1,2,0:T(2,128)S(1)}, f32[8,2,2,128]{3,1,2,0:T(2,128)S(1)}, u32[]{:S(2)}, u32[]{:S(2)}) collective-permute-start(f32[8,2,2,128]{3,1,2,0:T(2,128)S(1)} %get-tuple-element.864), channel_id=1, source_target_pairs={{16,0},{32,16},{48,32},{64,48},{80,64},{96,80},{112,96},{0,112},{1... | collective-permute-start | bytes 49160 | tf_op jit(solution)/shard_map/ppermute | solution.py:19
  135.3 19.3 %collective-permute-start.19 = (f32[8,8,1,128]{3,1,0,2:T(8,128)S(1)}, f32[8,8,1,128]{3,1,0,2:T(8,128)S(1)}, u32[]{:S(2)}, u32[]{:S(2)}) collective-permute-start(f32[8,8,1,128]{3,1,0,2:T(8,128)S(1)} %fusion.37), channel_id=1, source_target_pairs={{0,3},{1,4},{2,5},{3,6},{4,7},{5,8},{6,9},{7,10},{8,11},{9,12},{10... | collective-permute-start | bytes 98312 | tf_op jit(solution)/shard_map/ppermute | solution.py:27
  139.7 17.8 %collective-permute-start.20 = (f32[8,8,1,128]{3,1,0,2:T(8,128)S(1)}, f32[8,8,1,128]{3,1,0,2:T(8,128)S(1)}, u32[]{:S(2)}, u32[]{:S(2)}) collective-permute-start(f32[8,8,1,128]{3,1,0,2:T(8,128)S(1)} %fusion.37), channel_id=1, source_target_pairs={{0,2},{1,3},{2,4},{3,5},{4,6},{5,7},{6,8},{7,9},{8,10},{9,11},{10,... | collective-permute-start | bytes 98312 | tf_op jit(solution)/shard_map/ppermute | solution.py:27
  142.0 19.7 %collective-permute-start.21 = (f32[8,8,1,128]{3,1,0,2:T(8,128)S(1)}, f32[8,8,1,128]{3,1,0,2:T(8,128)S(1)}, u32[]{:S(2)}, u32[]{:S(2)}) collective-permute-start(f32[8,8,1,128]{3,1,0,2:T(8,128)S(1)} %fusion.37), channel_id=1, source_target_pairs={{0,1},{1,2},{2,3},{3,4},{4,5},{5,6},{6,7},{7,8},{8,9},{9,10},{10,1... | collective-permute-start | bytes 98312 | tf_op jit(solution)/shard_map/ppermute | solution.py:27
  145.7 21.2 %collective-permute-start.22 = (f32[8,8,1,128]{3,1,0,2:T(8,128)S(1)}, f32[8,8,1,128]{3,1,0,2:T(8,128)S(1)}, u32[]{:S(2)}, u32[]{:S(2)}) collective-permute-start(f32[8,8,1,128]{3,1,0,2:T(8,128)S(1)} %fusion.37), channel_id=1, source_target_pairs={{0,15},{1,0},{2,1},{3,2},{4,3},{5,4},{6,5},{7,6},{8,7},{9,8},{10,9... | collective-permute-start | bytes 98312 | tf_op jit(solution)/shard_map/ppermute | solution.py:27
  151.8 17.0 %collective-permute-start.23 = (f32[8,8,1,128]{3,1,0,2:T(8,128)S(1)}, f32[8,8,1,128]{3,1,0,2:T(8,128)S(1)}, u32[]{:S(2)}, u32[]{:S(2)}) collective-permute-start(f32[8,8,1,128]{3,1,0,2:T(8,128)S(1)} %fusion.37), channel_id=1, source_target_pairs={{0,14},{1,15},{2,0},{3,1},{4,2},{5,3},{6,4},{7,5},{8,6},{9,7},{10,... | collective-permute-start | bytes 98312 | tf_op jit(solution)/shard_map/ppermute | solution.py:27
  154.7 18.8 %collective-permute-start.24 = (f32[8,8,1,128]{3,1,0,2:T(8,128)S(1)}, f32[8,8,1,128]{3,1,0,2:T(8,128)S(1)}, u32[]{:S(2)}, u32[]{:S(2)}) collective-permute-start(f32[8,8,1,128]{3,1,0,2:T(8,128)S(1)} %fusion.37), channel_id=1, source_target_pairs={{0,13},{1,14},{2,15},{3,0},{4,1},{5,2},{6,3},{7,4},{8,5},{9,6},{10... | collective-permute-start | bytes 98312 | tf_op jit(solution)/shard_map/ppermute | solution.py:27
  157.6 36.8 %collective-permute-start.10 = (f32[8,8,2,128]{3,1,2,0:T(8,128)}, f32[8,8,2,128]{3,1,2,0:T(8,128)}, u32[]{:S(2)}, u32[]{:S(2)}) collective-permute-start(f32[8,8,2,128]{3,1,2,0:T(8,128)} %pad_maximum_fusion.4), channel_id=1, source_target_pairs={{0,1},{1,2},{2,3},{3,4},{4,5},{5,6},{6,7},{7,8},{8,9},{9,10},{10,1... | collective-permute-start | bytes 196616 | tf_op jit(solution)/shard_map/ppermute | solution.py:16
  161.6 32.8 %collective-permute-start.11 = (f32[8,8,2,128]{3,1,2,0:T(8,128)}, f32[8,8,2,128]{3,1,2,0:T(8,128)}, u32[]{:S(2)}, u32[]{:S(2)}) collective-permute-start(f32[8,8,2,128]{3,1,2,0:T(8,128)} %pad_maximum_fusion.4), channel_id=1, source_target_pairs={{1,0},{2,1},{3,2},{4,3},{5,4},{6,5},{7,6},{8,7},{9,8},{10,9},{11,1... | collective-permute-start | bytes 196616 | tf_op jit(solution)/shard_map/ppermute | solution.py:19
  166.9 17.2 %collective-permute-start.2 = (f32[12,2,4,128]{3,2,1,0:T(4,128)}, f32[12,2,4,128]{3,2,1,0:T(4,128)S(1)}, u32[]{:S(2)}, u32[]{:S(2)}) collective-permute-start(f32[12,2,4,128]{3,2,1,0:T(4,128)} %get-tuple-element.847), channel_id=1, source_target_pairs={{0,16},{16,32},{32,48},{48,64},{64,80},{80,96},{96,112},{112,0},{1... | collective-permute-start | bytes 147464 | tf_op jit(solution)/shard_map/ppermute | solution.py:16
  168.8 15.2 %collective-permute-start.3 = (f32[12,2,4,128]{3,2,1,0:T(4,128)S(1)}, f32[12,2,4,128]{3,2,1,0:T(4,128)S(1)}, u32[]{:S(2)}, u32[]{:S(2)}) collective-permute-start(f32[12,2,4,128]{3,2,1,0:T(4,128)S(1)} %get-tuple-element.848), channel_id=1, source_target_pairs={{16,0},{32,16},{48,32},{64,48},{80,64},{96,80},{112,96},{0,112},{1... | collective-permute-start | bytes 147464 | tf_op jit(solution)/shard_map/ppermute | solution.py:19
  185.0 21.7 %collective-permute-start.4 = (f32[12,12,2,128]{3,2,1,0:T(2,128)}, f32[12,12,2,128]{3,2,1,0:T(2,128)}, u32[]{:S(2)}, u32[]{:S(2)}) collective-permute-start(f32[12,12,2,128]{3,2,1,0:T(2,128)} %get-tuple-element.845), channel_id=1, source_target_pairs={{0,1},{1,2},{2,3},{3,4},{4,5},{5,6},{6,7},{7,8},{8,9},{9,10},{10,1... | collective-permute-start | bytes 442376 | tf_op jit(solution)/shard_map/ppermute | solution.py:16
  186.9 19.8 %collective-permute-start.5 = (f32[12,12,2,128]{3,2,1,0:T(2,128)}, f32[12,12,2,128]{3,2,1,0:T(2,128)}, u32[]{:S(2)}, u32[]{:S(2)}) collective-permute-start(f32[12,12,2,128]{3,2,1,0:T(2,128)} %get-tuple-element.846), channel_id=1, source_target_pairs={{1,0},{2,1},{3,2},{4,3},{5,4},{6,5},{7,6},{8,7},{9,8},{10,9},{11,1... | collective-permute-start | bytes 442376 | tf_op jit(solution)/shard_map/ppermute | solution.py:19
  225.8 33.9 %copy-start.5 = (f32[3,8,8,128]{3,2,1,0:T(8,128)S(1)}, f32[3,8,8,128]{3,2,1,0:T(8,128)}, u32[]{:S(2)}) copy-start(f32[3,8,8,128]{3,2,1,0:T(8,128)} %pad_maximum_fusion.3) | copy-start | bytes 294916
  259.7 101.8 %copy-start.6 = (f32[3,8,8,128]{3,2,1,0:T(8,128)}, f32[3,8,8,128]{3,2,1,0:T(8,128)S(1)}, u32[]{:S(2)}) copy-start(f32[3,8,8,128]{3,2,1,0:T(8,128)S(1)} %reshape.1502) | copy-start | bytes 294916
  (27 other events, 305.4 us)
where the time goes:
time: 364 us; the launch traced here: 361 us
  starting transfers between devices  102 us (28%)
  blocking collectives  101 us (28%)
  local copies, waits for them, and re-layouts  56.4 us (15%)
  matrix products  52.5 us (14%)
  other arithmetic  43.5 us (12%)
  loops' own time  4.6 us (1%)
    psum x1, blocking collectives, shards(): lax.psum(partial_virial, ('gx', 'gy', 'gz')) * (1.0 / math.sqrt(atom_total))  101 us
    ppermute x13, starting transfers between devices, shifted(): return lax.ppermute(value, axis, pairs)  51.6 us
    dot_general x1, matrix products, shards(): jnp.einsum('xyzsk,dk->dxyzs', weight, wave_numbers, precision=lax.Precisi...  33.5 us
    reduce_sum x1, other arithmetic, shards(): moments = (charge[..., None] * jnp.cos(angle)).reshape(side_x, side_y, si...  30.8 us
    ppermute x6, starting transfers between devices, padded_2(): lax.ppermute(lax.slice_in_dim(block, block.shape[dim] - width, None, axis...  25.3 us
    ppermute x6, starting transfers between devices, padded_2(): lax.ppermute(lax.slice_in_dim(block, 0, width, axis=dim), axis, backward)  25.1 us
    dot_general x18, matrix products, add_plane(): jnp.dot(operand.reshape(-1, coeffs), transfer_level, preferred_element_ty...  13.9 us
    gather x3, local copies, waits for them, and re-layouts, translate(): out_rows = jnp.take(out_table, flat, axis=0).reshape(6, 36, 8, coeffs)  12.7 us
  transfers between devices with their start and end apart: 25, of which 0 were waited for; matrix products, arithmetic and copies ran while one was open for 17% of the time, Pallas kernels for 0%

commit v1 on v0

v1 whole, which is shorter than its diff:
```python
import math

import jax
import jax.numpy as jnp
import numpy as np
from jax import lax
from jax.experimental import pallas as pl
from jax.experimental.pallas import tpu as pltpu
from jax.sharding import PartitionSpec as P

F32 = jnp.float32
BF16 = jnp.bfloat16
TURN = 1.0 / (2.0 * math.pi)
SIN_HALF = (4.4428679, -7.30744342, 3.59478808, -0.78437403)
COS_HALF = (1.4142135, -6.97885099, 5.73946117, -1.88356299, 0.31069819)
NT = (((1,), (1,)), ((), ()))
VMEM = pl.BlockSpec(memory_space=pltpu.VMEM)


def dot(a, b):
    return jnp.dot(a, b, preferred_element_type=F32)


def atoms_kernel(
    feat_hbm, pos_hbm, cnt_ref, wh_hbm, wc_ref, wave_ref, ph_ref, up_hbm,
    charge_ref, sin_ref, leaf_ref, mid_ref, top_ref, sa_ref, sb_ref,
    feat_ref, pos_ref, wh_ref, up_ref, cols_ref, cos_ref, low_ref, plane_sems, sems,
):
    def plane(x):
        return pltpu.make_async_copy(feat_hbm.at[x], feat_ref.at[x], plane_sems.at[x])

    others = [
        pltpu.make_async_copy(wh_hbm, wh_ref, sems.at[0]),
        pltpu.make_async_copy(pos_hbm, pos_ref, sems.at[1]),
        pltpu.make_async_copy(up_hbm, up_ref, sems.at[2]),
    ]
    plane(0).start()
    others[0].start()
    others[1].start()
    for x in range(1, 8):
        plane(x).start()
    others[2].start()

    table = jnp.concatenate(
        [wave_ref[...] * TURN, ph_ref[...] * TURN, jnp.zeros((4, 128), F32)], axis=0
    )
    columns = jnp.concatenate([table] * 16, axis=0).T
    for d in range(4):
        cols_ref[d] = jnp.broadcast_to(columns[:, d : d + 1], (128, 128))
    others[0].wait()
    others[1].wait()

    @pl.loop(0, 8)
    def _(x):
        plane(x).wait()
        atoms_plane(
            x, feat_ref, pos_ref, cnt_ref, wh_ref, wc_ref, charge_ref, sin_ref, leaf_ref,
            cols_ref, cos_ref, low_ref,
        )

    others[2].wait()
    atoms_lift(leaf_ref, up_ref, mid_ref, top_ref, sa_ref, sb_ref)


def atoms_plane(
    step, feat_ref, pos_ref, cnt_ref, wh_ref, wc_ref, charge_ref, sin_ref, leaf_ref,
    cols_ref, cos_ref, low_ref,
):
    lane_box = lax.broadcasted_iota(jnp.int32, (8, 128), 1) // 32
    lane_slot = lax.broadcasted_iota(jnp.int32, (8, 128), 1) % 32
    row_y = lax.broadcasted_iota(jnp.int32, (8, 128), 0)
    counts = jnp.zeros((8, 128), jnp.int32)
    columns = cnt_ref[step].T
    for z in range(4):
        counts = jnp.where(
            lane_box == z, jnp.broadcast_to(columns[:, z : z + 1], (8, 128)), counts
        )
    live = jnp.where(lane_slot < counts, 1.0, 0.0).astype(F32)

    hidden = dot(feat_ref[step].reshape(1024, 128), wh_ref[...])
    half = hidden * 0.5
    hidden = (half + half * jnp.tanh(half)).astype(BF16)
    wc = jnp.broadcast_to(wc_ref[...], (8, 128))
    raw = lax.dot_general(wc, hidden, NT, preferred_element_type=F32)
    charge = jnp.zeros((8, 128), F32)
    for y in range(8):
        charge = jnp.where(row_y == y, raw[:, y * 128 : (y + 1) * 128], charge)
    charge = charge * live
    charge_ref[step] = charge

    spread = []
    for z in range(4):
        spread.append(
            jnp.concatenate(
                [
                    jnp.where((row_y == y) & (lane_box == z), charge, 0.0)
                    for y in range(8)
                ],
                axis=1,
            )
        )
    spread = jnp.concatenate(spread, axis=0)
    spread_high = spread.astype(BF16)
    spread_low = (spread - spread_high.astype(F32)).astype(BF16)

    for y in range(8):
        p0 = pos_ref[0, step, y : y + 1, :] - 0.5
        p1 = pos_ref[1, step, y : y + 1, :] - 0.5
        p2 = pos_ref[2, step, y : y + 1, :] - 0.5
        turns = cols_ref[3] + cols_ref[0] * p0 + cols_ref[1] * p1 + cols_ref[2] * p2
        r = turns - jnp.round(turns)
        u = r * r
        s = SIN_HALF[3]
        for coef in SIN_HALF[2::-1]:
            s = s * u + coef
        s = s * r
        c = COS_HALF[4]
        for coef in COS_HALF[3::-1]:
            c = c * u + coef
        cosine = 1.0 - s * s
        cosine_high = cosine.astype(BF16)
        cos_ref[:, y * 128 : (y + 1) * 128] = cosine_high
        low_ref[:, y * 128 : (y + 1) * 128] = (cosine - cosine_high.astype(F32)).astype(BF16)
        sin_ref[step, :, y * 128 : (y + 1) * 128] = (s * c).astype(BF16)
    moments = lax.dot_general(
        jnp.concatenate([spread_high, spread_low], axis=0), cos_ref[...], NT,
        preferred_element_type=F32,
    )
    fine = lax.dot_general(spread_high, low_ref[...], NT, preferred_element_type=F32)
    moments = moments[0:32] + (moments[32:64] + fine)
    for z in range(4):
        leaf_ref[step, z] = moments[z * 8 : (z + 1) * 8]


def atoms_lift(leaf_ref, up_ref, mid_ref, top_ref, sa_ref, sb_ref):
    total = jnp.zeros((32, 128), F32)
    for child in range(8):
        cx, cy, cz = child // 4, child // 2 % 2, child % 2
        rows = jnp.concatenate(
            [
                leaf_ref[2 * x + cx, 2 * z + cz, pl.ds(cy, 4, stride=2), :]
                for x in range(4)
                for z in range(2)
            ],
            axis=0,
        )
        total = total + dot(rows.astype(BF16), up_ref[0, child])
    for x in range(4):
        for z in range(2):
            for y in range(4):
                row = (x * 2 + z) * 4 + y
                mid_ref[x, y, z : z + 1, :] = total[row : row + 1]
    crown = jnp.zeros((8, 128), F32)
    for child in range(8):
        cx, cy, cz = child // 4, child // 2 % 2, child % 2
        rows = jnp.concatenate(
            [
                mid_ref[2 * x + cx, 2 * y + cy, cz : cz + 1, :]
                for x in range(2)
                for y in range(2)
            ]
            + [jnp.zeros((4, 128), F32)],
            axis=0,
        )
        crown = crown + dot(rows.astype(BF16), up_ref[1, child])
    top_ref[...] = crown[0:4]
    odd = lax.axis_index("gx") % 2
    for ref, high in ((sa_ref, 1 - odd), (sb_ref, odd)):
        for x in range(2):
            for z in range(4):
                row = (x * 4 + z) * 8
                ref[row : row + 8, :] = leaf_ref[high * 6 + x, z]
            for y in range(4):
                row = 64 + (x * 4 + y) * 2
                ref[row : row + 2, :] = mid_ref[high * 2 + x, y]
        ref[80:84, :] = crown[0:4]
        ref[84:88, :] = jnp.zeros((4, 128), F32)


def run_atoms(features, positions, box_counts, w_hidden, w_charge, wave, phases, upward):
    hbm = pl.BlockSpec(memory_space=pltpu.HBM)
    return pl.pallas_call(
        atoms_kernel,
        in_specs=[hbm, hbm, VMEM, hbm, VMEM, VMEM, VMEM, hbm],
        out_specs=[VMEM] * 7,
        out_shape=[
            jax.ShapeDtypeStruct((8, 8, 128), F32),
            jax.ShapeDtypeStruct((8, 128, 1024), BF16),
            jax.ShapeDtypeStruct((8, 4, 8, 128), F32),
            jax.ShapeDtypeStruct((4, 4, 2, 128), F32),
            jax.ShapeDtypeStruct((4, 128), F32),
            jax.ShapeDtypeStruct((88, 128), F32),
            jax.ShapeDtypeStruct((88, 128), F32),
        ],
        scratch_shapes=[
            pltpu.VMEM((8, 8, 128, 128), BF16),
            pltpu.VMEM((3, 8, 8, 128), F32),
            pltpu.VMEM((128, 128), BF16),
            pltpu.VMEM((2, 8, 128, 128), BF16),
            pltpu.VMEM((4, 128, 128), F32),
            pltpu.VMEM((128, 1024), BF16),
            pltpu.VMEM((128, 1024), BF16),
            pltpu.SemaphoreType.DMA((8,)),
            pltpu.SemaphoreType.DMA((3,)),
        ],
        compiler_params=pltpu.CompilerParams(vmem_limit_bytes=58 << 20),
        name="atoms",
    )(features, positions, box_counts, w_hidden, w_charge, wave, phases, upward)


def glue_x_kernel(ra_ref, rb_ref, leaf_ref, mid_ref, top_ref, leafx_ref, midx_ref, topx_ref, ya_ref, yb_ref):
    odd = lax.axis_index("gx") % 2
    leafx_ref[2:10] = leaf_ref[...]
    midx_ref[2:6] = mid_ref[...]
    for ref, high in ((ra_ref, 1 - odd), (rb_ref, odd)):
        for x in range(2):
            for z in range(4):
                row = (x * 4 + z) * 8
                leafx_ref[high * 10 + x, z] = ref[row : row + 8, :]
            for y in range(4):
                row = 64 + (x * 4 + y) * 2
                midx_ref[high * 6 + x, y] = ref[row : row + 2, :]
    ta, tb = ra_ref[80:84, :], rb_ref[80:84, :]
    topx_ref[...] = jnp.concatenate(
        [
            jnp.where(odd == 1, ta, tb),
            top_ref[...],
            jnp.where(odd == 1, tb, ta),
            jnp.zeros((4, 128), F32),
        ],
        axis=0,
    )
    odd_y = lax.axis_index("gy") % 2
    for x in range(12):
        for z in range(4):
            tile = leafx_ref[x, z]
            low, high = tile[0:2], tile[6:8]
            row = (x * 4 + z) * 2
            ya_ref[row : row + 2, :] = jnp.where(odd_y == 1, low, high)
            yb_ref[row : row + 2, :] = jnp.where(odd_y == 1, high, low)
    for ref, side in ((ya_ref, 1 - odd_y), (yb_ref, odd_y)):
        for x in range(8):
            for y in range(2):
                row = 96 + (x * 2 + y) * 2
                ref[row : row + 2, :] = midx_ref[x, side * 2 + y]
        ref[128:144, :] = topx_ref[...]


def glue_x(ra, rb, leaf, mid, top):
    return pl.pallas_call(
        glue_x_kernel,
        in_specs=[VMEM] * 5,
        out_specs=[VMEM] * 5,
        out_shape=[
            jax.ShapeDtypeStruct((12, 4, 8, 128), F32),
            jax.ShapeDtypeStruct((8, 4, 2, 128), F32),
            jax.ShapeDtypeStruct((16, 128), F32),
            jax.ShapeDtypeStruct((144, 128), F32),
            jax.ShapeDtypeStruct((144, 128), F32),
        ],
        compiler_params=pltpu.CompilerParams(vmem_limit_bytes=8 << 20),
        name="glue_x",
    )(ra, rb, leaf, mid, top)


def glue_y_kernel(ra_ref, rb_ref, leafx_ref, midx_ref, topx_ref, leafxy_ref, midxy_ref, topxy_ref, za_ref, zb_ref):
    odd = lax.axis_index("gy") % 2
    for x in range(12):
        for z in range(4):
            row = (x * 4 + z) * 2
            a, b = ra_ref[row : row + 2, :], rb_ref[row : row + 2, :]
            leafxy_ref[x, z, 0:2, :] = jnp.where(odd == 1, a, b)
            leafxy_ref[x, z, 2:10, :] = leafx_ref[x, z]
            leafxy_ref[x, z, 10:12, :] = jnp.where(odd == 1, b, a)
    for x in range(8):
        midxy_ref[x, 2:6] = midx_ref[x]
        for ref, high in ((ra_ref, 1 - odd), (rb_ref, odd)):
            for y in range(2):
                row = 96 + (x * 2 + y) * 2
                midxy_ref[x, high * 6 + y] = ref[row : row + 2, :]
    for x in range(6):
        row = 128 + x * 2
        a, b = ra_ref[row : row + 2, :], rb_ref[row : row + 2, :]
        topxy_ref[x * 6 : x * 6 + 2, :] = jnp.where(odd == 1, a, b)
        topxy_ref[x * 6 + 2 : x * 6 + 4, :] = topx_ref[x * 2 : x * 2 + 2, :]
        topxy_ref[x * 6 + 4 : x * 6 + 6, :] = jnp.where(odd == 1, b, a)
    topxy_ref[36:40, :] = jnp.zeros((4, 128), F32)
    odd_z = lax.axis_index("gz") % 2
    for ref, side in ((za_ref, 1 - odd_z), (zb_ref, odd_z)):
        for x in range(12):
            for z in range(2):
                row = (x * 2 + z) * 12
                ref[row : row + 12, :] = leafxy_ref[x, side * 2 + z]
        for x in range(8):
            for y in range(8):
                row = 288 + (x * 8 + y) * 2
                ref[row : row + 2, :] = midxy_ref[x, y]
    za_ref[416:456, :] = topxy_ref[...]


def glue_y(ra, rb, leafx, midx, topx):
    return pl.pallas_call(
        glue_y_kernel,
        in_specs=[VMEM] * 5,
        out_specs=[VMEM] * 5,
        out_shape=[
            jax.ShapeDtypeStruct((12, 4, 12, 128), F32),
            jax.ShapeDtypeStruct((8, 8, 2, 128), F32),
            jax.ShapeDtypeStruct((40, 128), F32),
            jax.ShapeDtypeStruct((456, 128), F32),
            jax.ShapeDtypeStruct((416, 128), F32),
        ],
        compiler_params=pltpu.CompilerParams(vmem_limit_bytes=8 << 20),
        name="glue_y",
    )(ra, rb, leafx, midx, topx)


def glue_z_kernel(ra_ref, topxy_ref, pair_ref):
    odd = lax.axis_index("gz") % 2
    mine, other = topxy_ref[0:36, :], ra_ref[416:452, :]
    pair_ref[...] = jnp.concatenate(
        [jnp.where(odd == 1, other, mine), jnp.where(odd == 1, mine, other)], axis=0
    )


def glue_z(ra, topxy):
    return pl.pallas_call(
        glue_z_kernel,
        in_specs=[VMEM] * 2,
        out_specs=VMEM,
        out_shape=jax.ShapeDtypeStruct((72, 128), F32),
        compiler_params=pltpu.CompilerParams(vmem_limit_bytes=8 << 20),
        name="glue_z",
    )(ra, topxy)


def block_diagonal(core):
    zero = jnp.zeros((128, 128), BF16)
    return jnp.concatenate(
        [jnp.concatenate([core, zero], axis=1), jnp.concatenate([zero, core], axis=1)], axis=0
    )


def offset_tiles(out_ref, table, cz, masked):
    zero = jnp.zeros((2, 128), F32)
    keep_rows = lax.broadcasted_iota(jnp.int32, (8, 128), 0)
    near = (keep_rows >= 1 + cz) & (keep_rows <= 3 + cz)
    for xy in range(49):
        start = xy * 7 + 1 - cz
        tile = jnp.concatenate([table[start : start + 6, :], zero], axis=0)
        if masked and 2 <= xy // 7 <= 4 and 2 <= xy % 7 <= 4:
            tile = jnp.where(near, 0.0, tile)
        out_ref[xy] = tile


def far_kernel(
    leafxy_ref, midxy_ref, ra_ref, rb_ref, in_ref, out_ref, core_ref,
    far0_ref, far1_ref,
    leaf_ref, mid_ref, scale_ref, tin_ref, tout_ref, acc_ref,
):
    odd = lax.axis_index("gz") % 2
    leaf_ref[:, 2:6] = leafxy_ref[...]
    for ref, high in ((ra_ref, 1 - odd), (rb_ref, odd)):
        for x in range(12):
            for z in range(2):
                row = (x * 2 + z) * 12
                leaf_ref[x, high * 6 + z] = ref[row : row + 12, :]
    for x in range(8):
        for y in range(8):
            row = 288 + (x * 8 + y) * 2
            a, b = ra_ref[row : row + 2, :], rb_ref[row : row + 2, :]
            mid_ref[x, y] = jnp.concatenate(
                [
                    jnp.where(odd == 1, a, b),
                    midxy_ref[x, y],
                    jnp.where(odd == 1, b, a),
                    jnp.zeros((2, 128), F32),
                ],
                axis=0,
            )
    scale_ref[...] = in_ref[0]
    for x in range(2, 5):
        for y in range(2, 5):
            row = x * 49 + y * 7 + 2
            scale_ref[row : row + 3, :] = jnp.zeros((3, 128), F32)
    for cz in range(2):
        offset_tiles(tin_ref.at[cz], in_ref.at[1], cz, True)
        offset_tiles(tout_ref.at[cz], out_ref.at[1], cz, False)

    far0_ref[...] = jnp.zeros((8, 32, 128), F32)
    core0 = block_diagonal(core_ref[0])

    @pl.loop(0, 36)
    def _(step):
        qx, qz = step // 6, step % 6
        blocks = []
        for qy in range(6):
            tiles = []
            for x in range(4):
                for z in range(2):
                    tiles.append(leaf_ref[2 * x + qx, 2 * z + qz, pl.ds(qy, 4, stride=2), :])
            source = jnp.concatenate(tiles, axis=0)
            for pair in range(4):
                cx, cy = pair // 2, pair % 2
                halves = []
                for cz in range(2):
                    row = (qx + 1 - cx) * 49 + (qy + 1 - cy) * 7 + qz + 1 - cz
                    scale = jnp.broadcast_to(scale_ref[pl.ds(row, 1), :], (32, 128))
                    halves.append((source * scale).astype(BF16))
                blocks.append(jnp.concatenate(halves, axis=1))
        image = dot(jnp.concatenate(blocks, axis=0), core0)
        for pair in range(4):
            cx, cy = pair // 2, pair % 2
            for cz in range(2):
                total = far0_ref[pair * 2 + cz]
                for qy in range(6):
                    row = (qx + 1 - cx) * 49 + (qy + 1 - cy) * 7 + qz + 1 - cz
                    scale = jnp.broadcast_to(out_ref[0, pl.ds(row, 1), :], (32, 128))
                    start = (qy * 4 + pair) * 32
                    total = total + scale * image[start : start + 32, cz * 128 : cz * 128 + 128]
                far0_ref[pair * 2 + cz] = total

    acc_ref[...] = jnp.zeros((8, 32, 128), F32)
    core1 = block_diagonal(core_ref[1])

    @pl.loop(0, 6)
    def _(qx):
        blocks = []
        for qy in range(6):
            tiles = [mid_ref[2 * x + qx, 2 * y + qy] for x in range(2) for y in range(2)]
            for pair in range(4):
                cx, cy = pair // 2, pair % 2
                xy = (qx + 1 - cx) * 7 + qy + 1 - cy
                halves = []
                for cz in range(2):
                    scale = tin_ref[cz, xy]
                    halves.append(
                        jnp.concatenate([tile * scale for tile in tiles], axis=0).astype(BF16)
                    )
                blocks.append(jnp.concatenate(halves, axis=1))
        image = dot(jnp.concatenate(blocks, axis=0), core1)
        for pair in range(4):
            cx, cy = pair // 2, pair % 2
            for cz in range(2):
                total = acc_ref[pair * 2 + cz]
                for qy in range(6):
                    scale = tout_ref[cz, (qx + 1 - cx) * 7 + qy + 1 - cy]
                    scale = jnp.concatenate([scale] * 4, axis=0)
                    start = (qy * 4 + pair) * 32
                    total = total + scale * image[start : start + 32, cz * 128 : cz * 128 + 128]
                acc_ref[pair * 2 + cz] = total

    for child in range(8):
        for parent in range(4):
            tile = acc_ref[child, parent * 8 : parent * 8 + 8, :]
            far1_ref[child * 4 + parent : child * 4 + parent + 1, :] = jnp.sum(
                tile, axis=0, keepdims=True
            )


def run_far(leafxy, midxy, ra, rb, in_scale, out_scale, transfer):
    return pl.pallas_call(
        far_kernel,
        in_specs=[VMEM] * 7,
        out_specs=[VMEM] * 2,
        out_shape=[
            jax.ShapeDtypeStruct((8, 32, 128), F32),
            jax.ShapeDtypeStruct((32, 128), F32),
        ],
        scratch_shapes=[
            pltpu.VMEM((12, 8, 12, 128), F32),
            pltpu.VMEM((8, 8, 8, 128), F32),
            pltpu.VMEM((343, 128), F32),
            pltpu.VMEM((2, 49, 8, 128), F32),
            pltpu.VMEM((2, 49, 8, 128), F32),
            pltpu.VMEM((8, 32, 128), F32),
        ],
        cost_estimate=pl.CostEstimate(flops=4 << 30, bytes_accessed=4 << 20, transcendentals=0),
        compiler_params=pltpu.CompilerParams(vmem_limit_bytes=24 << 20),
        name="far",
    )(leafxy, midxy, ra, rb, in_scale, out_scale, transfer)


def force_kernel(
    far0_ref, far1_ref, pair_ref, near_ref, next_ref, in_ref, out_ref, core_ref, down_ref,
    charge_ref, sin_ref, pos_ref, wave_ref,
    forces_ref, share_ref,
    window_ref, tin_ref, tout_ref, operand_ref, mid_ref, local_ref,
):
    odd = lax.axis_index("gz") % 2
    for xy in range(36):
        rows = [
            (ref[xy : xy + 1, :], ref[36 + xy : 37 + xy, :]) for ref in (near_ref, next_ref)
        ]
        low = [jnp.where(odd == 1, rows[1][z], rows[0][z]) for z in range(2)]
        high = [jnp.where(odd == 1, rows[0][z], rows[1][z]) for z in range(2)]
        window_ref[xy] = jnp.concatenate(
            low
            + [pair_ref[xy : xy + 1, :], pair_ref[36 + xy : 37 + xy, :]]
            + high
            + [jnp.zeros((2, 128), F32)],
            axis=0,
        )
    lanes = lax.broadcasted_iota(jnp.int32, (8, 128), 0)
    near = (lanes >= 1 + odd) & (lanes <= 3 + odd)
    for xy in range(49):
        for ref, table, masked in ((tin_ref, in_ref, True), (tout_ref, out_ref, False)):
            rows = table[2, xy * 7 : xy * 7 + 7, :]
            tile = jnp.where(odd == 1, rows[0:6], rows[1:7])
            tile = jnp.concatenate([tile, jnp.zeros((2, 128), F32)], axis=0)
            if masked and 2 <= xy // 7 <= 4 and 2 <= xy % 7 <= 4:
                tile = jnp.where(near, 0.0, tile)
            ref[xy] = tile
    for qx in range(6):
        for qy in range(6):
            source = window_ref[qx * 6 + qy]
            tiles = []
            for pair in range(4):
                cx, cy = pair // 2, pair % 2
                tiles.append(source * tin_ref[(qx + 1 - cx) * 7 + qy + 1 - cy])
            start = (qx * 6 + qy) * 32
            operand_ref[start : start + 32, :] = jnp.concatenate(tiles, axis=0).astype(BF16)
    totals = [jnp.zeros((8, 128), F32) for _ in range(4)]
    for qx in range(6):
        image = dot(operand_ref[qx * 192 : qx * 192 + 192, :], core_ref[2])
        for qy in range(6):
            for pair in range(4):
                cx, cy = pair // 2, pair % 2
                scale = tout_ref[(qx + 1 - cx) * 7 + qy + 1 - cy]
                start = qy * 32 + pair * 8
                totals[pair] = totals[pair] + scale * image[start : start + 8]
    local_top = jnp.concatenate(
        [jnp.sum(total, axis=0, keepdims=True) for total in totals] + [jnp.zeros((4, 128), F32)],
        axis=0,
    ).astype(BF16)
    for child in range(8):
        cx, cy, cz = child // 4, child // 2 % 2, child % 2
        rows = far1_ref[child * 4 : child * 4 + 4, :] + dot(local_top, down_ref[1, child])[0:4]
        for parent in range(4):
            row = ((2 * (parent // 2) + cx) * 2 + cz) * 4 + 2 * (parent % 2) + cy
            mid_ref[row : row + 1, :] = rows[parent : parent + 1]
    local_mid = mid_ref[...].astype(BF16)
    for child in range(8):
        cx, cy, cz = child // 4, child // 2 % 2, child % 2
        rows = far0_ref[child] + dot(local_mid, down_ref[0, child])
        for x in range(4):
            for z in range(2):
                start = (x * 2 + z) * 4
                local_ref[2 * x + cx, 2 * z + cz, pl.ds(cy, 4, stride=2), :] = rows[start : start + 4]

    lane_box = lax.broadcasted_iota(jnp.int32, (8, 128), 1) // 32
    row_y = lax.broadcasted_iota(jnp.int32, (8, 128), 0)
    base_x = lax.axis_index("gx") * 8
    base_y = lax.axis_index("gy") * 8
    base_z = lax.axis_index("gz") * 4
    place_y0 = (base_y + row_y).astype(F32)
    place_z0 = (base_z + lane_box).astype(F32)

    def one_plane(x, sums):
        local = local_ref[x].reshape(32, 128)
        weights = jnp.concatenate([local * wave_ref[d : d + 1, :] for d in range(3)], axis=0)
        high = weights.astype(BF16)
        low = (weights - high.astype(F32)).astype(BF16)
        sines = sin_ref[x]
        product = dot(
            jnp.concatenate([high, low], axis=1), jnp.concatenate([sines, sines], axis=0)
        )
        charge = charge_ref[x]
        found = []
        for d in range(3):
            picked = jnp.zeros((8, 128), F32)
            for z in range(4):
                start = (d * 4 + z) * 8
                for y in range(8):
                    picked = jnp.where(
                        (row_y == y) & (lane_box == z),
                        product[start : start + 8, y * 128 : y * 128 + 128],
                        picked,
                    )
            picked = picked * charge
            forces_ref[d, x] = picked
            found.append(picked)
        places = (
            ((base_x + x).astype(F32) + pos_ref[0, x]) * (1.0 / 32),
            (place_y0 + pos_ref[1, x]) * (1.0 / 64),
            (place_z0 + pos_ref[2, x]) * (1.0 / 64),
        )
        return tuple(
            sums[d * 3 + e] + places[d] * found[e] for d in range(3) for e in range(3)
        )

    sums = lax.fori_loop(0, 8, one_plane, (jnp.zeros((8, 128), F32),) * 9)
    lane = lax.broadcasted_iota(jnp.int32, (8, 128), 1)
    row = jnp.zeros((8, 128), F32)
    for i in range(9):
        row = jnp.where(lane == i, jnp.sum(sums[i]), row)
    share_ref[...] = jnp.broadcast_to(row[0:1], (512, 128))


def run_forces(far0, far1, pair, near, following, in_scale, out_scale, transfer, downward, charge, sines, positions, wave):
    return pl.pallas_call(
        force_kernel,
        in_specs=[VMEM] * 13,
        out_specs=[VMEM] * 2,
        out_shape=[
            jax.ShapeDtypeStruct((3, 8, 8, 128), F32),
            jax.ShapeDtypeStruct((512, 128), F32),
        ],
        scratch_shapes=[
            pltpu.VMEM((36, 8, 128), F32),
            pltpu.VMEM((49, 8, 128), F32),
            pltpu.VMEM((49, 8, 128), F32),
            pltpu.VMEM((1152, 128), BF16),
            pltpu.VMEM((32, 128), F32),
            pltpu.VMEM((8, 4, 8, 128), F32),
        ],
        compiler_params=pltpu.CompilerParams(vmem_limit_bytes=24 << 20),
        name="forces",
    )(far0, far1, pair, near, following, in_scale, out_scale, transfer, downward, charge, sines, positions, wave)


def virial_kernel(scale, rows_ref, virial_ref):
    row = jnp.sum(rows_ref[...], axis=0, keepdims=True) * scale
    for d in range(3):
        virial_ref[d : d + 1, :] = row[:, d * 3 : d * 3 + 3]


def run_virial(rows, scale):
    return pl.pallas_call(
        lambda rows_ref, virial_ref: virial_kernel(scale, rows_ref, virial_ref),
        in_specs=[VMEM],
        out_specs=VMEM,
        out_shape=jax.ShapeDtypeStruct((3, 3), F32),
        compiler_params=pltpu.CompilerParams(vmem_limit_bytes=8 << 20),
        name="virial",
    )(rows)


def swapped(value, axis, kind):
    count = lax.axis_size(axis)
    pairs = []
    for i in range(count):
        hop = (1, -1, 3)[kind]
        pairs.append((i, (i + hop) % count if i % 2 == 0 else (i - hop) % count))
    return lax.ppermute(value, axis, pairs)


def shards(
    features, positions, box_counts, w_hidden, w_charge, wave_numbers, phases,
    upward, downward, transfer, out_scale, in_scale,
):
    charge, sines, leaf, mid, top, xa, xb = run_atoms(
        features, positions, box_counts.transpose(0, 2, 1), w_hidden, w_charge.reshape(1, 128), wave_numbers,
        phases.reshape(1, 128), upward,
    )
    ra, rb = swapped(xa, "gx", 0), swapped(xb, "gx", 1)
    leaf, mid, top, ya, yb = glue_x(ra, rb, leaf, mid, top)
    ra, rb = swapped(ya, "gy", 0), swapped(yb, "gy", 1)
    leaf, mid, top, za, zb = glue_y(ra, rb, leaf, mid, top)
    ra, rb = swapped(za, "gz", 0), swapped(zb, "gz", 1)
    pair = glue_z(ra, top)
    near, following = swapped(pair, "gz", 1), swapped(pair, "gz", 2)
    far0, far1 = run_far(leaf, mid, ra, rb, in_scale, out_scale, transfer)
    forces, share = run_forces(
        far0, far1, pair, near, following, in_scale, out_scale, transfer, downward, charge, sines,
        positions, wave_numbers,
    )
    rows = lax.all_to_all(share, ("gx", "gy", "gz"), 0, 0, tiled=True)
    return forces, run_virial(rows, 1.0 / math.sqrt(4194304))


def solution(mesh):
    in_specs = (
        P("gx", "gy", "gz", None),
        P(None, "gx", "gy", "gz"),
        P("gx", "gy", "gz"),
    ) + (P(),) * 9
    out_specs = (P(None, "gx", "gy", "gz"), P())
    return jax.shard_map(shards, mesh=mesh, in_specs=in_specs, out_specs=out_specs, check_vma=False)
```

time: 364 us -> 112 us (0.31)
  blocking collectives: 101 us -> 35.6 us
  starting transfers between devices: 102 us -> 37.4 us
  local copies, waits for them, and re-layouts: 56.4 us -> 2.34 us
  matrix products: 52.5 us -> 0 us
  other arithmetic: 43.5 us -> 0 us
  Pallas kernels: 0 us -> 28.6 us
  waiting for transfers between devices: 0.07 us -> 6.45 us
  loops' own time: 4.6 us -> 0 us
    psum x1 -> x0, blocking collectives: 101 us -> none  [shards(): lax.psum(partial_virial, ('gx', 'gy', 'gz')) * (1.0 / math.sqrt(atom_total))]
    ppermute x25 -> x8, starting transfers between devices: 102 us -> 37.4 us  [swapped(): return lax.ppermute(value, axis, pairs)]
    dot_general x25 -> x0, matrix products: 52.5 us -> none  [the longest x1 33.5 us: shards(): jnp.einsum('xyzsk,dk->dxyzs', weight, wave_numbers, precision=lax.Precisi...]
    all_to_all x0 -> x1, blocking collectives: none -> 35.6 us  [shards(): rows = lax.all_to_all(share, ('gx', 'gy', 'gz'), 0, 0, tiled=True)]
    reduce_sum x1 -> x0, other arithmetic: 30.8 us -> none  [shards(): moments = (charge[..., None] * jnp.cos(angle)).reshape(side_x, side_y, si...]
    pallas_call x0 -> x7, Pallas kernels: none -> 28.6 us  [the longest x1 12.7 us: run_atoms(): pl.pallas_call(atoms_kernel, in_specs=[hbm, hbm, VMEM, hbm, VMEM, VMEM, V...]
    gather x6 -> x0, local copies, waits for them, and re-layouts: 24.4 us -> none  [the longest x3 12.7 us: translate(): out_rows = jnp.take(out_table, flat, axis=0).reshape(6, 36, 8, coeffs)]
    mul x16 -> x0, local copies, waits for them, and re-layouts: 13.3 us -> none  [the longest x12 12.1 us: add_plane(): image = image.reshape(36, 8, parents, coeffs) * outer[:, :, None, :]]
  transfers between devices with their start and end apart: 25 -> 8, of which waited for: 0 -> 2; matrix products, arithmetic and copies ran while one was open for 17% -> 0% of each run, Pallas kernels for 0% -> 11%
where the time goes in v1:
time: 112 us; the launch traced here: 111 us
  starting transfers between devices  37.4 us (33%)
  blocking collectives  35.6 us (32%)
  Pallas kernels  28.6 us (26%)
  waiting for transfers between devices  6.45 us (6%)
  local copies, waits for them, and re-layouts  2.34 us (2%)
    ppermute x8, starting transfers between devices, swapped(): return lax.ppermute(value, axis, pairs)  37.4 us
    all_to_all x1, blocking collectives, shards(): rows = lax.all_to_all(share, ('gx', 'gy', 'gz'), 0, 0, tiled=True)  35.6 us
    pallas_call x1, Pallas kernels, run_atoms(): pl.pallas_call(atoms_kernel, in_specs=[hbm, hbm, VMEM, hbm, VMEM, VMEM, V...  12.7 us
    pallas_call x1, Pallas kernels, run_far(): pl.pallas_call(far_kernel, in_specs=[VMEM] * 7, out_specs=[VMEM] * 2, out...  11.8 us
    ppermute x8, waiting for transfers between devices, swapped(): return lax.ppermute(value, axis, pairs)  6.45 us
    pallas_call x1, Pallas kernels, run_forces(): pl.pallas_call(force_kernel, in_specs=[VMEM] * 13, out_specs=[VMEM] * 2,...  3.21 us
    unnamed x22, local copies, waits for them, and re-layouts  2.34 us
  transfers between devices with their start and end apart: 8, of which 2 were waited for; matrix products, arithmetic and copies ran while one was open for 0% of the time, Pallas kernels for 11%

profile of v1, /device:TPU:1, one launch (start us, length us, event | category | flops | bytes accessed | tf_op | source)
XLA Modules:
  0.0 111.3 jit_solution(15594954518947426438)
XLA Ops:
  0.6 0.0 copy-start.1
  0.6 0.0 copy-start.2
  0.7 0.0 copy-start.6
  0.7 12.7 %atoms.1 = (f32[8,8,128]{2,1,0:T(8,128)}, bf16[8,128,1024]{2,1,0:T(8,128)(2,1)}, f32[8,4,8,128]{3,2,1,0:T(8,128)}, f32[4,4,2,128]{3,2,1,0:T(2,128)}, f32[4,128]{...) custom-call(bf16[8,8,128,128]{3,2,1,0:T(8,128)(2,1)} %feat_hbm.1, f32[3,8,8,128]{3,2,1,0:T(8,128)} %pos_ref.1, ...), custom_call_target="tpu_custom_call" | custom-call | tf_op jit(solution)/shard_map/atoms/pallas_call | solution.py:182
  13.3 8.8 %collective-permute-start = (f32[88,128]{1,0:T(8,128)}, f32[88,128]{1,0:T(8,128)S(1)}, u32[]{:S(2)}, u32[]{:S(2)}) collective-permute-start(f32[88,128]{1,0:T(8,128)} %get-tuple-element.23), channel_id=1, source_target_pairs={{0,128},{128,0},{256,384},{384,256},{1,129},{129,1},{257,385},{385... | collective-permute-start | bytes 135176 | tf_op jit(solution)/shard_map/ppermute | solution.py:645
  22.1 5.2 %collective-permute-start.1 = (f32[88,128]{1,0:T(8,128)}, f32[88,128]{1,0:T(8,128)S(1)}, u32[]{:S(2)}, u32[]{:S(2)}) collective-permute-start(f32[88,128]{1,0:T(8,128)} %get-tuple-element.24), channel_id=1, source_target_pairs={{0,384},{128,256},{256,128},{384,0},{1,385},{129,257},{257,129},{3... | collective-permute-start | bytes 135176 | tf_op jit(solution)/shard_map/ppermute | solution.py:645
  27.3 0.0 collective-permute-done.ra_ref
  27.3 4.3 %collective-permute-done.1.rb_ref = f32[88,128]{1,0:T(8,128)S(1)} collective-permute-done((f32[88,128]{1,0:T(8,128)}, f32[88,128]{1,0:T(8,128)S(1)}, u32[]{:S(2)}, u32[]{:S(2)}) %collective-permute-start.1) | collective-permute-done | bytes 45088 | tf_op jit(solution)/shard_map/ppermute | solution.py:645
  31.6 0.9 copy-done.5
  32.5 0.7 copy-done.8
  33.2 0.7 copy-done.10
  33.9 0.1 glue_x.1
  34.0 1.9 %collective-permute-start.2 = (f32[144,128]{1,0:T(8,128)S(1)}, f32[144,128]{1,0:T(8,128)S(1)}, u32[]{:S(2)}, u32[]{:S(2)}) collective-permute-start(f32[144,128]{1,0:T(8,128)S(1)} %get-tuple-element.28), channel_id=1, source_target_pairs={{0,16},{16,0},{32,48},{48,32},{64,80},{80,64},{96,112},{112,96},{1... | collective-permute-start | bytes 221192 | tf_op jit(solution)/shard_map/ppermute | solution.py:645
  35.9 4.2 %collective-permute-start.3 = (f32[144,128]{1,0:T(8,128)S(1)}, f32[144,128]{1,0:T(8,128)S(1)}, u32[]{:S(2)}, u32[]{:S(2)}) collective-permute-start(f32[144,128]{1,0:T(8,128)S(1)} %get-tuple-element.29), channel_id=1, source_target_pairs={{0,112},{16,32},{32,16},{48,64},{64,48},{80,96},{96,80},{112,0},{1... | collective-permute-start | bytes 221192 | tf_op jit(solution)/shard_map/ppermute | solution.py:645
  40.1 0.0 collective-permute-done.2.ra_ref
  40.1 2.1 %collective-permute-done.3.rb_ref = f32[144,128]{1,0:T(8,128)S(1)} collective-permute-done((f32[144,128]{1,0:T(8,128)S(1)}, f32[144,128]{1,0:T(8,128)S(1)}, u32[]{:S(2)}, u32[]{:S(2)}) %collective-permute-start.3) | collective-permute-done | bytes 73760 | tf_op jit(solution)/shard_map/ppermute | solution.py:645
  42.2 0.1 glue_y.1
  42.3 2.7 %collective-permute-start.4 = (f32[456,128]{1,0:T(8,128)S(1)}, f32[456,128]{1,0:T(8,128)S(1)}, u32[]{:S(2)}, u32[]{:S(2)}) collective-permute-start(f32[456,128]{1,0:T(8,128)S(1)} %get-tuple-element.35), channel_id=1, source_target_pairs={{0,1},{1,0},{2,3},{3,2},{4,5},{5,4},{6,7},{7,6},{8,9},{9,8},{10,11... | collective-permute-start | bytes 700424 | tf_op jit(solution)/shard_map/ppermute | solution.py:645
  45.0 7.3 %collective-permute-start.5 = (f32[416,128]{1,0:T(8,128)S(1)}, f32[416,128]{1,0:T(8,128)S(1)}, u32[]{:S(2)}, u32[]{:S(2)}) collective-permute-start(f32[416,128]{1,0:T(8,128)S(1)} %get-tuple-element.36), channel_id=1, source_target_pairs={{0,15},{1,2},{2,1},{3,4},{4,3},{5,6},{6,5},{7,8},{8,7},{9,10},{10,... | collective-permute-start | bytes 638984 | tf_op jit(solution)/shard_map/ppermute | solution.py:645
  52.3 0.0 collective-permute-done.4.ra_ref
  52.4 2.0 %collective-permute-start.7 = (f32[72,128]{1,0:T(8,128)S(1)}, f32[72,128]{1,0:T(8,128)S(1)}, u32[]{:S(2)}, u32[]{:S(2)}) collective-permute-start(f32[72,128]{1,0:T(8,128)S(1)} %glue_z.1.pair_ref), channel_id=1, source_target_pairs={{0,3},{1,14},{2,5},{3,0},{4,7},{5,2},{6,9},{7,4},{8,11},{9,6},{10,... | collective-permute-start | bytes 110600 | tf_op jit(solution)/shard_map/ppermute | solution.py:645
  54.4 5.4 %collective-permute-start.6 = (f32[72,128]{1,0:T(8,128)S(1)}, f32[72,128]{1,0:T(8,128)S(1)}, u32[]{:S(2)}, u32[]{:S(2)}) collective-permute-start(f32[72,128]{1,0:T(8,128)S(1)} %glue_z.1.pair_ref), channel_id=1, source_target_pairs={{0,15},{1,2},{2,1},{3,4},{4,3},{5,6},{6,5},{7,8},{8,7},{9,10},{10,... | collective-permute-start | bytes 110600 | tf_op jit(solution)/shard_map/ppermute | solution.py:645
  59.7 0.0 collective-permute-done.5.rb_ref
  59.8 0.0 copy-start.3
  59.8 0.0 copy-start.4
  59.8 0.0 copy-start.9
  59.8 11.8 %far.1 = (f32[8,32,128]{2,1,0:T(8,128)S(1)}, f32[32,128]{1,0:T(8,128)S(1)}) custom-call(f32[12,4,12,128]{3,2,1,0:T(8,128)S(1)} %get-tuple-element.33.leafxy_ref, f32[8,8,2,128]{3,2,1,0:T(2,128)S(1)} %get-tuple-element.34.midxy_ref, f32[456,128]{1,0:T(8,128)S(1)} %collective-permute-done.4.ra_ref, f32[416,128]{1,0:T(8,128)S(1)} %collective-permute-done.5.rb_ref, ...), custom_call_target="tpu_custom_call" | custom-call | flops 4294967296 | bytes 4194304 | tf_op jit(solution)/shard_map/far/pallas_call | solution.py:462
  71.7 0.0 collective-permute-done.7.next_ref
  71.7 0.0 collective-permute-done.6.near_ref
  71.7 3.2 %forces.1 = (f32[3,8,8,128]{3,2,1,0:T(8,128)}, f32[512,128]{1,0:T(8,128)S(1)}) custom-call(f32[8,32,128]{2,1,0:T(8,128)S(1)} %get-tuple-element.37.far0_ref, f32[32,128]{1,0:T(8,128)S(1)} %get-tuple-element.38.far1_ref, f32[72,128]{1,0:T(8,128)S(1)} %glue_z.1.pair_ref, f32[72,128]{1,0:T(8,128)S(1)} %collective-permute-done.6.near_ref, ...), custom_call_target="tpu_custom_call" | custom-call | tf_op jit(solution)/shard_map/forces/pallas_call | solution.py:601
  74.9 35.6 %all_to_all.11 = f32[512,1,128]{2,1,0:T(1,128)S(1)} all-to-all(f32[512,1,128]{2,1,0:T(1,128)S(1)} %bitcast.8), channel_id=1, replica_groups=mesh['gx'=4,'gy'=8,'gz'=16] {'gx','gy','gz'}, dimensions={0} | all-to-all | bytes 524288 | tf_op jit(solution)/shard_map/all_to_all | solution.py:668
  110.6 0.7 virial.1
  (14 shorter events, 0.0 us)
Async XLA Ops:
  0.6 59.1 %copy-start.1 = (f32[3,343,128]{2,1,0:T(8,128)S(1)}, f32[3,343,128]{2,1,0:T(8,128)}, u32[]{:S(2)}) copy-start(f32[3,343,128]{2,1,0:T(8,128)} %in_ref.3) | copy-start | bytes 1580548
  0.6 59.1 %copy-start.2 = (f32[3,343,128]{2,1,0:T(8,128)S(1)}, f32[3,343,128]{2,1,0:T(8,128)}, u32[]{:S(2)}) copy-start(f32[3,343,128]{2,1,0:T(8,128)} %out_ref.3) | copy-start | bytes 1580548
  0.7 59.1 %copy-start.6 = (bf16[3,128,128]{2,1,0:T(8,128)(2,1)S(1)}, bf16[3,128,128]{2,1,0:T(8,128)(2,1)}, u32[]{:S(2)}) copy-start(bf16[3,128,128]{2,1,0:T(8,128)(2,1)} %core_ref.3) | copy-start | bytes 294916
  13.3 14.0 %collective-permute-start = (f32[88,128]{1,0:T(8,128)}, f32[88,128]{1,0:T(8,128)S(1)}, u32[]{:S(2)}, u32[]{:S(2)}) collective-permute-start(f32[88,128]{1,0:T(8,128)} %get-tuple-element.23), channel_id=1, source_target_pairs={{0,128},{128,0},{256,384},{384,256},{1,129},{129,1},{257,385},{385... | collective-permute-start | bytes 135176 | tf_op jit(solution)/shard_map/ppermute | solution.py:645
  22.1 9.5 %collective-permute-start.1 = (f32[88,128]{1,0:T(8,128)}, f32[88,128]{1,0:T(8,128)S(1)}, u32[]{:S(2)}, u32[]{:S(2)}) collective-permute-start(f32[88,128]{1,0:T(8,128)} %get-tuple-element.24), channel_id=1, source_target_pairs={{0,384},{128,256},{256,128},{384,0},{1,385},{129,257},{257,129},{3... | collective-permute-start | bytes 135176 | tf_op jit(solution)/shard_map/ppermute | solution.py:645
  31.6 0.9 copy-start.5
  32.5 0.7 copy-start.8
  33.2 0.7 copy-start.10
  34.0 6.1 %collective-permute-start.2 = (f32[144,128]{1,0:T(8,128)S(1)}, f32[144,128]{1,0:T(8,128)S(1)}, u32[]{:S(2)}, u32[]{:S(2)}) collective-permute-start(f32[144,128]{1,0:T(8,128)S(1)} %get-tuple-element.28), channel_id=1, source_target_pairs={{0,16},{16,0},{32,48},{48,32},{64,80},{80,64},{96,112},{112,96},{1... | collective-permute-start | bytes 221192 | tf_op jit(solution)/shard_map/ppermute | solution.py:645
  35.9 6.3 %collective-permute-start.3 = (f32[144,128]{1,0:T(8,128)S(1)}, f32[144,128]{1,0:T(8,128)S(1)}, u32[]{:S(2)}, u32[]{:S(2)}) collective-permute-start(f32[144,128]{1,0:T(8,128)S(1)} %get-tuple-element.29), channel_id=1, source_target_pairs={{0,112},{16,32},{32,16},{48,64},{64,48},{80,96},{96,80},{112,0},{1... | collective-permute-start | bytes 221192 | tf_op jit(solution)/shard_map/ppermute | solution.py:645
  42.3 10.0 %collective-permute-start.4 = (f32[456,128]{1,0:T(8,128)S(1)}, f32[456,128]{1,0:T(8,128)S(1)}, u32[]{:S(2)}, u32[]{:S(2)}) collective-permute-start(f32[456,128]{1,0:T(8,128)S(1)} %get-tuple-element.35), channel_id=1, source_target_pairs={{0,1},{1,0},{2,3},{3,2},{4,5},{5,4},{6,7},{7,6},{8,9},{9,8},{10,11... | collective-permute-start | bytes 700424 | tf_op jit(solution)/shard_map/ppermute | solution.py:645
  45.0 14.7 %collective-permute-start.5 = (f32[416,128]{1,0:T(8,128)S(1)}, f32[416,128]{1,0:T(8,128)S(1)}, u32[]{:S(2)}, u32[]{:S(2)}) collective-permute-start(f32[416,128]{1,0:T(8,128)S(1)} %get-tuple-element.36), channel_id=1, source_target_pairs={{0,15},{1,2},{2,1},{3,4},{4,3},{5,6},{6,5},{7,8},{8,7},{9,10},{10,... | collective-permute-start | bytes 638984 | tf_op jit(solution)/shard_map/ppermute | solution.py:645
  52.4 19.3 %collective-permute-start.7 = (f32[72,128]{1,0:T(8,128)S(1)}, f32[72,128]{1,0:T(8,128)S(1)}, u32[]{:S(2)}, u32[]{:S(2)}) collective-permute-start(f32[72,128]{1,0:T(8,128)S(1)} %glue_z.1.pair_ref), channel_id=1, source_target_pairs={{0,3},{1,14},{2,5},{3,0},{4,7},{5,2},{6,9},{7,4},{8,11},{9,6},{10,... | collective-permute-start | bytes 110600 | tf_op jit(solution)/shard_map/ppermute | solution.py:645
  54.4 17.3 %collective-permute-start.6 = (f32[72,128]{1,0:T(8,128)S(1)}, f32[72,128]{1,0:T(8,128)S(1)}, u32[]{:S(2)}, u32[]{:S(2)}) collective-permute-start(f32[72,128]{1,0:T(8,128)S(1)} %glue_z.1.pair_ref), channel_id=1, source_target_pairs={{0,15},{1,2},{2,1},{3,4},{4,3},{5,6},{6,5},{7,8},{8,7},{9,10},{10,... | collective-permute-start | bytes 110600 | tf_op jit(solution)/shard_map/ppermute | solution.py:645
  59.8 11.9 %copy-start = (bf16[8,128,1024]{2,1,0:T(8,128)(2,1)S(1)}, bf16[8,128,1024]{2,1,0:T(8,128)(2,1)}, u32[]{:S(2)}) copy-start(bf16[8,128,1024]{2,1,0:T(8,128)(2,1)} %get-tuple-element.41.sin_ref) | copy-start | bytes 6291460
  59.8 11.9 %copy-start.3 = (bf16[2,8,128,128]{3,2,1,0:T(8,128)(2,1)S(1)}, bf16[2,8,128,128]{3,2,1,0:T(8,128)(2,1)}, u32[]{:S(2)}) copy-start(bf16[2,8,128,128]{3,2,1,0:T(8,128)(2,1)} %down_ref.1) | copy-start | bytes 1572868
  59.8 11.9 %copy-start.4 = (f32[3,8,8,128]{3,2,1,0:T(8,128)S(1)}, f32[3,8,8,128]{3,2,1,0:T(8,128)}, u32[]{:S(2)}) copy-start(f32[3,8,8,128]{3,2,1,0:T(8,128)} %pos_ref.1) | copy-start | bytes 294916
  59.8 11.9 %copy-start.7 = (f32[8,8,128]{2,1,0:T(8,128)S(1)}, f32[8,8,128]{2,1,0:T(8,128)}, u32[]{:S(2)}) copy-start(f32[8,8,128]{2,1,0:T(8,128)} %get-tuple-element.40.charge_ref) | copy-start | bytes 98308
  59.8 11.9 %copy-start.9 = (f32[3,128]{1,0:T(4,128)S(1)}, f32[3,128]{1,0:T(4,128)}, u32[]{:S(2)}) copy-start(f32[3,128]{1,0:T(4,128)} %wave_ref.3) | copy-start | bytes 4612

commit v2 on v1

--- a/solution.py
+++ b/solution.py
@@ -23,8 +23,9 @@
 
 def atoms_kernel(
     feat_hbm, pos_hbm, cnt_ref, wh_hbm, wc_ref, wave_ref, ph_ref, up_hbm,
-    charge_ref, sin_ref, leaf_ref, mid_ref, top_ref, sa_ref, sb_ref,
-    feat_ref, pos_ref, wh_ref, up_ref, cols_ref, cos_ref, low_ref, plane_sems, sems,
+    charge_ref, sin_hbm, own_ref, send_ref,
+    feat_ref, pos_ref, wh_ref, up_ref, cols_ref, cos_ref, low_ref, sin_ref, leaf_ref, mid_ref,
+    plane_sems, sin_sems, sems,
 ):
     def plane(x):
         return pltpu.make_async_copy(feat_hbm.at[x], feat_ref.at[x], plane_sems.at[x])
@@ -57,9 +58,12 @@
             x, feat_ref, pos_ref, cnt_ref, wh_ref, wc_ref, charge_ref, sin_ref, leaf_ref,
             cols_ref, cos_ref, low_ref,
         )
+        pltpu.make_async_copy(sin_ref.at[x], sin_hbm.at[x], sin_sems.at[x]).start()
 
     others[2].wait()
-    atoms_lift(leaf_ref, up_ref, mid_ref, top_ref, sa_ref, sb_ref)
+    atoms_lift(leaf_ref, up_ref, mid_ref, own_ref, send_ref)
+    for x in range(8):
+        pltpu.make_async_copy(sin_ref.at[x], sin_hbm.at[x], sin_sems.at[x]).wait()
 
 
 def atoms_plane(
@@ -132,7 +136,7 @@
         leaf_ref[step, z] = moments[z * 8 : (z + 1) * 8]
 
 
-def atoms_lift(leaf_ref, up_ref, mid_ref, top_ref, sa_ref, sb_ref):
+def atoms_lift(leaf_ref, up_ref, mid_ref, own_ref, send_ref):
     total = jnp.zeros((32, 128), F32)
     for child in range(8):
         cx, cy, cz = child // 4, child // 2 % 2, child % 2
@@ -163,18 +167,21 @@
             axis=0,
         )
         crown = crown + dot(rows.astype(BF16), up_ref[1, child])
-    top_ref[...] = crown[0:4]
-    odd = lax.axis_index("gx") % 2
-    for ref, high in ((sa_ref, 1 - odd), (sb_ref, odd)):
-        for x in range(2):
-            for z in range(4):
-                row = (x * 4 + z) * 8
-                ref[row : row + 8, :] = leaf_ref[high * 6 + x, z]
-            for y in range(4):
-                row = 64 + (x * 4 + y) * 2
-                ref[row : row + 2, :] = mid_ref[high * 2 + x, y]
-        ref[80:84, :] = crown[0:4]
-        ref[84:88, :] = jnp.zeros((4, 128), F32)
+    odd = lax.axis_index("gz") % 2
+    for x in range(8):
+        for z in range(4):
+            row = (x * 4 + z) * 8
+            own_ref[row : row + 8, :] = leaf_ref[x, z]
+        for z in range(2):
+            row = (x * 2 + z) * 8
+            send_ref[row : row + 8, :] = leaf_ref[x, 2 * (1 - odd) + z]
+    for x in range(4):
+        for y in range(4):
+            row = (x * 4 + y) * 2
+            own_ref[256 + row : 258 + row, :] = mid_ref[x, y]
+            send_ref[128 + row : 130 + row, :] = mid_ref[x, y]
+    own_ref[288:296, :] = crown
+    send_ref[160:168, :] = crown
 
 
 def run_atoms(features, positions, box_counts, w_hidden, w_charge, wave, phases, upward):
@@ -182,15 +189,12 @@
     return pl.pallas_call(
         atoms_kernel,
         in_specs=[hbm, hbm, VMEM, hbm, VMEM, VMEM, VMEM, hbm],
-        out_specs=[VMEM] * 7,
+        out_specs=[VMEM, hbm, VMEM, VMEM],
         out_shape=[
             jax.ShapeDtypeStruct((8, 8, 128), F32),
             jax.ShapeDtypeStruct((8, 128, 1024), BF16),
-            jax.ShapeDtypeStruct((8, 4, 8, 128), F32),
-            jax.ShapeDtypeStruct((4, 4, 2, 128), F32),
-            jax.ShapeDtypeStruct((4, 128), F32),
-            jax.ShapeDtypeStruct((88, 128), F32),
-            jax.ShapeDtypeStruct((88, 128), F32),
+            jax.ShapeDtypeStruct((296, 128), F32),
+            jax.ShapeDtypeStruct((168, 128), F32),
         ],
         scratch_shapes=[
             pltpu.VMEM((8, 8, 128, 128), BF16),
@@ -200,6 +204,10 @@
             pltpu.VMEM((4, 128, 128), F32),
             pltpu.VMEM((128, 1024), BF16),
             pltpu.VMEM((128, 1024), BF16),
+            pltpu.VMEM((8, 128, 1024), BF16),
+            pltpu.VMEM((8, 4, 8, 128), F32),
+            pltpu.VMEM((4, 4, 2, 128), F32),
+            pltpu.SemaphoreType.DMA((8,)),
             pltpu.SemaphoreType.DMA((8,)),
             pltpu.SemaphoreType.DMA((3,)),
         ],
@@ -208,42 +216,87 @@
     )(features, positions, box_counts, w_hidden, w_charge, wave, phases, upward)
 
 
-def glue_x_kernel(ra_ref, rb_ref, leaf_ref, mid_ref, top_ref, leafx_ref, midx_ref, topx_ref, ya_ref, yb_ref):
+def glue_z_kernel(got_ref, own_ref, leafz_ref, midz_ref, topz_ref, xa_ref, xb_ref):
+    odd = lax.axis_index("gz") % 2
+    for x in range(8):
+        for z in range(4):
+            row = (x * 4 + z) * 8
+            leafz_ref[x, 2 * odd + z] = own_ref[row : row + 8, :]
+        for z in range(2):
+            row = (x * 2 + z) * 8
+            leafz_ref[x, 4 * (1 - odd) + z] = got_ref[row : row + 8, :]
+    for x in range(4):
+        for y in range(4):
+            row = (x * 4 + y) * 2
+            mine, other = own_ref[256 + row : 258 + row, :], got_ref[128 + row : 130 + row, :]
+            midz_ref[x, y] = jnp.concatenate(
+                [jnp.where(odd == 1, other, mine), jnp.where(odd == 1, mine, other)], axis=0
+            )
+    mine, other = own_ref[288:292, :], got_ref[160:164, :]
+    low, high = jnp.where(odd == 1, other, mine), jnp.where(odd == 1, mine, other)
+    pair = jnp.concatenate(
+        [piece[i : i + 1] for i in range(4) for piece in (low, high)], axis=0
+    )
+    topz_ref[...] = pair
+    odd_x = lax.axis_index("gx") % 2
+    for ref, side in ((xa_ref, 1 - odd_x), (xb_ref, odd_x)):
+        for x in range(2):
+            for z in range(6):
+                row = (x * 6 + z) * 8
+                ref[row : row + 8, :] = leafz_ref[side * 6 + x, z]
+            for y in range(4):
+                row = 96 + (x * 4 + y) * 4
+                ref[row : row + 4, :] = midz_ref[side * 2 + x, y]
+        ref[128:136, :] = pair
+
+
+def glue_z(got, own):
+    return pl.pallas_call(
+        glue_z_kernel,
+        in_specs=[VMEM] * 2,
+        out_specs=[VMEM] * 5,
+        out_shape=[
+            jax.ShapeDtypeStruct((8, 6, 8, 128), F32),
+            jax.ShapeDtypeStruct((4, 4, 4, 128), F32),
+            jax.ShapeDtypeStruct((8, 128), F32),
+            jax.ShapeDtypeStruct((136, 128), F32),
+            jax.ShapeDtypeStruct((136, 128), F32),
+        ],
+        compiler_params=pltpu.CompilerParams(vmem_limit_bytes=8 << 20),
+        name="glue_z",
+    )(got, own)
+
+
+def glue_x_kernel(ra_ref, rb_ref, leafz_ref, midz_ref, topz_ref, leafx_ref, midx_ref, topx_ref, ya_ref, yb_ref):
     odd = lax.axis_index("gx") % 2
-    leafx_ref[2:10] = leaf_ref[...]
-    midx_ref[2:6] = mid_ref[...]
+    leafx_ref[2:10] = leafz_ref[...]
+    midx_ref[2:6] = midz_ref[...]
     for ref, high in ((ra_ref, 1 - odd), (rb_ref, odd)):
         for x in range(2):
-            for z in range(4):
-                row = (x * 4 + z) * 8
+            for z in range(6):
+                row = (x * 6 + z) * 8
                 leafx_ref[high * 10 + x, z] = ref[row : row + 8, :]
             for y in range(4):
-                row = 64 + (x * 4 + y) * 2
-                midx_ref[high * 6 + x, y] = ref[row : row + 2, :]
-    ta, tb = ra_ref[80:84, :], rb_ref[80:84, :]
-    topx_ref[...] = jnp.concatenate(
-        [
-            jnp.where(odd == 1, ta, tb),
-            top_ref[...],
-            jnp.where(odd == 1, tb, ta),
-            jnp.zeros((4, 128), F32),
-        ],
-        axis=0,
-    )
+                row = 96 + (x * 4 + y) * 4
+                midx_ref[high * 6 + x, y] = ref[row : row + 4, :]
+    ta, tb = ra_ref[128:136, :], rb_ref[128:136, :]
+    topx_ref[0:8, :] = jnp.where(odd == 1, ta, tb)
+    topx_ref[8:16, :] = topz_ref[...]
+    topx_ref[16:24, :] = jnp.where(odd == 1, tb, ta)
     odd_y = lax.axis_index("gy") % 2
     for x in range(12):
-        for z in range(4):
+        for z in range(6):
             tile = leafx_ref[x, z]
             low, high = tile[0:2], tile[6:8]
-            row = (x * 4 + z) * 2
+            row = (x * 6 + z) * 2
             ya_ref[row : row + 2, :] = jnp.where(odd_y == 1, low, high)
             yb_ref[row : row + 2, :] = jnp.where(odd_y == 1, high, low)
     for ref, side in ((ya_ref, 1 - odd_y), (yb_ref, odd_y)):
         for x in range(8):
             for y in range(2):
-                row = 96 + (x * 2 + y) * 2
-                ref[row : row + 2, :] = midx_ref[x, side * 2 + y]
-        ref[128:144, :] = topx_ref[...]
+                row = 144 + (x * 2 + y) * 4
+                ref[row : row + 4, :] = midx_ref[x, side * 2 + y]
+        ref[208:232, :] = topx_ref[...]
 
 
 def glue_x(ra, rb, leaf, mid, top):
@@ -252,22 +305,22 @@
         in_specs=[VMEM] * 5,
         out_specs=[VMEM] * 5,
         out_shape=[
-            jax.ShapeDtypeStruct((12, 4, 8, 128), F32),
-            jax.ShapeDtypeStruct((8, 4, 2, 128), F32),
-            jax.ShapeDtypeStruct((16, 128), F32),
-            jax.ShapeDtypeStruct((144, 128), F32),
-            jax.ShapeDtypeStruct((144, 128), F32),
+            jax.ShapeDtypeStruct((12, 6, 8, 128), F32),
+            jax.ShapeDtypeStruct((8, 4, 4, 128), F32),
+            jax.ShapeDtypeStruct((24, 128), F32),
+            jax.ShapeDtypeStruct((232, 128), F32),
+            jax.ShapeDtypeStruct((232, 128), F32),
         ],
         compiler_params=pltpu.CompilerParams(vmem_limit_bytes=8 << 20),
         name="glue_x",
     )(ra, rb, leaf, mid, top)
 
 
-def glue_y_kernel(ra_ref, rb_ref, leafx_ref, midx_ref, topx_ref, leafxy_ref, midxy_ref, topxy_ref, za_ref, zb_ref):
+def glue_y_kernel(ra_ref, rb_ref, leafx_ref, midx_ref, topx_ref, leafxy_ref, midxy_ref, topxy_ref, near_ref):
     odd = lax.axis_index("gy") % 2
     for x in range(12):
-        for z in range(4):
-            row = (x * 4 + z) * 2
+        for z in range(6):
+            row = (x * 6 + z) * 2
             a, b = ra_ref[row : row + 2, :], rb_ref[row : row + 2, :]
             leafxy_ref[x, z, 0:2, :] = jnp.where(odd == 1, a, b)
             leafxy_ref[x, z, 2:10, :] = leafx_ref[x, z]
@@ -276,69 +329,41 @@
         midxy_ref[x, 2:6] = midx_ref[x]
         for ref, high in ((ra_ref, 1 - odd), (rb_ref, odd)):
             for y in range(2):
-                row = 96 + (x * 2 + y) * 2
-                midxy_ref[x, high * 6 + y] = ref[row : row + 2, :]
+                row = 144 + (x * 2 + y) * 4
+                midxy_ref[x, high * 6 + y] = ref[row : row + 4, :]
     for x in range(6):
-        row = 128 + x * 2
-        a, b = ra_ref[row : row + 2, :], rb_ref[row : row + 2, :]
-        topxy_ref[x * 6 : x * 6 + 2, :] = jnp.where(odd == 1, a, b)
-        topxy_ref[x * 6 + 2 : x * 6 + 4, :] = topx_ref[x * 2 : x * 2 + 2, :]
-        topxy_ref[x * 6 + 4 : x * 6 + 6, :] = jnp.where(odd == 1, b, a)
-    topxy_ref[36:40, :] = jnp.zeros((4, 128), F32)
+        row = 208 + x * 4
+        a, b = ra_ref[row : row + 4, :], rb_ref[row : row + 4, :]
+        topxy_ref[x * 12 : x * 12 + 4, :] = jnp.where(odd == 1, a, b)
+        topxy_ref[x * 12 + 4 : x * 12 + 8, :] = topx_ref[x * 4 : x * 4 + 4, :]
+        topxy_ref[x * 12 + 8 : x * 12 + 12, :] = jnp.where(odd == 1, b, a)
     odd_z = lax.axis_index("gz") % 2
-    for ref, side in ((za_ref, 1 - odd_z), (zb_ref, odd_z)):
-        for x in range(12):
-            for z in range(2):
-                row = (x * 2 + z) * 12
-                ref[row : row + 12, :] = leafxy_ref[x, side * 2 + z]
-        for x in range(8):
-            for y in range(8):
-                row = 288 + (x * 8 + y) * 2
-                ref[row : row + 2, :] = midxy_ref[x, y]
-    za_ref[416:456, :] = topxy_ref[...]
+    for x in range(12):
+        for z in range(2):
+            row = (x * 2 + z) * 12
+            near_ref[row : row + 12, :] = leafxy_ref[x, 4 * odd_z + z]
+    for x in range(8):
+        for y in range(8):
+            row = 288 + (x * 8 + y) * 2
+            tile = midxy_ref[x, y]
+            near_ref[row : row + 2, :] = jnp.where(odd_z == 1, tile[2:4], tile[0:2])
+    near_ref[416:488, :] = topxy_ref[...]
 
 
 def glue_y(ra, rb, leafx, midx, topx):
     return pl.pallas_call(
         glue_y_kernel,
         in_specs=[VMEM] * 5,
-        out_specs=[VMEM] * 5,
+        out_specs=[VMEM] * 4,
         out_shape=[
-            jax.ShapeDtypeStruct((12, 4, 12, 128), F32),
-            jax.ShapeDtypeStruct((8, 8, 2, 128), F32),
-            jax.ShapeDtypeStruct((40, 128), F32),
-            jax.ShapeDtypeStruct((456, 128), F32),
-            jax.ShapeDtypeStruct((416, 128), F32),
+            jax.ShapeDtypeStruct((12, 6, 12, 128), F32),
+            jax.ShapeDtypeStruct((8, 8, 4, 128), F32),
+            jax.ShapeDtypeStruct((72, 128), F32),
+            jax.ShapeDtypeStruct((488, 128), F32),
         ],
         compiler_params=pltpu.CompilerParams(vmem_limit_bytes=8 << 20),
         name="glue_y",
     )(ra, rb, leafx, midx, topx)
-
-
-def glue_z_kernel(ra_ref, topxy_ref, pair_ref):
-    odd = lax.axis_index("gz") % 2
-    mine, other = topxy_ref[0:36, :], ra_ref[416:452, :]
-    pair_ref[...] = jnp.concatenate(
-        [jnp.where(odd == 1, other, mine), jnp.where(odd == 1, mine, other)], axis=0
-    )
-
-
-def glue_z(ra, topxy):
-    return pl.pallas_call(
-        glue_z_kernel,
-        in_specs=[VMEM] * 2,
-        out_specs=VMEM,
-        out_shape=jax.ShapeDtypeStruct((72, 128), F32),
-        compiler_params=pltpu.CompilerParams(vmem_limit_bytes=8 << 20),
-        name="glue_z",
-    )(ra, topxy)
-
-
-def block_diagonal(core):
-    zero = jnp.zeros((128, 128), BF16)
-    return jnp.concatenate(
-        [jnp.concatenate([core, zero], axis=1), jnp.concatenate([zero, core], axis=1)], axis=0
-    )
 
 
 def offset_tiles(out_ref, table, cz, masked):
@@ -354,29 +379,26 @@
 
 
 def far_kernel(
-    leafxy_ref, midxy_ref, ra_ref, rb_ref, in_ref, out_ref, core_ref,
+    leafxy_ref, midxy_ref, near_ref, in_ref, out_ref, core_ref,
     far0_ref, far1_ref,
-    leaf_ref, mid_ref, scale_ref, tin_ref, tout_ref, acc_ref,
+    leaf_ref, mid_ref, scale_ref, tin_ref, tout_ref, acc_ref, even_ref, odd_ref,
 ):
     odd = lax.axis_index("gz") % 2
-    leaf_ref[:, 2:6] = leafxy_ref[...]
-    for ref, high in ((ra_ref, 1 - odd), (rb_ref, odd)):
-        for x in range(12):
-            for z in range(2):
-                row = (x * 2 + z) * 12
-                leaf_ref[x, high * 6 + z] = ref[row : row + 12, :]
+    for x in range(12):
+        for z in range(6):
+            leaf_ref[x, 2 * (1 - odd) + z] = leafxy_ref[x, z]
+        for z in range(2):
+            row = (x * 2 + z) * 12
+            leaf_ref[x, 6 * odd + z] = near_ref[row : row + 12, :]
+    zero = jnp.zeros((2, 128), F32)
     for x in range(8):
         for y in range(8):
             row = 288 + (x * 8 + y) * 2
-            a, b = ra_ref[row : row + 2, :], rb_ref[row : row + 2, :]
-            mid_ref[x, y] = jnp.concatenate(
-                [
-                    jnp.where(odd == 1, a, b),
-                    midxy_ref[x, y],
-                    jnp.where(odd == 1, b, a),
-                    jnp.zeros((2, 128), F32),
-                ],
-                axis=0,
+            inner, outer = midxy_ref[x, y], near_ref[row : row + 2, :]
+            mid_ref[x, y] = jnp.where(
+                odd == 1,
+                jnp.concatenate([inner, outer, zero], axis=0),
+                jnp.concatenate([outer, inner, zero], axis=0),
             )
     scale_ref[...] = in_ref[0]
     for x in range(2, 5):
@@ -388,12 +410,13 @@
         offset_tiles(tout_ref.at[cz], out_ref.at[1], cz, False)
 
     far0_ref[...] = jnp.zeros((8, 32, 128), F32)
-    core0 = block_diagonal(core_ref[0])
-
-    @pl.loop(0, 36)
-    def _(step):
+    core0 = core_ref[0]
+
+    def row_of(qx, qy, qz, pair, cz):
+        return (qx + 1 - pair // 2) * 49 + (qy + 1 - pair % 2) * 7 + qz + 1 - cz
+
+    def build_leaf(step, operand_ref):
         qx, qz = step // 6, step % 6
-        blocks = []
         for qy in range(6):
             tiles = []
             for x in range(4):
@@ -401,54 +424,71 @@
                     tiles.append(leaf_ref[2 * x + qx, 2 * z + qz, pl.ds(qy, 4, stride=2), :])
             source = jnp.concatenate(tiles, axis=0)
             for pair in range(4):
-                cx, cy = pair // 2, pair % 2
-                halves = []
                 for cz in range(2):
-                    row = (qx + 1 - cx) * 49 + (qy + 1 - cy) * 7 + qz + 1 - cz
+                    start = ((pair * 2 + cz) * 6 + qy) * 32
+                    row = row_of(qx, qy, qz, pair, cz)
                     scale = jnp.broadcast_to(scale_ref[pl.ds(row, 1), :], (32, 128))
-                    halves.append((source * scale).astype(BF16))
-                blocks.append(jnp.concatenate(halves, axis=1))
-        image = dot(jnp.concatenate(blocks, axis=0), core0)
+                    operand_ref[start : start + 32, :] = (source * scale).astype(BF16)
+
+    def apply_leaf(step, image):
+        qx, qz = step // 6, step % 6
         for pair in range(4):
-            cx, cy = pair // 2, pair % 2
             for cz in range(2):
                 total = far0_ref[pair * 2 + cz]
                 for qy in range(6):
-                    row = (qx + 1 - cx) * 49 + (qy + 1 - cy) * 7 + qz + 1 - cz
+                    row = row_of(qx, qy, qz, pair, cz)
                     scale = jnp.broadcast_to(out_ref[0, pl.ds(row, 1), :], (32, 128))
-                    start = (qy * 4 + pair) * 32
-                    total = total + scale * image[start : start + 32, cz * 128 : cz * 128 + 128]
+                    start = ((pair * 2 + cz) * 6 + qy) * 32
+                    total = total + scale * image[start : start + 32]
                 far0_ref[pair * 2 + cz] = total
 
+    build_leaf(0, even_ref)
+
+    @pl.loop(0, 18)
+    def _(turn):
+        image = dot(even_ref[...], core0)
+        build_leaf(2 * turn + 1, odd_ref)
+        apply_leaf(2 * turn, image)
+        image = dot(odd_ref[...], core0)
+        build_leaf(jnp.minimum(2 * turn + 2, 35), even_ref)
+        apply_leaf(2 * turn + 1, image)
+
     acc_ref[...] = jnp.zeros((8, 32, 128), F32)
-    core1 = block_diagonal(core_ref[1])
-
-    @pl.loop(0, 6)
-    def _(qx):
-        blocks = []
+    core1 = core_ref[1]
+
+    def build_mid(qx, operand_ref):
         for qy in range(6):
             tiles = [mid_ref[2 * x + qx, 2 * y + qy] for x in range(2) for y in range(2)]
             for pair in range(4):
-                cx, cy = pair // 2, pair % 2
-                xy = (qx + 1 - cx) * 7 + qy + 1 - cy
-                halves = []
+                xy = (qx + 1 - pair // 2) * 7 + qy + 1 - pair % 2
                 for cz in range(2):
                     scale = tin_ref[cz, xy]
-                    halves.append(
-                        jnp.concatenate([tile * scale for tile in tiles], axis=0).astype(BF16)
-                    )
-                blocks.append(jnp.concatenate(halves, axis=1))
-        image = dot(jnp.concatenate(blocks, axis=0), core1)
+                    start = ((pair * 2 + cz) * 6 + qy) * 32
+                    operand_ref[start : start + 32, :] = jnp.concatenate(
+                        [tile * scale for tile in tiles], axis=0
+                    ).astype(BF16)
+
+    def apply_mid(qx, image):
         for pair in range(4):
-            cx, cy = pair // 2, pair % 2
             for cz in range(2):
                 total = acc_ref[pair * 2 + cz]
                 for qy in range(6):
-                    scale = tout_ref[cz, (qx + 1 - cx) * 7 + qy + 1 - cy]
+                    scale = tout_ref[cz, (qx + 1 - pair // 2) * 7 + qy + 1 - pair % 2]
                     scale = jnp.concatenate([scale] * 4, axis=0)
-                    start = (qy * 4 + pair) * 32
-                    total = total + scale * image[start : start + 32, cz * 128 : cz * 128 + 128]
+                    start = ((pair * 2 + cz) * 6 + qy) * 32
+                    total = total + scale * image[start : start + 32]
                 acc_ref[pair * 2 + cz] = total
+
+    build_mid(0, even_ref)
+
+    @pl.loop(0, 3)
+    def _(turn):
+        image = dot(even_ref[...], core1)
+        build_mid(2 * turn + 1, odd_ref)
+        apply_mid(2 * turn, image)
+        image = dot(odd_ref[...], core1)
+        build_mid(jnp.minimum(2 * turn + 2, 5), even_ref)
+        apply_mid(2 * turn + 1, image)
 
     for child in range(8):
         for parent in range(4):
@@ -458,10 +498,10 @@
             )
 
 
-def run_far(leafxy, midxy, ra, rb, in_scale, out_scale, transfer):
+def run_far(leafxy, midxy, near, in_scale, out_scale, transfer):
     return pl.pallas_call(
         far_kernel,
-        in_specs=[VMEM] * 7,
+        in_specs=[VMEM] * 6,
         out_specs=[VMEM] * 2,
         out_shape=[
             jax.ShapeDtypeStruct((8, 32, 128), F32),
@@ -474,11 +514,13 @@
             pltpu.VMEM((2, 49, 8, 128), F32),
             pltpu.VMEM((2, 49, 8, 128), F32),
             pltpu.VMEM((8, 32, 128), F32),
+            pltpu.VMEM((1536, 128), BF16),
+            pltpu.VMEM((1536, 128), BF16),
         ],
         cost_estimate=pl.CostEstimate(flops=4 << 30, bytes_accessed=4 << 20, transcendentals=0),
         compiler_params=pltpu.CompilerParams(vmem_limit_bytes=24 << 20),
         name="far",
-    )(leafxy, midxy, ra, rb, in_scale, out_scale, transfer)
+    )(leafxy, midxy, near, in_scale, out_scale, transfer)
 
 
 def force_kernel(
@@ -489,16 +531,15 @@
 ):
     odd = lax.axis_index("gz") % 2
     for xy in range(36):
-        rows = [
-            (ref[xy : xy + 1, :], ref[36 + xy : 37 + xy, :]) for ref in (near_ref, next_ref)
-        ]
-        low = [jnp.where(odd == 1, rows[1][z], rows[0][z]) for z in range(2)]
-        high = [jnp.where(odd == 1, rows[0][z], rows[1][z]) for z in range(2)]
+        near = near_ref[416 + 2 * xy : 418 + 2 * xy, :]
+        behind = next_ref[2 * xy : 2 * xy + 2, :]
         window_ref[xy] = jnp.concatenate(
-            low
-            + [pair_ref[xy : xy + 1, :], pair_ref[36 + xy : 37 + xy, :]]
-            + high
-            + [jnp.zeros((2, 128), F32)],
+            [
+                jnp.where(odd == 1, behind, near),
+                pair_ref[2 * xy : 2 * xy + 2, :],
+                jnp.where(odd == 1, near, behind),
+                jnp.zeros((2, 128), F32),
+            ],
             axis=0,
         )
     lanes = lax.broadcasted_iota(jnp.int32, (8, 128), 0)
@@ -594,7 +635,7 @@
     row = jnp.zeros((8, 128), F32)
     for i in range(9):
         row = jnp.where(lane == i, jnp.sum(sums[i]), row)
-    share_ref[...] = jnp.broadcast_to(row[0:1], (512, 128))
+    share_ref[...] = jnp.broadcast_to(row[0:1], (64, 128))
 
 
 def run_forces(far0, far1, pair, near, following, in_scale, out_scale, transfer, downward, charge, sines, positions, wave):
@@ -604,7 +645,7 @@
         out_specs=[VMEM] * 2,
         out_shape=[
             jax.ShapeDtypeStruct((3, 8, 8, 128), F32),
-            jax.ShapeDtypeStruct((512, 128), F32),
+            jax.ShapeDtypeStruct((64, 128), F32),
         ],
         scratch_shapes=[
             pltpu.VMEM((36, 8, 128), F32),
@@ -617,6 +658,21 @@
         compiler_params=pltpu.CompilerParams(vmem_limit_bytes=24 << 20),
         name="forces",
     )(far0, far1, pair, near, following, in_scale, out_scale, transfer, downward, charge, sines, positions, wave)
+
+
+def fold_kernel(rows_ref, share_ref):
+    share_ref[...] = jnp.broadcast_to(jnp.sum(rows_ref[...], axis=0, keepdims=True), (8, 128))
+
+
+def fold(rows):
+    return pl.pallas_call(
+        fold_kernel,
+        in_specs=[VMEM],
+        out_specs=VMEM,
+        out_shape=jax.ShapeDtypeStruct((8, 128), F32),
+        compiler_params=pltpu.CompilerParams(vmem_limit_bytes=8 << 20),
+        name="fold",
+    )(rows)
 
 
 def virial_kernel(scale, rows_ref, virial_ref):
@@ -649,23 +705,23 @@
     features, positions, box_counts, w_hidden, w_charge, wave_numbers, phases,
     upward, downward, transfer, out_scale, in_scale,
 ):
-    charge, sines, leaf, mid, top, xa, xb = run_atoms(
-        features, positions, box_counts.transpose(0, 2, 1), w_hidden, w_charge.reshape(1, 128), wave_numbers,
-        phases.reshape(1, 128), upward,
+    charge, sines, own, send = run_atoms(
+        features, positions, box_counts.transpose(0, 2, 1), w_hidden, w_charge.reshape(1, 128),
+        wave_numbers, phases.reshape(1, 128), upward,
     )
+    leaf, mid, top, xa, xb = glue_z(swapped(send, "gz", 0), own)
     ra, rb = swapped(xa, "gx", 0), swapped(xb, "gx", 1)
     leaf, mid, top, ya, yb = glue_x(ra, rb, leaf, mid, top)
     ra, rb = swapped(ya, "gy", 0), swapped(yb, "gy", 1)
-    leaf, mid, top, za, zb = glue_y(ra, rb, leaf, mid, top)
-    ra, rb = swapped(za, "gz", 0), swapped(zb, "gz", 1)
-    pair = glue_z(ra, top)
-    near, following = swapped(pair, "gz", 1), swapped(pair, "gz", 2)
-    far0, far1 = run_far(leaf, mid, ra, rb, in_scale, out_scale, transfer)
+    leaf, mid, pair, side = glue_y(ra, rb, leaf, mid, top)
+    near, following = swapped(side, "gz", 1), swapped(pair, "gz", 2)
+    far0, far1 = run_far(leaf, mid, near, in_scale, out_scale, transfer)
     forces, share = run_forces(
         far0, far1, pair, near, following, in_scale, out_scale, transfer, downward, charge, sines,
         positions, wave_numbers,
     )
-    rows = lax.all_to_all(share, ("gx", "gy", "gz"), 0, 0, tiled=True)
+    rows = fold(lax.all_to_all(share, ("gx", "gz"), 0, 0, tiled=True))
+    rows = lax.all_to_all(rows, "gy", 0, 0, tiled=True)
     return forces, run_virial(rows, 1.0 / math.sqrt(4194304))
 
 

time: 112 us -> 111 us (level)
  waiting for transfers between devices: 6.45 us -> 13.4 us
  starting transfers between devices: 37.4 us -> 33.4 us
  Pallas kernels: 28.6 us -> 25.3 us
  local copies, waits for them, and re-layouts: 2.34 us -> 0.95 us
    ppermute x8 -> x7, waiting for transfers between devices: 6.45 us -> 13.4 us  [swapped(): return lax.ppermute(value, axis, pairs)]
    ppermute x8 -> x7, starting transfers between devices: 37.4 us -> 33.4 us  [swapped(): return lax.ppermute(value, axis, pairs)]
    pallas_call x3 -> x4, Pallas kernels: 11.9 us -> 8.81 us  [the longest x1 8.62 us: run_far(): pl.pallas_call(far_kernel, in_specs=[VMEM] * 6, out_specs=[VMEM] * 2, out...]
    unnamed x22 -> x18, local copies, waits for them, and re-layouts: 2.34 us -> 0.95 us
    all_to_all x1 -> x2, blocking collectives: 35.6 us -> 36.4 us  [the longest x1 24.8 us: shards(): rows = fold(lax.all_to_all(share, ('gx', 'gz'), 0, 0, tiled=True))]
  transfers between devices with their start and end apart: 8 -> 7, of which waited for: 2 -> 5; matrix products, arithmetic and copies ran while one was open for 0% -> 0% of each run, Pallas kernels for 11% -> 8%
where the time goes in v2:
time: 111 us; the launch traced here: 110 us
  blocking collectives  36.4 us (33%)
  starting transfers between devices  33.4 us (30%)
  Pallas kernels  25.3 us (23%)
  waiting for transfers between devices  13.4 us (12%)
    ppermute x7, starting transfers between devices, swapped(): return lax.ppermute(value, axis, pairs)  33.4 us
    all_to_all x1, blocking collectives, shards(): rows = fold(lax.all_to_all(share, ('gx', 'gz'), 0, 0, tiled=True))  24.8 us
    ppermute x7, waiting for transfers between devices, swapped(): return lax.ppermute(value, axis, pairs)  13.4 us
    pallas_call x1, Pallas kernels, run_atoms(): pl.pallas_call(atoms_kernel, in_specs=[hbm, hbm, VMEM, hbm, VMEM, VMEM, V...  12.5 us
    all_to_all x1, blocking collectives, shards(): rows = lax.all_to_all(rows, 'gy', 0, 0, tiled=True)  11.6 us
    pallas_call x1, Pallas kernels, run_far(): pl.pallas_call(far_kernel, in_specs=[VMEM] * 6, out_specs=[VMEM] * 2, out...  8.62 us
    pallas_call x1, Pallas kernels, run_forces(): pl.pallas_call(force_kernel, in_specs=[VMEM] * 13, out_specs=[VMEM] * 2,...  3.2 us
  transfers between devices with their start and end apart: 7, of which 5 were waited for; matrix products, arithmetic and copies ran while one was open for 0% of the time, Pallas kernels for 8%

profile of v2, /device:TPU:1, one launch (start us, length us, event | category | flops | bytes accessed | tf_op | source)
XLA Modules:
  0.0 110.3 jit_solution(13224511830349514295)
XLA Ops:
  0.7 12.5 %atoms.1 = (f32[8,8,128]{2,1,0:T(8,128)}, bf16[8,128,1024]{2,1,0:T(8,128)(2,1)}, f32[296,128]{1,0:T(8,128)}, f32[168,128]{1,0:T(8,128)}) custom-call(bf16[8,8,128,128]{3,2,1,0:T(8,128)(2,1)} %feat_hbm.1, f32[3,8,8,128]{3,2,1,0:T(8,128)} %pos_ref.1, s32[8,4,8]{2,1,0:T(4,128)} %bitcast.15, bf16[128,128]{1,0:T(8,128)(2,1)} %wh_hbm.1, bf16[1,128]{1,0:T(2,128)(2,1)} %bitcast.16, ...), custom_call_target="tpu_custom_call" | custom-call | tf_op jit(solution)/shard_map/atoms/pallas_call | solution.py:189
  13.2 4.8 %collective-permute-start = (f32[168,128]{1,0:T(8,128)}, f32[168,128]{1,0:T(8,128)S(1)}, u32[]{:S(2)}, u32[]{:S(2)}) collective-permute-start(f32[168,128]{1,0:T(8,128)} %get-tuple-element.24), channel_id=1, source_target_pairs={{0,1},{1,0},{2,3},{3,2},{4,5},{5,4},{6,7},{7,6},{8,9},{9,8},{10,11... | collective-permute-start | bytes 258056 | tf_op jit(solution)/shard_map/ppermute | solution.py:701
  18.0 2.1 %collective-permute-done.got_ref = f32[168,128]{1,0:T(8,128)S(1)} collective-permute-done((f32[168,128]{1,0:T(8,128)}, f32[168,128]{1,0:T(8,128)S(1)}, u32[]{:S(2)}, u32[]{:S(2)}) %collective-permute-start) | collective-permute-done | bytes 86048 | tf_op jit(solution)/shard_map/ppermute | solution.py:701
  20.1 0.9 copy-done.5
  21.1 8.5 %collective-permute-start.1 = (f32[136,128]{1,0:T(8,128)S(1)}, f32[136,128]{1,0:T(8,128)S(1)}, u32[]{:S(2)}, u32[]{:S(2)}) collective-permute-start(f32[136,128]{1,0:T(8,128)S(1)} %get-tuple-element.26), channel_id=1, source_target_pairs={{0,128},{128,0},{256,384},{384,256},{1,129},{129,1},{257,385},{385... | collective-permute-start | bytes 208904 | tf_op jit(solution)/shard_map/ppermute | solution.py:701
  29.5 5.2 %collective-permute-start.2 = (f32[136,128]{1,0:T(8,128)S(1)}, f32[136,128]{1,0:T(8,128)S(1)}, u32[]{:S(2)}, u32[]{:S(2)}) collective-permute-start(f32[136,128]{1,0:T(8,128)S(1)} %get-tuple-element.27), channel_id=1, source_target_pairs={{0,384},{128,256},{256,128},{384,0},{1,385},{129,257},{257,129},{3... | collective-permute-start | bytes 208904 | tf_op jit(solution)/shard_map/ppermute | solution.py:701
  34.7 0.0 collective-permute-done.1.ra_ref
  34.7 4.4 %collective-permute-done.2.rb_ref = f32[136,128]{1,0:T(8,128)S(1)} collective-permute-done((f32[136,128]{1,0:T(8,128)S(1)}, f32[136,128]{1,0:T(8,128)S(1)}, u32[]{:S(2)}, u32[]{:S(2)}) %collective-permute-start.2) | collective-permute-done | bytes 69664 | tf_op jit(solution)/shard_map/ppermute | solution.py:701
  39.1 0.1 glue_x.1
  39.2 1.9 %collective-permute-start.3 = (f32[232,128]{1,0:T(8,128)S(1)}, f32[232,128]{1,0:T(8,128)S(1)}, u32[]{:S(2)}, u32[]{:S(2)}) collective-permute-start(f32[232,128]{1,0:T(8,128)S(1)} %get-tuple-element.31), channel_id=1, source_target_pairs={{0,16},{16,0},{32,48},{48,32},{64,80},{80,64},{96,112},{112,96},{1... | collective-permute-start | bytes 356360 | tf_op jit(solution)/shard_map/ppermute | solution.py:701
  41.2 4.3 %collective-permute-start.4 = (f32[232,128]{1,0:T(8,128)S(1)}, f32[232,128]{1,0:T(8,128)S(1)}, u32[]{:S(2)}, u32[]{:S(2)}) collective-permute-start(f32[232,128]{1,0:T(8,128)S(1)} %get-tuple-element.32), channel_id=1, source_target_pairs={{0,112},{16,32},{32,16},{48,64},{64,48},{80,96},{96,80},{112,0},{1... | collective-permute-start | bytes 356360 | tf_op jit(solution)/shard_map/ppermute | solution.py:701
  45.5 0.4 collective-permute-done.3.ra_ref
  45.9 2.9 %collective-permute-done.4.rb_ref = f32[232,128]{1,0:T(8,128)S(1)} collective-permute-done((f32[232,128]{1,0:T(8,128)S(1)}, f32[232,128]{1,0:T(8,128)S(1)}, u32[]{:S(2)}, u32[]{:S(2)}) %collective-permute-start.4) | collective-permute-done | bytes 118816 | tf_op jit(solution)/shard_map/ppermute | solution.py:701
  48.8 0.1 glue_y.1
  49.0 6.7 %collective-permute-start.5 = (f32[488,128]{1,0:T(8,128)S(1)}, f32[488,128]{1,0:T(8,128)S(1)}, u32[]{:S(2)}, u32[]{:S(2)}) collective-permute-start(f32[488,128]{1,0:T(8,128)S(1)} %get-tuple-element.38), channel_id=1, source_target_pairs={{0,15},{1,2},{2,1},{3,4},{4,3},{5,6},{6,5},{7,8},{8,7},{9,10},{10,... | collective-permute-start | bytes 749576 | tf_op jit(solution)/shard_map/ppermute | solution.py:701
  55.7 1.9 %collective-permute-start.6 = (f32[72,128]{1,0:T(8,128)S(1)}, f32[72,128]{1,0:T(8,128)S(1)}, u32[]{:S(2)}, u32[]{:S(2)}) collective-permute-start(f32[72,128]{1,0:T(8,128)S(1)} %get-tuple-element.41.pair_ref), channel_id=1, source_target_pairs={{0,3},{1,14},{2,5},{3,0},{4,7},{5,2},{6,9},{7,4},{8,11},{9,6},{10,... | collective-permute-start | bytes 110600 | tf_op jit(solution)/shard_map/ppermute | solution.py:701
  57.6 3.6 %collective-permute-done.5.near_ref = f32[488,128]{1,0:T(8,128)S(1)} collective-permute-done((f32[488,128]{1,0:T(8,128)S(1)}, f32[488,128]{1,0:T(8,128)S(1)}, u32[]{:S(2)}, u32[]{:S(2)}) %collective-permute-start.5) | collective-permute-done | bytes 249888 | tf_op jit(solution)/shard_map/ppermute | solution.py:701
  61.3 0.0 copy-done.6
  61.3 0.0 copy-start
  61.3 0.0 copy-start.3
  61.3 0.0 copy-start.4
  61.3 0.0 copy-start.8
  61.3 8.6 %far.1 = (f32[8,32,128]{2,1,0:T(8,128)S(1)}, f32[32,128]{1,0:T(8,128)S(1)}) custom-call(f32[12,6,12,128]{3,2,1,0:T(8,128)S(1)} %get-tuple-element.36.leafxy_ref, f32[8,8,4,128]{3,2,1,0:T(4,128)S(1)} %get-tuple-element.37.midxy_ref, f32[488,128]{1,0:T(8,128)S(1)} %collective-permute-done.5.near_ref, f32[3,343,128]{2,1,0:T(8,128)S(1)} %copy-done.1, ...), custom_call_target="tpu_custom_call" | custom-call | flops 4294967296 | bytes 4194304 | tf_op jit(solution)/shard_map/far/pallas_call | solution.py:502
  70.0 0.0 collective-permute-done.6.next_ref
  70.0 0.0 copy-done
  70.0 0.0 copy-done.3
  70.0 0.0 copy-done.4
  70.0 0.0 copy-done.7
  70.0 3.2 %forces.1 = (f32[3,8,8,128]{3,2,1,0:T(8,128)}, f32[64,128]{1,0:T(8,128)S(1)}) custom-call(f32[8,32,128]{2,1,0:T(8,128)S(1)} %get-tuple-element.39.far0_ref, f32[32,128]{1,0:T(8,128)S(1)} %get-tuple-element.40.far1_ref, f32[72,128]{1,0:T(8,128)S(1)} %get-tuple-element.41.pair_ref, f32[488,128]{1,0:T(8,128)S(1)} %collective-permute-done.5.near_ref, ...), custom_call_target="tpu_custom_call" | custom-call | tf_op jit(solution)/shard_map/forces/pallas_call | solution.py:642
  73.2 24.8 %all_to_all.22 = f32[64,1,128]{2,1,0:T(1,128)S(1)} all-to-all(f32[64,1,128]{2,1,0:T(1,128)S(1)} %bitcast.12), channel_id=1, replica_groups=mesh['gx'=4,'gy'=8,'gz'=16] {'gx','gz'}, dimensions={0} | all-to-all | bytes 65536 | tf_op jit(solution)/shard_map/all_to_all | solution.py:723
  98.0 11.6 %all_to_all.23 = f32[8,1,128]{2,1,0:T(1,128)S(1)} all-to-all(f32[8,1,128]{2,1,0:T(1,128)S(1)} %bitcast.13), channel_id=1, replica_groups=mesh['gx'=4,'gy'=8,'gz'=16] {'gy'}, dimensions={0} | all-to-all | bytes 8192 | tf_op jit(solution)/shard_map/all_to_all | solution.py:724
  109.6 0.7 virial.1
  (10 shorter events, 0.1 us)
Async XLA Ops:
  0.6 60.6 %copy-start.1 = (f32[3,343,128]{2,1,0:T(8,128)S(1)}, f32[3,343,128]{2,1,0:T(8,128)}, u32[]{:S(2)}) copy-start(f32[3,343,128]{2,1,0:T(8,128)} %in_ref.3) | copy-start | bytes 1580548
  0.6 60.6 %copy-start.2 = (f32[3,343,128]{2,1,0:T(8,128)S(1)}, f32[3,343,128]{2,1,0:T(8,128)}, u32[]{:S(2)}) copy-start(f32[3,343,128]{2,1,0:T(8,128)} %out_ref.3) | copy-start | bytes 1580548
  0.7 60.6 %copy-start.6 = (bf16[3,128,128]{2,1,0:T(8,128)(2,1)S(1)}, bf16[3,128,128]{2,1,0:T(8,128)(2,1)}, u32[]{:S(2)}) copy-start(bf16[3,128,128]{2,1,0:T(8,128)(2,1)} %core_ref.3) | copy-start | bytes 294916
  13.2 6.9 %collective-permute-start = (f32[168,128]{1,0:T(8,128)}, f32[168,128]{1,0:T(8,128)S(1)}, u32[]{:S(2)}, u32[]{:S(2)}) collective-permute-start(f32[168,128]{1,0:T(8,128)} %get-tuple-element.24), channel_id=1, source_target_pairs={{0,1},{1,0},{2,3},{3,2},{4,5},{5,4},{6,7},{7,6},{8,9},{9,8},{10,11... | collective-permute-start | bytes 258056 | tf_op jit(solution)/shard_map/ppermute | solution.py:701
  20.1 0.9 copy-start.5
  21.1 13.6 %collective-permute-start.1 = (f32[136,128]{1,0:T(8,128)S(1)}, f32[136,128]{1,0:T(8,128)S(1)}, u32[]{:S(2)}, u32[]{:S(2)}) collective-permute-start(f32[136,128]{1,0:T(8,128)S(1)} %get-tuple-element.26), channel_id=1, source_target_pairs={{0,128},{128,0},{256,384},{384,256},{1,129},{129,1},{257,385},{385... | collective-permute-start | bytes 208904 | tf_op jit(solution)/shard_map/ppermute | solution.py:701
  29.5 9.6 %collective-permute-start.2 = (f32[136,128]{1,0:T(8,128)S(1)}, f32[136,128]{1,0:T(8,128)S(1)}, u32[]{:S(2)}, u32[]{:S(2)}) collective-permute-start(f32[136,128]{1,0:T(8,128)S(1)} %get-tuple-element.27), channel_id=1, source_target_pairs={{0,384},{128,256},{256,128},{384,0},{1,385},{129,257},{257,129},{3... | collective-permute-start | bytes 208904 | tf_op jit(solution)/shard_map/ppermute | solution.py:701
  39.2 6.7 %collective-permute-start.3 = (f32[232,128]{1,0:T(8,128)S(1)}, f32[232,128]{1,0:T(8,128)S(1)}, u32[]{:S(2)}, u32[]{:S(2)}) collective-permute-start(f32[232,128]{1,0:T(8,128)S(1)} %get-tuple-element.31), channel_id=1, source_target_pairs={{0,16},{16,0},{32,48},{48,32},{64,80},{80,64},{96,112},{112,96},{1... | collective-permute-start | bytes 356360 | tf_op jit(solution)/shard_map/ppermute | solution.py:701
  41.2 7.7 %collective-permute-start.4 = (f32[232,128]{1,0:T(8,128)S(1)}, f32[232,128]{1,0:T(8,128)S(1)}, u32[]{:S(2)}, u32[]{:S(2)}) collective-permute-start(f32[232,128]{1,0:T(8,128)S(1)} %get-tuple-element.32), channel_id=1, source_target_pairs={{0,112},{16,32},{32,16},{48,64},{64,48},{80,96},{96,80},{112,0},{1... | collective-permute-start | bytes 356360 | tf_op jit(solution)/shard_map/ppermute | solution.py:701
  49.0 12.3 %collective-permute-start.5 = (f32[488,128]{1,0:T(8,128)S(1)}, f32[488,128]{1,0:T(8,128)S(1)}, u32[]{:S(2)}, u32[]{:S(2)}) collective-permute-start(f32[488,128]{1,0:T(8,128)S(1)} %get-tuple-element.38), channel_id=1, source_target_pairs={{0,15},{1,2},{2,1},{3,4},{4,3},{5,6},{6,5},{7,8},{8,7},{9,10},{10,... | collective-permute-start | bytes 749576 | tf_op jit(solution)/shard_map/ppermute | solution.py:701
  55.7 14.2 %collective-permute-start.6 = (f32[72,128]{1,0:T(8,128)S(1)}, f32[72,128]{1,0:T(8,128)S(1)}, u32[]{:S(2)}, u32[]{:S(2)}) collective-permute-start(f32[72,128]{1,0:T(8,128)S(1)} %get-tuple-element.41.pair_ref), channel_id=1, source_target_pairs={{0,3},{1,14},{2,5},{3,0},{4,7},{5,2},{6,9},{7,4},{8,11},{9,6},{10,... | collective-permute-start | bytes 110600 | tf_op jit(solution)/shard_map/ppermute | solution.py:701
  61.3 8.7 %copy-start = (bf16[8,128,1024]{2,1,0:T(8,128)(2,1)S(1)}, bf16[8,128,1024]{2,1,0:T(8,128)(2,1)}, u32[]{:S(2)}) copy-start(bf16[8,128,1024]{2,1,0:T(8,128)(2,1)} %get-tuple-element.43.sin_ref) | copy-start | bytes 6291460
  61.3 8.7 %copy-start.3 = (bf16[2,8,128,128]{3,2,1,0:T(8,128)(2,1)S(1)}, bf16[2,8,128,128]{3,2,1,0:T(8,128)(2,1)}, u32[]{:S(2)}) copy-start(bf16[2,8,128,128]{3,2,1,0:T(8,128)(2,1)} %down_ref.1) | copy-start | bytes 1572868
  61.3 8.7 %copy-start.4 = (f32[3,8,8,128]{3,2,1,0:T(8,128)S(1)}, f32[3,8,8,128]{3,2,1,0:T(8,128)}, u32[]{:S(2)}) copy-start(f32[3,8,8,128]{3,2,1,0:T(8,128)} %pos_ref.1) | copy-start | bytes 294916
  61.3 8.7 %copy-start.7 = (f32[8,8,128]{2,1,0:T(8,128)S(1)}, f32[8,8,128]{2,1,0:T(8,128)}, u32[]{:S(2)}) copy-start(f32[8,8,128]{2,1,0:T(8,128)} %get-tuple-element.42.charge_ref) | copy-start | bytes 98308
  61.3 8.7 %copy-start.8 = (f32[3,128]{1,0:T(4,128)S(1)}, f32[3,128]{1,0:T(4,128)}, u32[]{:S(2)}) copy-start(f32[3,128]{1,0:T(4,128)} %wave_ref.3) | copy-start | bytes 4612

commit v3 on v1

--- a/solution.py
+++ b/solution.py
@@ -1,3 +1,4 @@
+import functools
 import math
 
 import jax
@@ -21,10 +22,77 @@
     return jnp.dot(a, b, preferred_element_type=F32)
 
 
+def split(value):
+    high = value.astype(BF16).astype(F32)
+    rest = value - high
+    middle = rest.astype(BF16).astype(F32)
+    return high, middle, rest - middle
+
+
+def wave_table(wave_ref, ph_ref, table_ref):
+    blocks = []
+    for d in range(3):
+        high, middle, low = split(wave_ref[d : d + 1, :] * TURN)
+        for part in (high, middle, low, high, middle, high):
+            blocks.append(jnp.broadcast_to(part, (8, 128)))
+    blocks += list(split(ph_ref[...] * TURN)) + [jnp.zeros((109, 128), F32)]
+    table_ref[...] = jnp.concatenate(blocks, axis=0).T.astype(BF16)
+
+
+def turns_of(step, pos_ref, table_ref):
+    row_y = lax.broadcasted_iota(jnp.int32, (8, 128), 0)
+    blocks = []
+    for d in range(3):
+        spread = []
+        for part in split(pos_ref[d, step] - 0.5):
+            spread.append(
+                jnp.concatenate([jnp.where(row_y == y, part, 0.0) for y in range(8)], axis=1)
+            )
+        blocks += [spread[0]] * 3 + [spread[1]] * 2 + [spread[2]]
+    blocks += [jnp.ones((8, 1024), F32), jnp.zeros((8, 1024), F32)]
+    return dot(table_ref[:, 0:160], jnp.concatenate(blocks, axis=0).astype(BF16))
+
+
+def poly(coefs, u):
+    value = coefs[-1]
+    for coef in coefs[-2::-1]:
+        value = value * u + coef
+    return value
+
+
+def sines_kernel(start, pos_ref, wave_ref, ph_ref, _, sin_ref, table_ref):
+    wave_table(wave_ref, ph_ref, table_ref)
+
+    @pl.loop(0, sin_ref.shape[0])
+    def _(x):
+        turns = turns_of(start + x, pos_ref, table_ref)
+        for y in range(8):
+            t = turns[:, y * 128 : (y + 1) * 128]
+            r = t - jnp.round(t)
+            u = r * r
+            sin_ref[x, :, y * 128 : (y + 1) * 128] = (
+                poly(SIN_HALF, u) * r * poly(COS_HALF, u)
+            ).astype(BF16)
+
+
+def run_sines(positions, wave, phases, after, start, planes):
+    return pl.pallas_call(
+        functools.partial(sines_kernel, start),
+        in_specs=[VMEM] * 4,
+        out_specs=VMEM,
+        out_shape=jax.ShapeDtypeStruct((planes, 128, 1024), BF16),
+        scratch_shapes=[pltpu.VMEM((128, 256), BF16)],
+        cost_estimate=pl.CostEstimate(flops=1 << 30, bytes_accessed=6 << 20, transcendentals=0),
+        compiler_params=pltpu.CompilerParams(vmem_limit_bytes=16 << 20),
+        name="sines",
+    )(positions, wave, phases, after)
+
+
 def atoms_kernel(
     feat_hbm, pos_hbm, cnt_ref, wh_hbm, wc_ref, wave_ref, ph_ref, up_hbm,
-    charge_ref, sin_ref, leaf_ref, mid_ref, top_ref, sa_ref, sb_ref,
-    feat_ref, pos_ref, wh_ref, up_ref, cols_ref, cos_ref, low_ref, plane_sems, sems,
+    charge_ref, own_ref, sa_ref, sb_ref,
+    feat_ref, pos_ref, wh_ref, up_ref, table_ref, cos_ref, low_ref, leaf_ref, mid_ref,
+    plane_sems, sems,
 ):
     def plane(x):
         return pltpu.make_async_copy(feat_hbm.at[x], feat_ref.at[x], plane_sems.at[x])
@@ -40,13 +108,7 @@
     for x in range(1, 8):
         plane(x).start()
     others[2].start()
-
-    table = jnp.concatenate(
-        [wave_ref[...] * TURN, ph_ref[...] * TURN, jnp.zeros((4, 128), F32)], axis=0
-    )
-    columns = jnp.concatenate([table] * 16, axis=0).T
-    for d in range(4):
-        cols_ref[d] = jnp.broadcast_to(columns[:, d : d + 1], (128, 128))
+    wave_table(wave_ref, ph_ref, table_ref)
     others[0].wait()
     others[1].wait()
 
@@ -54,17 +116,17 @@
     def _(x):
         plane(x).wait()
         atoms_plane(
-            x, feat_ref, pos_ref, cnt_ref, wh_ref, wc_ref, charge_ref, sin_ref, leaf_ref,
-            cols_ref, cos_ref, low_ref,
+            x, feat_ref, pos_ref, cnt_ref, wh_ref, wc_ref, charge_ref, leaf_ref, table_ref,
+            cos_ref, low_ref,
         )
 
     others[2].wait()
-    atoms_lift(leaf_ref, up_ref, mid_ref, top_ref, sa_ref, sb_ref)
+    atoms_lift(leaf_ref, up_ref, mid_ref, own_ref, sa_ref, sb_ref)
 
 
 def atoms_plane(
-    step, feat_ref, pos_ref, cnt_ref, wh_ref, wc_ref, charge_ref, sin_ref, leaf_ref,
-    cols_ref, cos_ref, low_ref,
+    step, feat_ref, pos_ref, cnt_ref, wh_ref, wc_ref, charge_ref, leaf_ref, table_ref,
+    cos_ref, low_ref,
 ):
     lane_box = lax.broadcasted_iota(jnp.int32, (8, 128), 1) // 32
     lane_slot = lax.broadcasted_iota(jnp.int32, (8, 128), 1) % 32
@@ -103,25 +165,15 @@
     spread_high = spread.astype(BF16)
     spread_low = (spread - spread_high.astype(F32)).astype(BF16)
 
+    turns = turns_of(step, pos_ref, table_ref)
     for y in range(8):
-        p0 = pos_ref[0, step, y : y + 1, :] - 0.5
-        p1 = pos_ref[1, step, y : y + 1, :] - 0.5
-        p2 = pos_ref[2, step, y : y + 1, :] - 0.5
-        turns = cols_ref[3] + cols_ref[0] * p0 + cols_ref[1] * p1 + cols_ref[2] * p2
-        r = turns - jnp.round(turns)
-        u = r * r
-        s = SIN_HALF[3]
-        for coef in SIN_HALF[2::-1]:
-            s = s * u + coef
-        s = s * r
-        c = COS_HALF[4]
-        for coef in COS_HALF[3::-1]:
-            c = c * u + coef
+        t = turns[:, y * 128 : (y + 1) * 128]
+        r = t - jnp.round(t)
+        s = poly(SIN_HALF, r * r) * r
         cosine = 1.0 - s * s
         cosine_high = cosine.astype(BF16)
         cos_ref[:, y * 128 : (y + 1) * 128] = cosine_high
         low_ref[:, y * 128 : (y + 1) * 128] = (cosine - cosine_high.astype(F32)).astype(BF16)
-        sin_ref[step, :, y * 128 : (y + 1) * 128] = (s * c).astype(BF16)
     moments = lax.dot_general(
         jnp.concatenate([spread_high, spread_low], axis=0), cos_ref[...], NT,
         preferred_element_type=F32,
@@ -132,7 +184,7 @@
         leaf_ref[step, z] = moments[z * 8 : (z + 1) * 8]
 
 
-def atoms_lift(leaf_ref, up_ref, mid_ref, top_ref, sa_ref, sb_ref):
+def atoms_lift(leaf_ref, up_ref, mid_ref, own_ref, sa_ref, sb_ref):
     total = jnp.zeros((32, 128), F32)
     for child in range(8):
         cx, cy, cz = child // 4, child // 2 % 2, child % 2
@@ -163,7 +215,12 @@
             axis=0,
         )
         crown = crown + dot(rows.astype(BF16), up_ref[1, child])
-    top_ref[...] = crown[0:4]
+    own_ref[0:256, :] = leaf_ref[...].reshape(256, 128)
+    for x in range(4):
+        for y in range(4):
+            row = 256 + (x * 4 + y) * 2
+            own_ref[row : row + 2, :] = mid_ref[x, y]
+    own_ref[288:296, :] = crown
     odd = lax.axis_index("gx") % 2
     for ref, high in ((sa_ref, 1 - odd), (sb_ref, odd)):
         for x in range(2):
@@ -182,13 +239,10 @@
     return pl.pallas_call(
         atoms_kernel,
         in_specs=[hbm, hbm, VMEM, hbm, VMEM, VMEM, VMEM, hbm],
-        out_specs=[VMEM] * 7,
+        out_specs=[VMEM] * 4,
         out_shape=[
             jax.ShapeDtypeStruct((8, 8, 128), F32),
-            jax.ShapeDtypeStruct((8, 128, 1024), BF16),
-            jax.ShapeDtypeStruct((8, 4, 8, 128), F32),
-            jax.ShapeDtypeStruct((4, 4, 2, 128), F32),
-            jax.ShapeDtypeStruct((4, 128), F32),
+            jax.ShapeDtypeStruct((296, 128), F32),
             jax.ShapeDtypeStruct((88, 128), F32),
             jax.ShapeDtypeStruct((88, 128), F32),
         ],
@@ -197,9 +251,11 @@
             pltpu.VMEM((3, 8, 8, 128), F32),
             pltpu.VMEM((128, 128), BF16),
             pltpu.VMEM((2, 8, 128, 128), BF16),
-            pltpu.VMEM((4, 128, 128), F32),
+            pltpu.VMEM((128, 256), BF16),
             pltpu.VMEM((128, 1024), BF16),
             pltpu.VMEM((128, 1024), BF16),
+            pltpu.VMEM((8, 4, 8, 128), F32),
+            pltpu.VMEM((4, 4, 2, 128), F32),
             pltpu.SemaphoreType.DMA((8,)),
             pltpu.SemaphoreType.DMA((3,)),
         ],
@@ -208,10 +264,13 @@
     )(features, positions, box_counts, w_hidden, w_charge, wave, phases, upward)
 
 
-def glue_x_kernel(ra_ref, rb_ref, leaf_ref, mid_ref, top_ref, leafx_ref, midx_ref, topx_ref, ya_ref, yb_ref):
+def glue_x_kernel(ra_ref, rb_ref, own_ref, _, leafx_ref, midx_ref, topx_ref, ya_ref, yb_ref):
     odd = lax.axis_index("gx") % 2
-    leafx_ref[2:10] = leaf_ref[...]
-    midx_ref[2:6] = mid_ref[...]
+    leafx_ref[2:10] = own_ref[0:256, :].reshape(8, 4, 8, 128)
+    for x in range(4):
+        for y in range(4):
+            row = 256 + (x * 4 + y) * 2
+            midx_ref[2 + x, y] = own_ref[row : row + 2, :]
     for ref, high in ((ra_ref, 1 - odd), (rb_ref, odd)):
         for x in range(2):
             for z in range(4):
@@ -224,7 +283,7 @@
     topx_ref[...] = jnp.concatenate(
         [
             jnp.where(odd == 1, ta, tb),
-            top_ref[...],
+            own_ref[288:292, :],
             jnp.where(odd == 1, tb, ta),
             jnp.zeros((4, 128), F32),
         ],
@@ -246,10 +305,10 @@
         ref[128:144, :] = topx_ref[...]
 
 
-def glue_x(ra, rb, leaf, mid, top):
+def glue_x(ra, rb, own, front):
     return pl.pallas_call(
         glue_x_kernel,
-        in_specs=[VMEM] * 5,
+        in_specs=[VMEM] * 3 + [pl.BlockSpec(memory_space=pl.ANY)],
         out_specs=[VMEM] * 5,
         out_shape=[
             jax.ShapeDtypeStruct((12, 4, 8, 128), F32),
@@ -260,10 +319,10 @@
         ],
         compiler_params=pltpu.CompilerParams(vmem_limit_bytes=8 << 20),
         name="glue_x",
-    )(ra, rb, leaf, mid, top)
-
-
-def glue_y_kernel(ra_ref, rb_ref, leafx_ref, midx_ref, topx_ref, leafxy_ref, midxy_ref, topxy_ref, za_ref, zb_ref):
+    )(ra, rb, own, front)
+
+
+def glue_y_kernel(ra_ref, rb_ref, leafx_ref, midx_ref, topx_ref, _, leafxy_ref, midxy_ref, topxy_ref, za_ref, zb_ref):
     odd = lax.axis_index("gy") % 2
     for x in range(12):
         for z in range(4):
@@ -298,10 +357,10 @@
     za_ref[416:456, :] = topxy_ref[...]
 
 
-def glue_y(ra, rb, leafx, midx, topx):
+def glue_y(ra, rb, leafx, midx, topx, back):
     return pl.pallas_call(
         glue_y_kernel,
-        in_specs=[VMEM] * 5,
+        in_specs=[VMEM] * 5 + [pl.BlockSpec(memory_space=pl.ANY)],
         out_specs=[VMEM] * 5,
         out_shape=[
             jax.ShapeDtypeStruct((12, 4, 12, 128), F32),
@@ -312,7 +371,7 @@
         ],
         compiler_params=pltpu.CompilerParams(vmem_limit_bytes=8 << 20),
         name="glue_y",
-    )(ra, rb, leafx, midx, topx)
+    )(ra, rb, leafx, midx, topx, back)
 
 
 def glue_z_kernel(ra_ref, topxy_ref, pair_ref):
@@ -332,13 +391,6 @@
         compiler_params=pltpu.CompilerParams(vmem_limit_bytes=8 << 20),
         name="glue_z",
     )(ra, topxy)
-
-
-def block_diagonal(core):
-    zero = jnp.zeros((128, 128), BF16)
-    return jnp.concatenate(
-        [jnp.concatenate([core, zero], axis=1), jnp.concatenate([zero, core], axis=1)], axis=0
-    )
 
 
 def offset_tiles(out_ref, table, cz, masked):
@@ -356,7 +408,7 @@
 def far_kernel(
     leafxy_ref, midxy_ref, ra_ref, rb_ref, in_ref, out_ref, core_ref,
     far0_ref, far1_ref,
-    leaf_ref, mid_ref, scale_ref, tin_ref, tout_ref, acc_ref,
+    leaf_ref, mid_ref, scale_ref, tin_ref, tout_ref, acc_ref, even_ref, odd_ref,
 ):
     odd = lax.axis_index("gz") % 2
     leaf_ref[:, 2:6] = leafxy_ref[...]
@@ -388,12 +440,13 @@
         offset_tiles(tout_ref.at[cz], out_ref.at[1], cz, False)
 
     far0_ref[...] = jnp.zeros((8, 32, 128), F32)
-    core0 = block_diagonal(core_ref[0])
-
-    @pl.loop(0, 36)
-    def _(step):
+    core0 = core_ref[0]
+
+    def row_of(qx, qy, qz, pair, cz):
+        return (qx + 1 - pair // 2) * 49 + (qy + 1 - pair % 2) * 7 + qz + 1 - cz
+
+    def build_leaf(step, operand_ref):
         qx, qz = step // 6, step % 6
-        blocks = []
         for qy in range(6):
             tiles = []
             for x in range(4):
@@ -401,54 +454,71 @@
                     tiles.append(leaf_ref[2 * x + qx, 2 * z + qz, pl.ds(qy, 4, stride=2), :])
             source = jnp.concatenate(tiles, axis=0)
             for pair in range(4):
-                cx, cy = pair // 2, pair % 2
-                halves = []
                 for cz in range(2):
-                    row = (qx + 1 - cx) * 49 + (qy + 1 - cy) * 7 + qz + 1 - cz
+                    start = ((pair * 2 + cz) * 6 + qy) * 32
+                    row = row_of(qx, qy, qz, pair, cz)
                     scale = jnp.broadcast_to(scale_ref[pl.ds(row, 1), :], (32, 128))
-                    halves.append((source * scale).astype(BF16))
-                blocks.append(jnp.concatenate(halves, axis=1))
-        image = dot(jnp.concatenate(blocks, axis=0), core0)
+                    operand_ref[start : start + 32, :] = (source * scale).astype(BF16)
+
+    def apply_leaf(step, image):
+        qx, qz = step // 6, step % 6
         for pair in range(4):
-            cx, cy = pair // 2, pair % 2
             for cz in range(2):
                 total = far0_ref[pair * 2 + cz]
                 for qy in range(6):
-                    row = (qx + 1 - cx) * 49 + (qy + 1 - cy) * 7 + qz + 1 - cz
+                    row = row_of(qx, qy, qz, pair, cz)
                     scale = jnp.broadcast_to(out_ref[0, pl.ds(row, 1), :], (32, 128))
-                    start = (qy * 4 + pair) * 32
-                    total = total + scale * image[start : start + 32, cz * 128 : cz * 128 + 128]
+                    start = ((pair * 2 + cz) * 6 + qy) * 32
+                    total = total + scale * image[start : start + 32]
                 far0_ref[pair * 2 + cz] = total
 
+    build_leaf(0, even_ref)
+
+    @pl.loop(0, 18)
+    def _(turn):
+        image = dot(even_ref[...], core0)
+        build_leaf(2 * turn + 1, odd_ref)
+        apply_leaf(2 * turn, image)
+        image = dot(odd_ref[...], core0)
+        build_leaf(jnp.minimum(2 * turn + 2, 35), even_ref)
+        apply_leaf(2 * turn + 1, image)
+
     acc_ref[...] = jnp.zeros((8, 32, 128), F32)
-    core1 = block_diagonal(core_ref[1])
-
-    @pl.loop(0, 6)
-    def _(qx):
-        blocks = []
+    core1 = core_ref[1]
+
+    def build_mid(qx, operand_ref):
         for qy in range(6):
             tiles = [mid_ref[2 * x + qx, 2 * y + qy] for x in range(2) for y in range(2)]
             for pair in range(4):
-                cx, cy = pair // 2, pair % 2
-                xy = (qx + 1 - cx) * 7 + qy + 1 - cy
-                halves = []
+                xy = (qx + 1 - pair // 2) * 7 + qy + 1 - pair % 2
                 for cz in range(2):
                     scale = tin_ref[cz, xy]
-                    halves.append(
-                        jnp.concatenate([tile * scale for tile in tiles], axis=0).astype(BF16)
-                    )
-                blocks.append(jnp.concatenate(halves, axis=1))
-        image = dot(jnp.concatenate(blocks, axis=0), core1)
+                    start = ((pair * 2 + cz) * 6 + qy) * 32
+                    operand_ref[start : start + 32, :] = jnp.concatenate(
+                        [tile * scale for tile in tiles], axis=0
+                    ).astype(BF16)
+
+    def apply_mid(qx, image):
         for pair in range(4):
-            cx, cy = pair // 2, pair % 2
             for cz in range(2):
                 total = acc_ref[pair * 2 + cz]
                 for qy in range(6):
-                    scale = tout_ref[cz, (qx + 1 - cx) * 7 + qy + 1 - cy]
+                    scale = tout_ref[cz, (qx + 1 - pair // 2) * 7 + qy + 1 - pair % 2]
                     scale = jnp.concatenate([scale] * 4, axis=0)
-                    start = (qy * 4 + pair) * 32
-                    total = total + scale * image[start : start + 32, cz * 128 : cz * 128 + 128]
+                    start = ((pair * 2 + cz) * 6 + qy) * 32
+                    total = total + scale * image[start : start + 32]
                 acc_ref[pair * 2 + cz] = total
+
+    build_mid(0, even_ref)
+
+    @pl.loop(0, 3)
+    def _(turn):
+        image = dot(even_ref[...], core1)
+        build_mid(2 * turn + 1, odd_ref)
+        apply_mid(2 * turn, image)
+        image = dot(odd_ref[...], core1)
+        build_mid(jnp.minimum(2 * turn + 2, 5), even_ref)
+        apply_mid(2 * turn + 1, image)
 
     for child in range(8):
         for parent in range(4):
@@ -474,6 +544,8 @@
             pltpu.VMEM((2, 49, 8, 128), F32),
             pltpu.VMEM((2, 49, 8, 128), F32),
             pltpu.VMEM((8, 32, 128), F32),
+            pltpu.VMEM((1536, 128), BF16),
+            pltpu.VMEM((1536, 128), BF16),
         ],
         cost_estimate=pl.CostEstimate(flops=4 << 30, bytes_accessed=4 << 20, transcendentals=0),
         compiler_params=pltpu.CompilerParams(vmem_limit_bytes=24 << 20),
@@ -483,7 +555,7 @@
 
 def force_kernel(
     far0_ref, far1_ref, pair_ref, near_ref, next_ref, in_ref, out_ref, core_ref, down_ref,
-    charge_ref, sin_ref, pos_ref, wave_ref,
+    charge_ref, front_ref, back_ref, pos_ref, wave_ref,
     forces_ref, share_ref,
     window_ref, tin_ref, tout_ref, operand_ref, mid_ref, local_ref,
 ):
@@ -556,12 +628,11 @@
     place_y0 = (base_y + row_y).astype(F32)
     place_z0 = (base_z + lane_box).astype(F32)
 
-    def one_plane(x, sums):
+    def one_plane(x, sums, sines):
         local = local_ref[x].reshape(32, 128)
         weights = jnp.concatenate([local * wave_ref[d : d + 1, :] for d in range(3)], axis=0)
         high = weights.astype(BF16)
         low = (weights - high.astype(F32)).astype(BF16)
-        sines = sin_ref[x]
         product = dot(
             jnp.concatenate([high, low], axis=1), jnp.concatenate([sines, sines], axis=0)
         )
@@ -589,7 +660,9 @@
             sums[d * 3 + e] + places[d] * found[e] for d in range(3) for e in range(3)
         )
 
-    sums = lax.fori_loop(0, 8, one_plane, (jnp.zeros((8, 128), F32),) * 9)
+    sums = (jnp.zeros((8, 128), F32),) * 9
+    sums = lax.fori_loop(0, 4, lambda x, sums: one_plane(x, sums, front_ref[x]), sums)
+    sums = lax.fori_loop(0, 4, lambda x, sums: one_plane(x + 4, sums, back_ref[x]), sums)
     lane = lax.broadcasted_iota(jnp.int32, (8, 128), 1)
     row = jnp.zeros((8, 128), F32)
     for i in range(9):
@@ -597,10 +670,10 @@
     share_ref[...] = jnp.broadcast_to(row[0:1], (512, 128))
 
 
-def run_forces(far0, far1, pair, near, following, in_scale, out_scale, transfer, downward, charge, sines, positions, wave):
+def run_forces(far0, far1, pair, near, following, in_scale, out_scale, transfer, downward, charge, front, back, positions, wave):
     return pl.pallas_call(
         force_kernel,
-        in_specs=[VMEM] * 13,
+        in_specs=[VMEM] * 14,
         out_specs=[VMEM] * 2,
         out_shape=[
             jax.ShapeDtypeStruct((3, 8, 8, 128), F32),
@@ -616,7 +689,7 @@
         ],
         compiler_params=pltpu.CompilerParams(vmem_limit_bytes=24 << 20),
         name="forces",
-    )(far0, far1, pair, near, following, in_scale, out_scale, transfer, downward, charge, sines, positions, wave)
+    )(far0, far1, pair, near, following, in_scale, out_scale, transfer, downward, charge, front, back, positions, wave)
 
 
 def virial_kernel(scale, rows_ref, virial_ref):
@@ -649,20 +722,23 @@
     features, positions, box_counts, w_hidden, w_charge, wave_numbers, phases,
     upward, downward, transfer, out_scale, in_scale,
 ):
-    charge, sines, leaf, mid, top, xa, xb = run_atoms(
-        features, positions, box_counts.transpose(0, 2, 1), w_hidden, w_charge.reshape(1, 128), wave_numbers,
-        phases.reshape(1, 128), upward,
+    phases = phases.reshape(1, 128)
+    charge, own, xa, xb = run_atoms(
+        features, positions, box_counts.transpose(0, 2, 1), w_hidden, w_charge.reshape(1, 128),
+        wave_numbers, phases, upward,
     )
+    front = run_sines(positions, wave_numbers, phases, own, 0, 4)
     ra, rb = swapped(xa, "gx", 0), swapped(xb, "gx", 1)
-    leaf, mid, top, ya, yb = glue_x(ra, rb, leaf, mid, top)
+    leaf, mid, top, ya, yb = glue_x(ra, rb, own, front)
+    back = run_sines(positions, wave_numbers, phases, top, 4, 4)
     ra, rb = swapped(ya, "gy", 0), swapped(yb, "gy", 1)
-    leaf, mid, top, za, zb = glue_y(ra, rb, leaf, mid, top)
+    leaf, mid, top, za, zb = glue_y(ra, rb, leaf, mid, top, back)
     ra, rb = swapped(za, "gz", 0), swapped(zb, "gz", 1)
     pair = glue_z(ra, top)
     near, following = swapped(pair, "gz", 1), swapped(pair, "gz", 2)
     far0, far1 = run_far(leaf, mid, ra, rb, in_scale, out_scale, transfer)
     forces, share = run_forces(
-        far0, far1, pair, near, following, in_scale, out_scale, transfer, downward, charge, sines,
+        far0, far1, pair, near, following, in_scale, out_scale, transfer, downward, charge, front, back,
         positions, wave_numbers,
     )
     rows = lax.all_to_all(share, ("gx", "gy", "gz"), 0, 0, tiled=True)

time: 112 us -> 104 us (0.929)
  waiting for transfers between devices: 6.45 us -> 1.29 us
  local copies, waits for them, and re-layouts: 2.34 us -> 0.95 us
    ppermute x8, waiting for transfers between devices: 6.45 us -> 1.29 us  [swapped(): return lax.ppermute(value, axis, pairs)]
    pallas_call x3 -> x5, Pallas kernels: 3.4 us -> 7.56 us  [the longest x2 4.18 us: run_sines(): pl.pallas_call(functools.partial(sines_kernel, start), in_specs=[VMEM] *...]
    pallas_call x1, Pallas kernels: 11.8 us -> 8.55 us  [run_far(): pl.pallas_call(far_kernel, in_specs=[VMEM] * 7, out_specs=[VMEM] * 2, out...]
    pallas_call x1, Pallas kernels: 12.7 us -> 11 us  [run_atoms(): pl.pallas_call(atoms_kernel, in_specs=[hbm, hbm, VMEM, hbm, VMEM, VMEM, V...]
    unnamed x22 -> x18, local copies, waits for them, and re-layouts: 2.34 us -> 0.95 us
  transfers between devices with their start and end apart: 8 -> 8, of which waited for: 2 -> 1; matrix products, arithmetic and copies ran while one was open for 0% -> 0% of each run, Pallas kernels for 11% -> 12%
where the time goes in v3:
time: 104 us
  starting transfers between devices  37.9 us (36%)
  blocking collectives  35.1 us (34%)
  Pallas kernels  27.8 us (27%)
  waiting for transfers between devices  1.29 us (1%)
    ppermute x8, starting transfers between devices, swapped(): return lax.ppermute(value, axis, pairs)  37.9 us
    all_to_all x1, blocking collectives, shards(): rows = lax.all_to_all(share, ('gx', 'gy', 'gz'), 0, 0, tiled=True)  35.1 us
    pallas_call x1, Pallas kernels, run_atoms(): pl.pallas_call(atoms_kernel, in_specs=[hbm, hbm, VMEM, hbm, VMEM, VMEM, V...  11 us
    pallas_call x1, Pallas kernels, run_far(): pl.pallas_call(far_kernel, in_specs=[VMEM] * 7, out_specs=[VMEM] * 2, out...  8.55 us
    pallas_call x2, Pallas kernels, run_sines(): pl.pallas_call(functools.partial(sines_kernel, start), in_specs=[VMEM] *...  4.18 us
    pallas_call x1, Pallas kernels, run_forces(): pl.pallas_call(force_kernel, in_specs=[VMEM] * 14, out_specs=[VMEM] * 2,...  3.19 us
  transfers between devices with their start and end apart: 8, of which 1 were waited for; matrix products, arithmetic and copies ran while one was open for 0% of the time, Pallas kernels for 12%

profile of v3, /device:TPU:1, one launch (start us, length us, event | category | flops | bytes accessed | tf_op | source)
XLA Modules:
  0.0 104.0 jit_solution(17095208942954922418)
XLA Ops:
  0.6 0.0 copy-start.7
  0.6 0.0 copy-start.3
  0.7 11.0 %atoms.1 = (f32[8,8,128]{2,1,0:T(8,128)}, f32[296,128]{1,0:T(8,128)}, f32[88,128]{1,0:T(8,128)}, f32[88,128]{1,0:T(8,128)}) custom-call(bf16[8,8,128,128]{3,2,1,0:T(8,128)(2,1)} %feat_hbm.1, f32[3,8,8,128]{3,2,1,0:T(8,128)} %pos_ref.5, s32[8,4,8]{2,1,0:T(4,128)} %bitcast.12, bf16[128,128]{1,0:T(8,128)(2,1)} %wh_hbm.1, bf16[1,128]{1,0:T(2,128)(2,1)} %bitcast.13, ...), custom_call_target="tpu_custom_call" | custom-call | tf_op jit(solution)/shard_map/atoms/pallas_call | solution.py:239
  11.7 8.8 %collective-permute-start = (f32[88,128]{1,0:T(8,128)}, f32[88,128]{1,0:T(8,128)S(1)}, u32[]{:S(2)}, u32[]{:S(2)}) collective-permute-start(f32[88,128]{1,0:T(8,128)} %get-tuple-element.20), channel_id=1, source_target_pairs={{0,128},{128,0},{256,384},{384,256},{1,129},{129,1},{257,385},{385... | collective-permute-start | bytes 135176 | tf_op jit(solution)/shard_map/ppermute | solution.py:718
  20.5 5.2 %collective-permute-start.1 = (f32[88,128]{1,0:T(8,128)}, f32[88,128]{1,0:T(8,128)S(1)}, u32[]{:S(2)}, u32[]{:S(2)}) collective-permute-start(f32[88,128]{1,0:T(8,128)} %get-tuple-element.21), channel_id=1, source_target_pairs={{0,384},{128,256},{256,128},{384,0},{1,385},{129,257},{257,129},{3... | collective-permute-start | bytes 135176 | tf_op jit(solution)/shard_map/ppermute | solution.py:718
  25.7 0.9 copy-done.4
  26.6 2.1 %sines.2._.front_ref = bf16[4,128,1024]{2,1,0:T(8,128)(2,1)S(1)} custom-call(f32[3,8,8,128]{3,2,1,0:T(8,128)S(1)} %copy-done.3, f32[3,128]{1,0:T(4,128)S(1)} %copy-done.7, f32[1,128]{1,0:T(1,128)S(1)} %bitcast.10, f32[296,128]{1,0:T(8,128)S(1)} %copy-done.4), custom_call_target="tpu_custom_call" | custom-call | flops 1073741824 | bytes 6291456 | tf_op jit(solution)/shard_map/sines/pallas_call | solution.py:79
  28.7 0.0 collective-permute-done.ra_ref
  28.7 1.3 %collective-permute-done.1.rb_ref = f32[88,128]{1,0:T(8,128)S(1)} collective-permute-done((f32[88,128]{1,0:T(8,128)}, f32[88,128]{1,0:T(8,128)S(1)}, u32[]{:S(2)}, u32[]{:S(2)}) %collective-permute-start.1) | collective-permute-done | bytes 45088 | tf_op jit(solution)/shard_map/ppermute | solution.py:718
  29.9 0.1 glue_x.1
  30.0 2.0 %collective-permute-start.2 = (f32[144,128]{1,0:T(8,128)S(1)}, f32[144,128]{1,0:T(8,128)S(1)}, u32[]{:S(2)}, u32[]{:S(2)}) collective-permute-start(f32[144,128]{1,0:T(8,128)S(1)} %get-tuple-element.23), channel_id=1, source_target_pairs={{0,16},{16,0},{32,48},{48,32},{64,80},{80,64},{96,112},{112,96},{1... | collective-permute-start | bytes 221192 | tf_op jit(solution)/shard_map/ppermute | solution.py:718
  32.0 4.9 %collective-permute-start.3 = (f32[144,128]{1,0:T(8,128)S(1)}, f32[144,128]{1,0:T(8,128)S(1)}, u32[]{:S(2)}, u32[]{:S(2)}) collective-permute-start(f32[144,128]{1,0:T(8,128)S(1)} %get-tuple-element.24), channel_id=1, source_target_pairs={{0,112},{16,32},{32,16},{48,64},{64,48},{80,96},{96,80},{112,0},{1... | collective-permute-start | bytes 221192 | tf_op jit(solution)/shard_map/ppermute | solution.py:718
  36.8 0.0 copy-start
  36.8 0.0 copy-start.1
  36.9 0.0 copy-start.5
  36.9 2.1 %sines.3._.back_ref = bf16[4,128,1024]{2,1,0:T(8,128)(2,1)S(1)} custom-call(f32[3,8,8,128]{3,2,1,0:T(8,128)S(1)} %copy-done.3, f32[3,128]{1,0:T(4,128)S(1)} %copy-done.7, f32[1,128]{1,0:T(1,128)S(1)} %bitcast.11, f32[16,128]{1,0:T(8,128)S(1)} %get-tuple-element.27._.topx_ref), custom_call_target="tpu_custom_call" | custom-call | flops 1073741824 | bytes 6291456 | tf_op jit(solution)/shard_map/sines/pallas_call | solution.py:79
  39.0 0.0 collective-permute-done.2.ra_ref
  39.0 0.0 collective-permute-done.3.rb_ref
  39.0 0.1 glue_y.1
  39.1 3.1 %collective-permute-start.4 = (f32[456,128]{1,0:T(8,128)S(1)}, f32[456,128]{1,0:T(8,128)S(1)}, u32[]{:S(2)}, u32[]{:S(2)}) collective-permute-start(f32[456,128]{1,0:T(8,128)S(1)} %get-tuple-element.30), channel_id=1, source_target_pairs={{0,1},{1,0},{2,3},{3,2},{4,5},{5,4},{6,7},{7,6},{8,9},{9,8},{10,11... | collective-permute-start | bytes 700424 | tf_op jit(solution)/shard_map/ppermute | solution.py:718
  42.2 6.6 %collective-permute-start.5 = (f32[416,128]{1,0:T(8,128)S(1)}, f32[416,128]{1,0:T(8,128)S(1)}, u32[]{:S(2)}, u32[]{:S(2)}) collective-permute-start(f32[416,128]{1,0:T(8,128)S(1)} %get-tuple-element.31), channel_id=1, source_target_pairs={{0,15},{1,2},{2,1},{3,4},{4,3},{5,6},{6,5},{7,8},{8,7},{9,10},{10,... | collective-permute-start | bytes 638984 | tf_op jit(solution)/shard_map/ppermute | solution.py:718
  48.8 0.0 collective-permute-done.4.ra_ref
  48.8 3.1 %collective-permute-start.7 = (f32[72,128]{1,0:T(8,128)S(1)}, f32[72,128]{1,0:T(8,128)S(1)}, u32[]{:S(2)}, u32[]{:S(2)}) collective-permute-start(f32[72,128]{1,0:T(8,128)S(1)} %glue_z.1.pair_ref), channel_id=1, source_target_pairs={{0,3},{1,14},{2,5},{3,0},{4,7},{5,2},{6,9},{7,4},{8,11},{9,6},{10,... | collective-permute-start | bytes 110600 | tf_op jit(solution)/shard_map/ppermute | solution.py:718
  51.9 4.4 %collective-permute-start.6 = (f32[72,128]{1,0:T(8,128)S(1)}, f32[72,128]{1,0:T(8,128)S(1)}, u32[]{:S(2)}, u32[]{:S(2)}) collective-permute-start(f32[72,128]{1,0:T(8,128)S(1)} %glue_z.1.pair_ref), channel_id=1, source_target_pairs={{0,15},{1,2},{2,1},{3,4},{4,3},{5,6},{6,5},{7,8},{8,7},{9,10},{10,... | collective-permute-start | bytes 110600 | tf_op jit(solution)/shard_map/ppermute | solution.py:718
  56.3 0.0 collective-permute-done.5.rb_ref
  56.3 0.0 copy-start.2
  56.4 8.6 %far.1 = (f32[8,32,128]{2,1,0:T(8,128)S(1)}, f32[32,128]{1,0:T(8,128)S(1)}) custom-call(f32[12,4,12,128]{3,2,1,0:T(8,128)S(1)} %get-tuple-element.28.leafxy_ref, f32[8,8,2,128]{3,2,1,0:T(2,128)S(1)} %get-tuple-element.29.midxy_ref, f32[456,128]{1,0:T(8,128)S(1)} %collective-permute-done.4.ra_ref, f32[416,128]{1,0:T(8,128)S(1)} %collective-permute-done.5.rb_ref, ...), custom_call_target="tpu_custom_call" | custom-call | flops 4294967296 | bytes 4194304 | tf_op jit(solution)/shard_map/far/pallas_call | solution.py:532
  64.9 0.0 collective-permute-done.7.next_ref
  64.9 0.0 collective-permute-done.6.near_ref
  65.0 3.2 %forces.1 = (f32[3,8,8,128]{3,2,1,0:T(8,128)}, f32[512,128]{1,0:T(8,128)S(1)}) custom-call(f32[8,32,128]{2,1,0:T(8,128)S(1)} %get-tuple-element.32.far0_ref, f32[32,128]{1,0:T(8,128)S(1)} %get-tuple-element.33.far1_ref, f32[72,128]{1,0:T(8,128)S(1)} %glue_z.1.pair_ref, f32[72,128]{1,0:T(8,128)S(1)} %collective-permute-done.6.near_ref, ...), custom_call_target="tpu_custom_call" | custom-call | tf_op jit(solution)/shard_map/forces/pallas_call | solution.py:674
  68.1 35.1 %all_to_all.11 = f32[512,1,128]{2,1,0:T(1,128)S(1)} all-to-all(f32[512,1,128]{2,1,0:T(1,128)S(1)} %bitcast.8), channel_id=1, replica_groups=mesh['gx'=4,'gy'=8,'gz'=16] {'gx','gy','gz'}, dimensions={0} | all-to-all | bytes 524288 | tf_op jit(solution)/shard_map/all_to_all | solution.py:744
  103.3 0.7 virial.1
  (12 shorter events, 0.0 us)
Async XLA Ops:
  0.6 25.0 %copy-start.7 = (f32[3,128]{1,0:T(4,128)S(1)}, f32[3,128]{1,0:T(4,128)}, u32[]{:S(2)}) copy-start(f32[3,128]{1,0:T(4,128)} %wave_ref.7) | copy-start | bytes 4612
  0.6 25.0 %copy-start.3 = (f32[3,8,8,128]{3,2,1,0:T(8,128)S(1)}, f32[3,8,8,128]{3,2,1,0:T(8,128)}, u32[]{:S(2)}) copy-start(f32[3,8,8,128]{3,2,1,0:T(8,128)} %pos_ref.5) | copy-start | bytes 294916
  0.7 25.0 %copy-start.8 = (f32[128]{0:T(128)S(1)}, f32[128]{0:T(128)}, u32[]{:S(2)}) copy-start(f32[128]{0:T(128)} %param.18) | copy-start | bytes 1540
  11.7 17.0 %collective-permute-start = (f32[88,128]{1,0:T(8,128)}, f32[88,128]{1,0:T(8,128)S(1)}, u32[]{:S(2)}, u32[]{:S(2)}) collective-permute-start(f32[88,128]{1,0:T(8,128)} %get-tuple-element.20), channel_id=1, source_target_pairs={{0,128},{128,0},{256,384},{384,256},{1,129},{129,1},{257,385},{385... | collective-permute-start | bytes 135176 | tf_op jit(solution)/shard_map/ppermute | solution.py:718
  20.5 9.5 %collective-permute-start.1 = (f32[88,128]{1,0:T(8,128)}, f32[88,128]{1,0:T(8,128)S(1)}, u32[]{:S(2)}, u32[]{:S(2)}) collective-permute-start(f32[88,128]{1,0:T(8,128)} %get-tuple-element.21), channel_id=1, source_target_pairs={{0,384},{128,256},{256,128},{384,0},{1,385},{129,257},{257,129},{3... | collective-permute-start | bytes 135176 | tf_op jit(solution)/shard_map/ppermute | solution.py:718
  25.6 0.9 copy-start.4
  30.0 9.0 %collective-permute-start.2 = (f32[144,128]{1,0:T(8,128)S(1)}, f32[144,128]{1,0:T(8,128)S(1)}, u32[]{:S(2)}, u32[]{:S(2)}) collective-permute-start(f32[144,128]{1,0:T(8,128)S(1)} %get-tuple-element.23), channel_id=1, source_target_pairs={{0,16},{16,0},{32,48},{48,32},{64,80},{80,64},{96,112},{112,96},{1... | collective-permute-start | bytes 221192 | tf_op jit(solution)/shard_map/ppermute | solution.py:718
  32.0 7.0 %collective-permute-start.3 = (f32[144,128]{1,0:T(8,128)S(1)}, f32[144,128]{1,0:T(8,128)S(1)}, u32[]{:S(2)}, u32[]{:S(2)}) collective-permute-start(f32[144,128]{1,0:T(8,128)S(1)} %get-tuple-element.24), channel_id=1, source_target_pairs={{0,112},{16,32},{32,16},{48,64},{64,48},{80,96},{96,80},{112,0},{1... | collective-permute-start | bytes 221192 | tf_op jit(solution)/shard_map/ppermute | solution.py:718
  36.8 19.5 %copy-start = (f32[3,343,128]{2,1,0:T(8,128)S(1)}, f32[3,343,128]{2,1,0:T(8,128)}, u32[]{:S(2)}) copy-start(f32[3,343,128]{2,1,0:T(8,128)} %in_ref.3) | copy-start | bytes 1580548
  36.8 19.5 %copy-start.1 = (f32[3,343,128]{2,1,0:T(8,128)S(1)}, f32[3,343,128]{2,1,0:T(8,128)}, u32[]{:S(2)}) copy-start(f32[3,343,128]{2,1,0:T(8,128)} %out_ref.3) | copy-start | bytes 1580548
  36.9 19.5 %copy-start.5 = (bf16[3,128,128]{2,1,0:T(8,128)(2,1)S(1)}, bf16[3,128,128]{2,1,0:T(8,128)(2,1)}, u32[]{:S(2)}) copy-start(bf16[3,128,128]{2,1,0:T(8,128)(2,1)} %core_ref.3) | copy-start | bytes 294916
  39.1 9.7 %collective-permute-start.4 = (f32[456,128]{1,0:T(8,128)S(1)}, f32[456,128]{1,0:T(8,128)S(1)}, u32[]{:S(2)}, u32[]{:S(2)}) collective-permute-start(f32[456,128]{1,0:T(8,128)S(1)} %get-tuple-element.30), channel_id=1, source_target_pairs={{0,1},{1,0},{2,3},{3,2},{4,5},{5,4},{6,7},{7,6},{8,9},{9,8},{10,11... | collective-permute-start | bytes 700424 | tf_op jit(solution)/shard_map/ppermute | solution.py:718
  42.2 14.1 %collective-permute-start.5 = (f32[416,128]{1,0:T(8,128)S(1)}, f32[416,128]{1,0:T(8,128)S(1)}, u32[]{:S(2)}, u32[]{:S(2)}) collective-permute-start(f32[416,128]{1,0:T(8,128)S(1)} %get-tuple-element.31), channel_id=1, source_target_pairs={{0,15},{1,2},{2,1},{3,4},{4,3},{5,6},{6,5},{7,8},{8,7},{9,10},{10,... | collective-permute-start | bytes 638984 | tf_op jit(solution)/shard_map/ppermute | solution.py:718
  48.8 16.1 %collective-permute-start.7 = (f32[72,128]{1,0:T(8,128)S(1)}, f32[72,128]{1,0:T(8,128)S(1)}, u32[]{:S(2)}, u32[]{:S(2)}) collective-permute-start(f32[72,128]{1,0:T(8,128)S(1)} %glue_z.1.pair_ref), channel_id=1, source_target_pairs={{0,3},{1,14},{2,5},{3,0},{4,7},{5,2},{6,9},{7,4},{8,11},{9,6},{10,... | collective-permute-start | bytes 110600 | tf_op jit(solution)/shard_map/ppermute | solution.py:718
  51.9 13.0 %collective-permute-start.6 = (f32[72,128]{1,0:T(8,128)S(1)}, f32[72,128]{1,0:T(8,128)S(1)}, u32[]{:S(2)}, u32[]{:S(2)}) collective-permute-start(f32[72,128]{1,0:T(8,128)S(1)} %glue_z.1.pair_ref), channel_id=1, source_target_pairs={{0,15},{1,2},{2,1},{3,4},{4,3},{5,6},{6,5},{7,8},{8,7},{9,10},{10,... | collective-permute-start | bytes 110600 | tf_op jit(solution)/shard_map/ppermute | solution.py:718
  56.3 8.6 %copy-start.2 = (bf16[2,8,128,128]{3,2,1,0:T(8,128)(2,1)S(1)}, bf16[2,8,128,128]{3,2,1,0:T(8,128)(2,1)}, u32[]{:S(2)}) copy-start(bf16[2,8,128,128]{3,2,1,0:T(8,128)(2,1)} %down_ref.1) | copy-start | bytes 1572868
  56.3 8.6 %copy-start.6 = (f32[8,8,128]{2,1,0:T(8,128)S(1)}, f32[8,8,128]{2,1,0:T(8,128)}, u32[]{:S(2)}) copy-start(f32[8,8,128]{2,1,0:T(8,128)} %get-tuple-element.35.charge_ref) | copy-start | bytes 98308

commit v4 on v3

--- a/solution.py
+++ b/solution.py
@@ -89,99 +89,98 @@
 
 
 def atoms_kernel(
-    feat_hbm, pos_hbm, cnt_ref, wh_hbm, wc_ref, wave_ref, ph_ref, up_hbm,
+    feat_hbm, pos_hbm, cnt_hbm, wh_hbm, wc_hbm, wave_hbm, ph_hbm, up_hbm,
     charge_ref, own_ref, sa_ref, sb_ref,
-    feat_ref, pos_ref, wh_ref, up_ref, table_ref, cos_ref, low_ref, leaf_ref, mid_ref,
+    feat_ref, pos_ref, cnt_ref, wh_ref, wc_ref, wave_ref, ph_ref, up_ref, parts_ref, leaf_ref, mid_ref,
     plane_sems, sems,
 ):
     def plane(x):
         return pltpu.make_async_copy(feat_hbm.at[x], feat_ref.at[x], plane_sems.at[x])
 
     others = [
-        pltpu.make_async_copy(wh_hbm, wh_ref, sems.at[0]),
-        pltpu.make_async_copy(pos_hbm, pos_ref, sems.at[1]),
-        pltpu.make_async_copy(up_hbm, up_ref, sems.at[2]),
+        pltpu.make_async_copy(source, target, sems.at[i])
+        for i, (source, target) in enumerate(
+            (
+                (wave_hbm, wave_ref),
+                (ph_hbm, ph_ref),
+                (wc_hbm, wc_ref),
+                (pos_hbm, pos_ref),
+                (wh_hbm, wh_ref),
+                (cnt_hbm, cnt_ref),
+                (up_hbm, up_ref),
+            )
+        )
     ]
+    for copy in others[:3]:
+        copy.start()
     plane(0).start()
-    others[0].start()
-    others[1].start()
+    for copy in others[3:6]:
+        copy.start()
     for x in range(1, 8):
         plane(x).start()
-    others[2].start()
-    wave_table(wave_ref, ph_ref, table_ref)
-    others[0].wait()
-    others[1].wait()
+    others[6].start()
+    for copy in others[:3]:
+        copy.wait()
+    rows = []
+    for d in range(3):
+        high, middle, low = split(wave_ref[d : d + 1, :] * TURN)
+        rows += [high, middle, low, high, middle, high]
+    rows += list(split(ph_ref[...] * TURN)) + [jnp.zeros((11, 128), F32)]
+    table = jnp.concatenate(rows, axis=0).astype(BF16)
+    for row in range(18, 32):
+        parts_ref[row * 8 : row * 8 + 8, :] = jnp.full((8, 128), 1.0 if row < 21 else 0.0, F32)
+    column = jnp.broadcast_to(wc_ref[...].astype(F32), (128, 128)).T.astype(BF16)
+    for copy in others[3:6]:
+        copy.wait()
 
     @pl.loop(0, 8)
     def _(x):
         plane(x).wait()
         atoms_plane(
-            x, feat_ref, pos_ref, cnt_ref, wh_ref, wc_ref, charge_ref, leaf_ref, table_ref,
-            cos_ref, low_ref,
+            x, feat_ref, pos_ref, cnt_ref, wh_ref, wc_ref, charge_ref, leaf_ref, table, column,
+            parts_ref,
         )
 
-    others[2].wait()
+    others[6].wait()
     atoms_lift(leaf_ref, up_ref, mid_ref, own_ref, sa_ref, sb_ref)
 
 
 def atoms_plane(
-    step, feat_ref, pos_ref, cnt_ref, wh_ref, wc_ref, charge_ref, leaf_ref, table_ref,
-    cos_ref, low_ref,
+    step, feat_ref, pos_ref, cnt_ref, wh_ref, wc_ref, charge_ref, leaf_ref, table, column,
+    parts_ref,
 ):
     lane_box = lax.broadcasted_iota(jnp.int32, (8, 128), 1) // 32
     lane_slot = lax.broadcasted_iota(jnp.int32, (8, 128), 1) % 32
     row_y = lax.broadcasted_iota(jnp.int32, (8, 128), 0)
-    counts = jnp.zeros((8, 128), jnp.int32)
-    columns = cnt_ref[step].T
-    for z in range(4):
-        counts = jnp.where(
-            lane_box == z, jnp.broadcast_to(columns[:, z : z + 1], (8, 128)), counts
-        )
-    live = jnp.where(lane_slot < counts, 1.0, 0.0).astype(F32)
+    slot = lax.broadcasted_iota(jnp.int32, (32, 128), 0)
+    for d in range(3):
+        high, middle, low = split(pos_ref[d, step] - 0.5)
+        for i, part in enumerate((high, high, high, middle, middle, low)):
+            row = (d * 6 + i) * 8
+            parts_ref[row : row + 8, :] = part
+    lines = [parts_ref[pl.ds(y, 32, stride=8), :].T.astype(BF16) for y in range(8)]
+    turns = dot(jnp.concatenate(lines, axis=0), table)
 
     hidden = dot(feat_ref[step].reshape(1024, 128), wh_ref[...])
     half = hidden * 0.5
     hidden = (half + half * jnp.tanh(half)).astype(BF16)
+    broad = dot(hidden, column)
     wc = jnp.broadcast_to(wc_ref[...], (8, 128))
     raw = lax.dot_general(wc, hidden, NT, preferred_element_type=F32)
+    counts = jnp.zeros((8, 128), jnp.int32)
     charge = jnp.zeros((8, 128), F32)
     for y in range(8):
         charge = jnp.where(row_y == y, raw[:, y * 128 : (y + 1) * 128], charge)
-    charge = charge * live
-    charge_ref[step] = charge
-
-    spread = []
-    for z in range(4):
-        spread.append(
-            jnp.concatenate(
-                [
-                    jnp.where((row_y == y) & (lane_box == z), charge, 0.0)
-                    for y in range(8)
-                ],
-                axis=1,
-            )
-        )
-    spread = jnp.concatenate(spread, axis=0)
-    spread_high = spread.astype(BF16)
-    spread_low = (spread - spread_high.astype(F32)).astype(BF16)
-
-    turns = turns_of(step, pos_ref, table_ref)
-    for y in range(8):
-        t = turns[:, y * 128 : (y + 1) * 128]
-        r = t - jnp.round(t)
-        s = poly(SIN_HALF, r * r) * r
-        cosine = 1.0 - s * s
-        cosine_high = cosine.astype(BF16)
-        cos_ref[:, y * 128 : (y + 1) * 128] = cosine_high
-        low_ref[:, y * 128 : (y + 1) * 128] = (cosine - cosine_high.astype(F32)).astype(BF16)
-    moments = lax.dot_general(
-        jnp.concatenate([spread_high, spread_low], axis=0), cos_ref[...], NT,
-        preferred_element_type=F32,
-    )
-    fine = lax.dot_general(spread_high, low_ref[...], NT, preferred_element_type=F32)
-    moments = moments[0:32] + (moments[32:64] + fine)
-    for z in range(4):
-        leaf_ref[step, z] = moments[z * 8 : (z + 1) * 8]
+        for z in range(4):
+            count = cnt_ref[step, z, y]
+            counts = jnp.where((row_y == y) & (lane_box == z), count, counts)
+            start = y * 128 + z * 32
+            t = turns[start : start + 32]
+            r = t - jnp.round(t)
+            s = poly(SIN_HALF, r * r) * r
+            terms = jnp.where(slot < count, broad[start : start + 32], 0.0) * (1.0 - s * s)
+            leaf_ref[step, z, y : y + 1, :] = jnp.sum(terms, axis=0, keepdims=True)
+    charge_ref[step] = jnp.where(lane_slot < counts, charge, 0.0)
 
 
 def atoms_lift(leaf_ref, up_ref, mid_ref, own_ref, sa_ref, sb_ref):
@@ -238,7 +237,7 @@
     hbm = pl.BlockSpec(memory_space=pltpu.HBM)
     return pl.pallas_call(
         atoms_kernel,
-        in_specs=[hbm, hbm, VMEM, hbm, VMEM, VMEM, VMEM, hbm],
+        in_specs=[hbm] * 8,
         out_specs=[VMEM] * 4,
         out_shape=[
             jax.ShapeDtypeStruct((8, 8, 128), F32),
@@ -249,22 +248,24 @@
         scratch_shapes=[
             pltpu.VMEM((8, 8, 128, 128), BF16),
             pltpu.VMEM((3, 8, 8, 128), F32),
+            pltpu.SMEM((8, 4, 8), jnp.int32),
             pltpu.VMEM((128, 128), BF16),
+            pltpu.VMEM((1, 128), BF16),
+            pltpu.VMEM((3, 128), F32),
+            pltpu.VMEM((1, 128), F32),
             pltpu.VMEM((2, 8, 128, 128), BF16),
-            pltpu.VMEM((128, 256), BF16),
-            pltpu.VMEM((128, 1024), BF16),
-            pltpu.VMEM((128, 1024), BF16),
+            pltpu.VMEM((256, 128), F32),
             pltpu.VMEM((8, 4, 8, 128), F32),
             pltpu.VMEM((4, 4, 2, 128), F32),
             pltpu.SemaphoreType.DMA((8,)),
-            pltpu.SemaphoreType.DMA((3,)),
+            pltpu.SemaphoreType.DMA((7,)),
         ],
         compiler_params=pltpu.CompilerParams(vmem_limit_bytes=58 << 20),
         name="atoms",
     )(features, positions, box_counts, w_hidden, w_charge, wave, phases, upward)
 
 
-def glue_x_kernel(ra_ref, rb_ref, own_ref, _, leafx_ref, midx_ref, topx_ref, ya_ref, yb_ref):
+def glue_x_kernel(ra_ref, rb_ref, own_ref, _, __, leafx_ref, midx_ref, topx_ref, ya_ref, yb_ref):
     odd = lax.axis_index("gx") % 2
     leafx_ref[2:10] = own_ref[0:256, :].reshape(8, 4, 8, 128)
     for x in range(4):
@@ -305,10 +306,10 @@
         ref[128:144, :] = topx_ref[...]
 
 
-def glue_x(ra, rb, own, front):
+def glue_x(ra, rb, own, front, scale):
     return pl.pallas_call(
         glue_x_kernel,
-        in_specs=[VMEM] * 3 + [pl.BlockSpec(memory_space=pl.ANY)],
+        in_specs=[VMEM] * 3 + [pl.BlockSpec(memory_space=pl.ANY)] * 2,
         out_specs=[VMEM] * 5,
         out_shape=[
             jax.ShapeDtypeStruct((12, 4, 8, 128), F32),
@@ -319,7 +320,7 @@
         ],
         compiler_params=pltpu.CompilerParams(vmem_limit_bytes=8 << 20),
         name="glue_x",
-    )(ra, rb, own, front)
+    )(ra, rb, own, front, scale)
 
 
 def glue_y_kernel(ra_ref, rb_ref, leafx_ref, midx_ref, topx_ref, _, leafxy_ref, midxy_ref, topxy_ref, za_ref, zb_ref):
@@ -405,10 +406,50 @@
         out_ref[xy] = tile
 
 
+def tables_kernel(in_ref, out_ref, _, scale_ref, tin_ref, tout_ref, top_in_ref, top_out_ref):
+    scale_ref[...] = in_ref[0]
+    for x in range(2, 5):
+        for y in range(2, 5):
+            row = x * 49 + y * 7 + 2
+            scale_ref[row : row + 3, :] = jnp.zeros((3, 128), F32)
+    for cz in range(2):
+        offset_tiles(tin_ref.at[cz], in_ref.at[1], cz, True)
+        offset_tiles(tout_ref.at[cz], out_ref.at[1], cz, False)
+    odd = lax.axis_index("gz") % 2
+    lanes = lax.broadcasted_iota(jnp.int32, (8, 128), 0)
+    near = (lanes >= 1 + odd) & (lanes <= 3 + odd)
+    for xy in range(49):
+        for ref, table, masked in ((top_in_ref, in_ref, True), (top_out_ref, out_ref, False)):
+            rows = table[2, xy * 7 : xy * 7 + 7, :]
+            tile = jnp.where(odd == 1, rows[0:6], rows[1:7])
+            tile = jnp.concatenate([tile, jnp.zeros((2, 128), F32)], axis=0)
+            if masked and 2 <= xy // 7 <= 4 and 2 <= xy % 7 <= 4:
+                tile = jnp.where(near, 0.0, tile)
+            ref[xy] = tile
+
+
+def run_tables(in_scale, out_scale, after):
+    return pl.pallas_call(
+        tables_kernel,
+        in_specs=[VMEM] * 2 + [pl.BlockSpec(memory_space=pl.ANY)],
+        out_specs=[VMEM] * 5,
+        out_shape=[
+            jax.ShapeDtypeStruct((343, 128), F32),
+            jax.ShapeDtypeStruct((2, 49, 8, 128), F32),
+            jax.ShapeDtypeStruct((2, 49, 8, 128), F32),
+            jax.ShapeDtypeStruct((49, 8, 128), F32),
+            jax.ShapeDtypeStruct((49, 8, 128), F32),
+        ],
+        cost_estimate=pl.CostEstimate(flops=1 << 28, bytes_accessed=3 << 20, transcendentals=0),
+        compiler_params=pltpu.CompilerParams(vmem_limit_bytes=8 << 20),
+        name="tables",
+    )(in_scale, out_scale, after)
+
+
 def far_kernel(
-    leafxy_ref, midxy_ref, ra_ref, rb_ref, in_ref, out_ref, core_ref,
+    leafxy_ref, midxy_ref, ra_ref, rb_ref, scale_ref, tin_ref, tout_ref, out_ref, core_ref,
     far0_ref, far1_ref,
-    leaf_ref, mid_ref, scale_ref, tin_ref, tout_ref, acc_ref, even_ref, odd_ref,
+    leaf_ref, mid_ref, acc_ref, even_ref, odd_ref,
 ):
     odd = lax.axis_index("gz") % 2
     leaf_ref[:, 2:6] = leafxy_ref[...]
@@ -430,15 +471,6 @@
                 ],
                 axis=0,
             )
-    scale_ref[...] = in_ref[0]
-    for x in range(2, 5):
-        for y in range(2, 5):
-            row = x * 49 + y * 7 + 2
-            scale_ref[row : row + 3, :] = jnp.zeros((3, 128), F32)
-    for cz in range(2):
-        offset_tiles(tin_ref.at[cz], in_ref.at[1], cz, True)
-        offset_tiles(tout_ref.at[cz], out_ref.at[1], cz, False)
-
     far0_ref[...] = jnp.zeros((8, 32, 128), F32)
     core0 = core_ref[0]
 
@@ -528,10 +560,10 @@
             )
 
 
-def run_far(leafxy, midxy, ra, rb, in_scale, out_scale, transfer):
+def run_far(leafxy, midxy, ra, rb, scale, tin, tout, out_scale, transfer):
     return pl.pallas_call(
         far_kernel,
-        in_specs=[VMEM] * 7,
+        in_specs=[VMEM] * 9,
         out_specs=[VMEM] * 2,
         out_shape=[
             jax.ShapeDtypeStruct((8, 32, 128), F32),
@@ -540,9 +572,6 @@
         scratch_shapes=[
             pltpu.VMEM((12, 8, 12, 128), F32),
             pltpu.VMEM((8, 8, 8, 128), F32),
-            pltpu.VMEM((343, 128), F32),
-            pltpu.VMEM((2, 49, 8, 128), F32),
-            pltpu.VMEM((2, 49, 8, 128), F32),
             pltpu.VMEM((8, 32, 128), F32),
             pltpu.VMEM((1536, 128), BF16),
             pltpu.VMEM((1536, 128), BF16),
@@ -550,14 +579,14 @@
         cost_estimate=pl.CostEstimate(flops=4 << 30, bytes_accessed=4 << 20, transcendentals=0),
         compiler_params=pltpu.CompilerParams(vmem_limit_bytes=24 << 20),
         name="far",
-    )(leafxy, midxy, ra, rb, in_scale, out_scale, transfer)
+    )(leafxy, midxy, ra, rb, scale, tin, tout, out_scale, transfer)
 
 
 def force_kernel(
-    far0_ref, far1_ref, pair_ref, near_ref, next_ref, in_ref, out_ref, core_ref, down_ref,
+    far0_ref, far1_ref, pair_ref, near_ref, next_ref, tin_ref, tout_ref, core_ref, down_ref,
     charge_ref, front_ref, back_ref, pos_ref, wave_ref,
     forces_ref, share_ref,
-    window_ref, tin_ref, tout_ref, operand_ref, mid_ref, local_ref,
+    window_ref, operand_ref, mid_ref, local_ref,
 ):
     odd = lax.axis_index("gz") % 2
     for xy in range(36):
@@ -573,16 +602,6 @@
             + [jnp.zeros((2, 128), F32)],
             axis=0,
         )
-    lanes = lax.broadcasted_iota(jnp.int32, (8, 128), 0)
-    near = (lanes >= 1 + odd) & (lanes <= 3 + odd)
-    for xy in range(49):
-        for ref, table, masked in ((tin_ref, in_ref, True), (tout_ref, out_ref, False)):
-            rows = table[2, xy * 7 : xy * 7 + 7, :]
-            tile = jnp.where(odd == 1, rows[0:6], rows[1:7])
-            tile = jnp.concatenate([tile, jnp.zeros((2, 128), F32)], axis=0)
-            if masked and 2 <= xy // 7 <= 4 and 2 <= xy % 7 <= 4:
-                tile = jnp.where(near, 0.0, tile)
-            ref[xy] = tile
     for qx in range(6):
         for qy in range(6):
             source = window_ref[qx * 6 + qy]
@@ -670,7 +689,7 @@
     share_ref[...] = jnp.broadcast_to(row[0:1], (512, 128))
 
 
-def run_forces(far0, far1, pair, near, following, in_scale, out_scale, transfer, downward, charge, front, back, positions, wave):
+def run_forces(far0, far1, pair, near, following, top_in, top_out, transfer, downward, charge, front, back, positions, wave):
     return pl.pallas_call(
         force_kernel,
         in_specs=[VMEM] * 14,
@@ -681,15 +700,13 @@
         ],
         scratch_shapes=[
             pltpu.VMEM((36, 8, 128), F32),
-            pltpu.VMEM((49, 8, 128), F32),
-            pltpu.VMEM((49, 8, 128), F32),
             pltpu.VMEM((1152, 128), BF16),
             pltpu.VMEM((32, 128), F32),
             pltpu.VMEM((8, 4, 8, 128), F32),
         ],
         compiler_params=pltpu.CompilerParams(vmem_limit_bytes=24 << 20),
         name="forces",
-    )(far0, far1, pair, near, following, in_scale, out_scale, transfer, downward, charge, front, back, positions, wave)
+    )(far0, far1, pair, near, following, top_in, top_out, transfer, downward, charge, front, back, positions, wave)
 
 
 def virial_kernel(scale, rows_ref, virial_ref):
@@ -728,17 +745,18 @@
         wave_numbers, phases, upward,
     )
     front = run_sines(positions, wave_numbers, phases, own, 0, 4)
+    scale, tin, tout, top_in, top_out = run_tables(in_scale, out_scale, own)
     ra, rb = swapped(xa, "gx", 0), swapped(xb, "gx", 1)
-    leaf, mid, top, ya, yb = glue_x(ra, rb, own, front)
+    leaf, mid, top, ya, yb = glue_x(ra, rb, own, front, scale)
     back = run_sines(positions, wave_numbers, phases, top, 4, 4)
     ra, rb = swapped(ya, "gy", 0), swapped(yb, "gy", 1)
     leaf, mid, top, za, zb = glue_y(ra, rb, leaf, mid, top, back)
     ra, rb = swapped(za, "gz", 0), swapped(zb, "gz", 1)
     pair = glue_z(ra, top)
     near, following = swapped(pair, "gz", 1), swapped(pair, "gz", 2)
-    far0, far1 = run_far(leaf, mid, ra, rb, in_scale, out_scale, transfer)
+    far0, far1 = run_far(leaf, mid, ra, rb, scale, tin, tout, out_scale, transfer)
     forces, share = run_forces(
-        far0, far1, pair, near, following, in_scale, out_scale, transfer, downward, charge, front, back,
+        far0, far1, pair, near, following, top_in, top_out, transfer, downward, charge, front, back,
         positions, wave_numbers,
     )
     rows = lax.all_to_all(share, ("gx", "gy", "gz"), 0, 0, tiled=True)

time: 104 us -> 101 us (0.971)
  Pallas kernels: 27.8 us -> 24.4 us
    pallas_call x2 -> x3, Pallas kernels: 19.5 us -> 16.1 us  [the longest x1 8.54 us: run_far(): pl.pallas_call(far_kernel, in_specs=[VMEM] * 9, out_specs=[VMEM] * 2, out...]
  transfers between devices with their start and end apart: 8 -> 8, of which waited for: 1 -> 1; matrix products, arithmetic and copies ran while one was open for 0% -> 0% of each run, Pallas kernels for 12% -> 13%
where the time goes in v4:
time: 101 us; the launch traced here: 100 us
  starting transfers between devices  38 us (38%)
  blocking collectives  35 us (35%)
  Pallas kernels  24.4 us (24%)
  waiting for transfers between devices  1.11 us (1%)
    ppermute x8, starting transfers between devices, swapped(): return lax.ppermute(value, axis, pairs)  38 us
    all_to_all x1, blocking collectives, shards(): rows = lax.all_to_all(share, ('gx', 'gy', 'gz'), 0, 0, tiled=True)  35 us
    pallas_call x1, Pallas kernels, run_far(): pl.pallas_call(far_kernel, in_specs=[VMEM] * 9, out_specs=[VMEM] * 2, out...  8.54 us
    pallas_call x1, Pallas kernels, run_atoms(): pl.pallas_call(atoms_kernel, in_specs=[hbm] * 8, out_specs=[VMEM] * 4, ou...  7.44 us
    pallas_call x2, Pallas kernels, run_sines(): pl.pallas_call(functools.partial(sines_kernel, start), in_specs=[VMEM] *...  4.18 us
    pallas_call x1, Pallas kernels, run_forces(): pl.pallas_call(force_kernel, in_specs=[VMEM] * 14, out_specs=[VMEM] * 2,...  3.18 us
  transfers between devices with their start and end apart: 8, of which 1 were waited for; matrix products, arithmetic and copies ran while one was open for 0% of the time, Pallas kernels for 13%

profile of v4, /device:TPU:1, one launch (start us, length us, event | category | flops | bytes accessed | tf_op | source)
XLA Modules:
  0.0 100.4 jit_solution(11114800008268778470)
XLA Ops:
  0.6 0.0 copy-start.7
  0.6 0.0 copy-start.4
  0.7 7.4 %atoms.1 = (f32[8,8,128]{2,1,0:T(8,128)}, f32[296,128]{1,0:T(8,128)}, f32[88,128]{1,0:T(8,128)}, f32[88,128]{1,0:T(8,128)}) custom-call(bf16[8,8,128,128]{3,2,1,0:T(8,128)(2,1)} %feat_hbm.1, f32[3,8,8,128]{3,2,1,0:T(8,128)} %pos_ref.5, s32[8,4,8]{2,1,0:T(4,128)} %bitcast.12, bf16[128,128]{1,0:T(8,128)(2,1)} %wh_hbm.1, bf16[1,128]{1,0:T(2,128)(2,1)} %bitcast.13, ...), custom_call_target="tpu_custom_call" | custom-call | tf_op jit(solution)/shard_map/atoms/pallas_call | solution.py:238
  8.1 8.8 %collective-permute-start = (f32[88,128]{1,0:T(8,128)}, f32[88,128]{1,0:T(8,128)S(1)}, u32[]{:S(2)}, u32[]{:S(2)}) collective-permute-start(f32[88,128]{1,0:T(8,128)} %get-tuple-element.25), channel_id=1, source_target_pairs={{0,128},{128,0},{256,384},{384,256},{1,129},{129,1},{257,385},{385... | collective-permute-start | bytes 135176 | tf_op jit(solution)/shard_map/ppermute | solution.py:735
  16.9 5.2 %collective-permute-start.1 = (f32[88,128]{1,0:T(8,128)}, f32[88,128]{1,0:T(8,128)S(1)}, u32[]{:S(2)}, u32[]{:S(2)}) collective-permute-start(f32[88,128]{1,0:T(8,128)} %get-tuple-element.26), channel_id=1, source_target_pairs={{0,384},{128,256},{256,128},{384,0},{1,385},{129,257},{257,129},{3... | collective-permute-start | bytes 135176 | tf_op jit(solution)/shard_map/ppermute | solution.py:735
  22.1 0.9 copy-done
  23.0 2.1 %sines.2._.front_ref = bf16[4,128,1024]{2,1,0:T(8,128)(2,1)S(1)} custom-call(f32[3,8,8,128]{3,2,1,0:T(8,128)S(1)} %copy-done.4, f32[3,128]{1,0:T(4,128)S(1)} %copy-done.7, f32[1,128]{1,0:T(1,128)S(1)} %bitcast.10, f32[296,128]{1,0:T(8,128)S(1)} %copy-done), custom_call_target="tpu_custom_call" | custom-call | flops 1073741824 | bytes 6291456 | tf_op jit(solution)/shard_map/sines/pallas_call | solution.py:79
  25.2 0.1 tables.1
  25.3 0.0 collective-permute-done.ra_ref
  25.3 1.1 %collective-permute-done.1.rb_ref = f32[88,128]{1,0:T(8,128)S(1)} collective-permute-done((f32[88,128]{1,0:T(8,128)}, f32[88,128]{1,0:T(8,128)S(1)}, u32[]{:S(2)}, u32[]{:S(2)}) %collective-permute-start.1) | collective-permute-done | bytes 45088 | tf_op jit(solution)/shard_map/ppermute | solution.py:735
  26.4 0.1 glue_x.1
  26.5 2.1 %collective-permute-start.2 = (f32[144,128]{1,0:T(8,128)S(1)}, f32[144,128]{1,0:T(8,128)S(1)}, u32[]{:S(2)}, u32[]{:S(2)}) collective-permute-start(f32[144,128]{1,0:T(8,128)S(1)} %get-tuple-element.29), channel_id=1, source_target_pairs={{0,16},{16,0},{32,48},{48,32},{64,80},{80,64},{96,112},{112,96},{1... | collective-permute-start | bytes 221192 | tf_op jit(solution)/shard_map/ppermute | solution.py:735
  28.6 4.9 %collective-permute-start.3 = (f32[144,128]{1,0:T(8,128)S(1)}, f32[144,128]{1,0:T(8,128)S(1)}, u32[]{:S(2)}, u32[]{:S(2)}) collective-permute-start(f32[144,128]{1,0:T(8,128)S(1)} %get-tuple-element.30), channel_id=1, source_target_pairs={{0,112},{16,32},{32,16},{48,64},{64,48},{80,96},{96,80},{112,0},{1... | collective-permute-start | bytes 221192 | tf_op jit(solution)/shard_map/ppermute | solution.py:735
  33.5 0.0 copy-start.5
  33.5 2.1 %sines.3._.back_ref = bf16[4,128,1024]{2,1,0:T(8,128)(2,1)S(1)} custom-call(f32[3,8,8,128]{3,2,1,0:T(8,128)S(1)} %copy-done.4, f32[3,128]{1,0:T(4,128)S(1)} %copy-done.7, f32[1,128]{1,0:T(1,128)S(1)} %bitcast.11, f32[16,128]{1,0:T(8,128)S(1)} %get-tuple-element.33._.topx_ref), custom_call_target="tpu_custom_call" | custom-call | flops 1073741824 | bytes 6291456 | tf_op jit(solution)/shard_map/sines/pallas_call | solution.py:79
  35.6 0.0 collective-permute-done.2.ra_ref
  35.6 0.0 collective-permute-done.3.rb_ref
  35.6 0.1 glue_y.1
  35.8 3.1 %collective-permute-start.4 = (f32[456,128]{1,0:T(8,128)S(1)}, f32[456,128]{1,0:T(8,128)S(1)}, u32[]{:S(2)}, u32[]{:S(2)}) collective-permute-start(f32[456,128]{1,0:T(8,128)S(1)} %get-tuple-element.36), channel_id=1, source_target_pairs={{0,1},{1,0},{2,3},{3,2},{4,5},{5,4},{6,7},{7,6},{8,9},{9,8},{10,11... | collective-permute-start | bytes 700424 | tf_op jit(solution)/shard_map/ppermute | solution.py:735
  38.9 6.4 %collective-permute-start.5 = (f32[416,128]{1,0:T(8,128)S(1)}, f32[416,128]{1,0:T(8,128)S(1)}, u32[]{:S(2)}, u32[]{:S(2)}) collective-permute-start(f32[416,128]{1,0:T(8,128)S(1)} %get-tuple-element.37), channel_id=1, source_target_pairs={{0,15},{1,2},{2,1},{3,4},{4,3},{5,6},{6,5},{7,8},{8,7},{9,10},{10,... | collective-permute-start | bytes 638984 | tf_op jit(solution)/shard_map/ppermute | solution.py:735
  45.3 0.0 collective-permute-done.4.ra_ref
  45.3 3.2 %collective-permute-start.7 = (f32[72,128]{1,0:T(8,128)S(1)}, f32[72,128]{1,0:T(8,128)S(1)}, u32[]{:S(2)}, u32[]{:S(2)}) collective-permute-start(f32[72,128]{1,0:T(8,128)S(1)} %glue_z.1.pair_ref), channel_id=1, source_target_pairs={{0,3},{1,14},{2,5},{3,0},{4,7},{5,2},{6,9},{7,4},{8,11},{9,6},{10,... | collective-permute-start | bytes 110600 | tf_op jit(solution)/shard_map/ppermute | solution.py:735
  48.5 4.4 %collective-permute-start.6 = (f32[72,128]{1,0:T(8,128)S(1)}, f32[72,128]{1,0:T(8,128)S(1)}, u32[]{:S(2)}, u32[]{:S(2)}) collective-permute-start(f32[72,128]{1,0:T(8,128)S(1)} %glue_z.1.pair_ref), channel_id=1, source_target_pairs={{0,15},{1,2},{2,1},{3,4},{4,3},{5,6},{6,5},{7,8},{8,7},{9,10},{10,... | collective-permute-start | bytes 110600 | tf_op jit(solution)/shard_map/ppermute | solution.py:735
  52.9 0.0 collective-permute-done.5.rb_ref
  52.9 0.0 copy-start.3
  52.9 0.0 copy-start.6
  52.9 8.5 %far.1 = (f32[8,32,128]{2,1,0:T(8,128)S(1)}, f32[32,128]{1,0:T(8,128)S(1)}) custom-call(f32[12,4,12,128]{3,2,1,0:T(8,128)S(1)} %get-tuple-element.34.leafxy_ref, f32[8,8,2,128]{3,2,1,0:T(2,128)S(1)} %get-tuple-element.35.midxy_ref, f32[456,128]{1,0:T(8,128)S(1)} %collective-permute-done.4.ra_ref, f32[416,128]{1,0:T(8,128)S(1)} %collective-permute-done.5.rb_ref, ...), custom_call_target="tpu_custom_call" | custom-call | flops 4294967296 | bytes 4194304 | tf_op jit(solution)/shard_map/far/pallas_call | solution.py:564
  61.5 0.0 collective-permute-done.7.next_ref
  61.5 0.0 collective-permute-done.6.near_ref
  61.5 3.2 %forces.1 = (f32[3,8,8,128]{3,2,1,0:T(8,128)}, f32[512,128]{1,0:T(8,128)S(1)}) custom-call(f32[8,32,128]{2,1,0:T(8,128)S(1)} %get-tuple-element.40.far0_ref, f32[32,128]{1,0:T(8,128)S(1)} %get-tuple-element.41.far1_ref, f32[72,128]{1,0:T(8,128)S(1)} %glue_z.1.pair_ref, f32[72,128]{1,0:T(8,128)S(1)} %collective-permute-done.6.near_ref, ...), custom_call_target="tpu_custom_call" | custom-call | tf_op jit(solution)/shard_map/forces/pallas_call | solution.py:693
  64.7 35.0 %all_to_all.11 = f32[512,1,128]{2,1,0:T(1,128)S(1)} all-to-all(f32[512,1,128]{2,1,0:T(1,128)S(1)} %bitcast.8), channel_id=1, replica_groups=mesh['gx'=4,'gy'=8,'gz'=16] {'gx','gy','gz'}, dimensions={0} | all-to-all | bytes 524288 | tf_op jit(solution)/shard_map/all_to_all | solution.py:762
  99.7 0.7 virial.1
  (13 shorter events, 0.0 us)
Async XLA Ops:
  0.6 21.5 %copy-start.7 = (f32[3,128]{1,0:T(4,128)S(1)}, f32[3,128]{1,0:T(4,128)}, u32[]{:S(2)}) copy-start(f32[3,128]{1,0:T(4,128)} %wave_ref.5) | copy-start | bytes 4612
  0.6 21.5 %copy-start.4 = (f32[3,8,8,128]{3,2,1,0:T(8,128)S(1)}, f32[3,8,8,128]{3,2,1,0:T(8,128)}, u32[]{:S(2)}) copy-start(f32[3,8,8,128]{3,2,1,0:T(8,128)} %pos_ref.5) | copy-start | bytes 294916
  0.7 21.5 %copy-start.8 = (f32[128]{0:T(128)S(1)}, f32[128]{0:T(128)}, u32[]{:S(2)}) copy-start(f32[128]{0:T(128)} %param.18) | copy-start | bytes 1540
  0.7 24.5 %copy-start.1 = (f32[3,343,128]{2,1,0:T(8,128)S(1)}, f32[3,343,128]{2,1,0:T(8,128)}, u32[]{:S(2)}) copy-start(f32[3,343,128]{2,1,0:T(8,128)} %in_ref.1) | copy-start | bytes 1580548
  0.7 24.5 %copy-start.2 = (f32[3,343,128]{2,1,0:T(8,128)S(1)}, f32[3,343,128]{2,1,0:T(8,128)}, u32[]{:S(2)}) copy-start(f32[3,343,128]{2,1,0:T(8,128)} %out_ref.3) | copy-start | bytes 1580548
  8.1 17.2 %collective-permute-start = (f32[88,128]{1,0:T(8,128)}, f32[88,128]{1,0:T(8,128)S(1)}, u32[]{:S(2)}, u32[]{:S(2)}) collective-permute-start(f32[88,128]{1,0:T(8,128)} %get-tuple-element.25), channel_id=1, source_target_pairs={{0,128},{128,0},{256,384},{384,256},{1,129},{129,1},{257,385},{385... | collective-permute-start | bytes 135176 | tf_op jit(solution)/shard_map/ppermute | solution.py:735
  16.9 9.5 %collective-permute-start.1 = (f32[88,128]{1,0:T(8,128)}, f32[88,128]{1,0:T(8,128)S(1)}, u32[]{:S(2)}, u32[]{:S(2)}) collective-permute-start(f32[88,128]{1,0:T(8,128)} %get-tuple-element.26), channel_id=1, source_target_pairs={{0,384},{128,256},{256,128},{384,0},{1,385},{129,257},{257,129},{3... | collective-permute-start | bytes 135176 | tf_op jit(solution)/shard_map/ppermute | solution.py:735
  22.1 0.9 copy-start
  26.5 9.1 %collective-permute-start.2 = (f32[144,128]{1,0:T(8,128)S(1)}, f32[144,128]{1,0:T(8,128)S(1)}, u32[]{:S(2)}, u32[]{:S(2)}) collective-permute-start(f32[144,128]{1,0:T(8,128)S(1)} %get-tuple-element.29), channel_id=1, source_target_pairs={{0,16},{16,0},{32,48},{48,32},{64,80},{80,64},{96,112},{112,96},{1... | collective-permute-start | bytes 221192 | tf_op jit(solution)/shard_map/ppermute | solution.py:735
  28.6 7.0 %collective-permute-start.3 = (f32[144,128]{1,0:T(8,128)S(1)}, f32[144,128]{1,0:T(8,128)S(1)}, u32[]{:S(2)}, u32[]{:S(2)}) collective-permute-start(f32[144,128]{1,0:T(8,128)S(1)} %get-tuple-element.30), channel_id=1, source_target_pairs={{0,112},{16,32},{32,16},{48,64},{64,48},{80,96},{96,80},{112,0},{1... | collective-permute-start | bytes 221192 | tf_op jit(solution)/shard_map/ppermute | solution.py:735
  33.5 19.4 %copy-start.5 = (bf16[3,128,128]{2,1,0:T(8,128)(2,1)S(1)}, bf16[3,128,128]{2,1,0:T(8,128)(2,1)}, u32[]{:S(2)}) copy-start(bf16[3,128,128]{2,1,0:T(8,128)(2,1)} %core_ref.3) | copy-start | bytes 294916
  35.8 9.5 %collective-permute-start.4 = (f32[456,128]{1,0:T(8,128)S(1)}, f32[456,128]{1,0:T(8,128)S(1)}, u32[]{:S(2)}, u32[]{:S(2)}) collective-permute-start(f32[456,128]{1,0:T(8,128)S(1)} %get-tuple-element.36), channel_id=1, source_target_pairs={{0,1},{1,0},{2,3},{3,2},{4,5},{5,4},{6,7},{7,6},{8,9},{9,8},{10,11... | collective-permute-start | bytes 700424 | tf_op jit(solution)/shard_map/ppermute | solution.py:735
  38.9 14.0 %collective-permute-start.5 = (f32[416,128]{1,0:T(8,128)S(1)}, f32[416,128]{1,0:T(8,128)S(1)}, u32[]{:S(2)}, u32[]{:S(2)}) collective-permute-start(f32[416,128]{1,0:T(8,128)S(1)} %get-tuple-element.37), channel_id=1, source_target_pairs={{0,15},{1,2},{2,1},{3,4},{4,3},{5,6},{6,5},{7,8},{8,7},{9,10},{10,... | collective-permute-start | bytes 638984 | tf_op jit(solution)/shard_map/ppermute | solution.py:735
  45.3 16.2 %collective-permute-start.7 = (f32[72,128]{1,0:T(8,128)S(1)}, f32[72,128]{1,0:T(8,128)S(1)}, u32[]{:S(2)}, u32[]{:S(2)}) collective-permute-start(f32[72,128]{1,0:T(8,128)S(1)} %glue_z.1.pair_ref), channel_id=1, source_target_pairs={{0,3},{1,14},{2,5},{3,0},{4,7},{5,2},{6,9},{7,4},{8,11},{9,6},{10,... | collective-permute-start | bytes 110600 | tf_op jit(solution)/shard_map/ppermute | solution.py:735
  48.5 13.0 %collective-permute-start.6 = (f32[72,128]{1,0:T(8,128)S(1)}, f32[72,128]{1,0:T(8,128)S(1)}, u32[]{:S(2)}, u32[]{:S(2)}) collective-permute-start(f32[72,128]{1,0:T(8,128)S(1)} %glue_z.1.pair_ref), channel_id=1, source_target_pairs={{0,15},{1,2},{2,1},{3,4},{4,3},{5,6},{6,5},{7,8},{8,7},{9,10},{10,... | collective-permute-start | bytes 110600 | tf_op jit(solution)/shard_map/ppermute | solution.py:735
  52.9 8.6 %copy-start.3 = (bf16[2,8,128,128]{3,2,1,0:T(8,128)(2,1)S(1)}, bf16[2,8,128,128]{3,2,1,0:T(8,128)(2,1)}, u32[]{:S(2)}) copy-start(bf16[2,8,128,128]{3,2,1,0:T(8,128)(2,1)} %down_ref.1) | copy-start | bytes 1572868
  52.9 8.6 %copy-start.6 = (f32[8,8,128]{2,1,0:T(8,128)S(1)}, f32[8,8,128]{2,1,0:T(8,128)}, u32[]{:S(2)}) copy-start(f32[8,8,128]{2,1,0:T(8,128)} %get-tuple-element.45.charge_ref) | copy-start | bytes 98308

commit v5 on v4

--- a/solution.py
+++ b/solution.py
@@ -75,6 +75,30 @@
             ).astype(BF16)
 
 
+def front_kernel(pos_ref, wave_ref, ph_ref, own_ref, sin_ref, send_ref, table_ref):
+    side = 1 - lax.axis_index("gx") % 2
+    send_ref[0:64, :] = own_ref[pl.ds(pl.multiple_of(side * 192, 8), 64), :]
+    send_ref[64:80, :] = own_ref[pl.ds(pl.multiple_of(256 + side * 16, 8), 16), :]
+    send_ref[80:88, :] = own_ref[288:296, :]
+    sines_kernel(0, pos_ref, wave_ref, ph_ref, None, sin_ref, table_ref)
+
+
+def run_front(positions, wave, phases, own, planes):
+    return pl.pallas_call(
+        front_kernel,
+        in_specs=[VMEM] * 4,
+        out_specs=[VMEM] * 2,
+        out_shape=[
+            jax.ShapeDtypeStruct((planes, 128, 1024), BF16),
+            jax.ShapeDtypeStruct((88, 128), F32),
+        ],
+        scratch_shapes=[pltpu.VMEM((128, 256), BF16)],
+        cost_estimate=pl.CostEstimate(flops=1 << 30, bytes_accessed=6 << 20, transcendentals=0),
+        compiler_params=pltpu.CompilerParams(vmem_limit_bytes=16 << 20),
+        name="front",
+    )(positions, wave, phases, own)
+
+
 def run_sines(positions, wave, phases, after, start, planes):
     return pl.pallas_call(
         functools.partial(sines_kernel, start),
@@ -90,7 +114,7 @@
 
 def atoms_kernel(
     feat_hbm, pos_hbm, cnt_hbm, wh_hbm, wc_hbm, wave_hbm, ph_hbm, up_hbm,
-    charge_ref, own_ref, sa_ref, sb_ref,
+    charge_ref, own_ref, sb_ref,
     feat_ref, pos_ref, cnt_ref, wh_ref, wc_ref, wave_ref, ph_ref, up_ref, parts_ref, leaf_ref, mid_ref,
     plane_sems, sems,
 ):
@@ -142,7 +166,7 @@
         )
 
     others[6].wait()
-    atoms_lift(leaf_ref, up_ref, mid_ref, own_ref, sa_ref, sb_ref)
+    atoms_lift(leaf_ref, up_ref, mid_ref, own_ref, sb_ref)
 
 
 def atoms_plane(
@@ -183,7 +207,7 @@
     charge_ref[step] = jnp.where(lane_slot < counts, charge, 0.0)
 
 
-def atoms_lift(leaf_ref, up_ref, mid_ref, own_ref, sa_ref, sb_ref):
+def atoms_lift(leaf_ref, up_ref, mid_ref, own_ref, sb_ref):
     total = jnp.zeros((32, 128), F32)
     for child in range(8):
         cx, cy, cz = child // 4, child // 2 % 2, child % 2
@@ -221,7 +245,7 @@
             own_ref[row : row + 2, :] = mid_ref[x, y]
     own_ref[288:296, :] = crown
     odd = lax.axis_index("gx") % 2
-    for ref, high in ((sa_ref, 1 - odd), (sb_ref, odd)):
+    for ref, high in ((sb_ref, odd),):
         for x in range(2):
             for z in range(4):
                 row = (x * 4 + z) * 8
@@ -238,11 +262,10 @@
     return pl.pallas_call(
         atoms_kernel,
         in_specs=[hbm] * 8,
-        out_specs=[VMEM] * 4,
+        out_specs=[VMEM] * 3,
         out_shape=[
             jax.ShapeDtypeStruct((8, 8, 128), F32),
             jax.ShapeDtypeStruct((296, 128), F32),
-            jax.ShapeDtypeStruct((88, 128), F32),
             jax.ShapeDtypeStruct((88, 128), F32),
         ],
         scratch_shapes=[
@@ -740,13 +763,14 @@
     upward, downward, transfer, out_scale, in_scale,
 ):
     phases = phases.reshape(1, 128)
-    charge, own, xa, xb = run_atoms(
+    charge, own, xb = run_atoms(
         features, positions, box_counts.transpose(0, 2, 1), w_hidden, w_charge.reshape(1, 128),
         wave_numbers, phases, upward,
     )
-    front = run_sines(positions, wave_numbers, phases, own, 0, 4)
+    rb = swapped(xb, "gx", 1)
+    front, xa = run_front(positions, wave_numbers, phases, own, 4)
     scale, tin, tout, top_in, top_out = run_tables(in_scale, out_scale, own)
-    ra, rb = swapped(xa, "gx", 0), swapped(xb, "gx", 1)
+    ra = swapped(xa, "gx", 0)
     leaf, mid, top, ya, yb = glue_x(ra, rb, own, front, scale)
     back = run_sines(positions, wave_numbers, phases, top, 4, 4)
     ra, rb = swapped(ya, "gy", 0), swapped(yb, "gy", 1)

time: 101 us -> 98.6 us (0.976)
  blocking collectives: 35 us -> 31.5 us
  starting transfers between devices: 38 us -> 39.4 us
    all_to_all x1, blocking collectives: 35 us -> 31.5 us  [shards(): rows = lax.all_to_all(share, ('gx', 'gy', 'gz'), 0, 0, tiled=True)]
    pallas_call x2 -> x1, Pallas kernels: 4.18 us -> 2.09 us  [run_sines(): pl.pallas_call(functools.partial(sines_kernel, start), in_specs=[VMEM] *...]
    pallas_call x1 -> x2, Pallas kernels: 7.44 us -> 9.52 us  [the longest x1 7.44 us: run_atoms(): pl.pallas_call(atoms_kernel, in_specs=[hbm] * 8, out_specs=[VMEM] * 3, ou...]
    ppermute x8, starting transfers between devices: 38 us -> 39.4 us  [swapped(): return lax.ppermute(value, axis, pairs)]
  transfers between devices with their start and end apart: 8 -> 8, of which waited for: 1 -> 2; matrix products, arithmetic and copies ran while one was open for 0% -> 0% of each run, Pallas kernels for 13% -> 13%
where the time goes in v5:
time: 98.6 us; the launch traced here: 98.3 us
  starting transfers between devices  39.4 us (40%)
  blocking collectives  31.5 us (32%)
  Pallas kernels  24.4 us (25%)
  waiting for transfers between devices  1.14 us (1%)
    ppermute x8, starting transfers between devices, swapped(): return lax.ppermute(value, axis, pairs)  39.4 us
    all_to_all x1, blocking collectives, shards(): rows = lax.all_to_all(share, ('gx', 'gy', 'gz'), 0, 0, tiled=True)  31.5 us
    pallas_call x1, Pallas kernels, run_far(): pl.pallas_call(far_kernel, in_specs=[VMEM] * 9, out_specs=[VMEM] * 2, out...  8.54 us
    pallas_call x1, Pallas kernels, run_atoms(): pl.pallas_call(atoms_kernel, in_specs=[hbm] * 8, out_specs=[VMEM] * 3, ou...  7.44 us
    pallas_call x1, Pallas kernels, run_forces(): pl.pallas_call(force_kernel, in_specs=[VMEM] * 14, out_specs=[VMEM] * 2,...  3.18 us
    pallas_call x1, Pallas kernels, run_sines(): pl.pallas_call(functools.partial(sines_kernel, start), in_specs=[VMEM] *...  2.09 us
    pallas_call x1, Pallas kernels, run_front(): pl.pallas_call(front_kernel, in_specs=[VMEM] * 4, out_specs=[VMEM] * 2, o...  2.09 us
  transfers between devices with their start and end apart: 8, of which 2 were waited for; matrix products, arithmetic and copies ran while one was open for 0% of the time, Pallas kernels for 13%

profile of v5, /device:TPU:1, one launch (start us, length us, event | category | flops | bytes accessed | tf_op | source)
XLA Modules:
  0.0 98.3 jit_solution(8390912031013340227)
XLA Ops:
  0.7 7.4 %atoms.1 = (f32[8,8,128]{2,1,0:T(8,128)}, f32[296,128]{1,0:T(8,128)}, f32[88,128]{1,0:T(8,128)}) custom-call(bf16[8,8,128,128]{3,2,1,0:T(8,128)(2,1)} %feat_hbm.1, f32[3,8,8,128]{3,2,1,0:T(8,128)} %pos_ref.5, s32[8,4,8]{2,1,0:T(4,128)} %bitcast.12, bf16[128,128]{1,0:T(8,128)(2,1)} %wh_hbm.1, bf16[1,128]{1,0:T(2,128)(2,1)} %bitcast.13, f32[3,128]{1,0:T(4,128)} %wave_ref.5, ...), custom_call_target="tpu_custom_call" | custom-call | tf_op jit(solution)/shard_map/atoms/pallas_call | solution.py:262
  8.1 12.0 %collective-permute-start.1 = (f32[88,128]{1,0:T(8,128)}, f32[88,128]{1,0:T(8,128)S(1)}, u32[]{:S(2)}, u32[]{:S(2)}) collective-permute-start(f32[88,128]{1,0:T(8,128)} %get-tuple-element.28), channel_id=1, source_target_pairs={{0,384},{128,256},{256,128},{384,0},{1,385},{129,257},{257,129},{3... | collective-permute-start | bytes 135176 | tf_op jit(solution)/shard_map/ppermute | solution.py:758
  20.2 0.9 copy-done
  21.1 2.1 %front.1 = (bf16[4,128,1024]{2,1,0:T(8,128)(2,1)S(1)}, f32[88,128]{1,0:T(8,128)S(1)}) custom-call(f32[3,8,8,128]{3,2,1,0:T(8,128)S(1)} %copy-done.4, f32[3,128]{1,0:T(4,128)S(1)} %copy-done.7, f32[1,128]{1,0:T(1,128)S(1)} %bitcast.10, f32[296,128]{1,0:T(8,128)S(1)} %copy-done), custom_call_target="tpu_custom_call" | custom-call | flops 1073741824 | bytes 6291456 | tf_op jit(solution)/shard_map/front/pallas_call | solution.py:87
  23.2 1.9 %collective-permute-start = (f32[88,128]{1,0:T(8,128)S(1)}, f32[88,128]{1,0:T(8,128)S(1)}, u32[]{:S(2)}, u32[]{:S(2)}) collective-permute-start(f32[88,128]{1,0:T(8,128)S(1)} %get-tuple-element.27), channel_id=1, source_target_pairs={{0,128},{128,0},{256,384},{384,256},{1,129},{129,1},{257,385},{385... | collective-permute-start | bytes 135176 | tf_op jit(solution)/shard_map/ppermute | solution.py:758
  25.1 0.1 tables.1
  25.3 0.0 collective-permute-done.1.rb_ref
  25.3 1.0 %collective-permute-done.ra_ref = f32[88,128]{1,0:T(8,128)S(1)} collective-permute-done((f32[88,128]{1,0:T(8,128)S(1)}, f32[88,128]{1,0:T(8,128)S(1)}, u32[]{:S(2)}, u32[]{:S(2)}) %collective-permute-start) | collective-permute-done | bytes 45088 | tf_op jit(solution)/shard_map/ppermute | solution.py:758
  26.3 0.1 glue_x.1
  26.4 3.2 %collective-permute-start.2 = (f32[144,128]{1,0:T(8,128)S(1)}, f32[144,128]{1,0:T(8,128)S(1)}, u32[]{:S(2)}, u32[]{:S(2)}) collective-permute-start(f32[144,128]{1,0:T(8,128)S(1)} %get-tuple-element.31), channel_id=1, source_target_pairs={{0,16},{16,0},{32,48},{48,32},{64,80},{80,64},{96,112},{112,96},{1... | collective-permute-start | bytes 221192 | tf_op jit(solution)/shard_map/ppermute | solution.py:758
  29.6 4.9 %collective-permute-start.3 = (f32[144,128]{1,0:T(8,128)S(1)}, f32[144,128]{1,0:T(8,128)S(1)}, u32[]{:S(2)}, u32[]{:S(2)}) collective-permute-start(f32[144,128]{1,0:T(8,128)S(1)} %get-tuple-element.32), channel_id=1, source_target_pairs={{0,112},{16,32},{32,16},{48,64},{64,48},{80,96},{96,80},{112,0},{1... | collective-permute-start | bytes 221192 | tf_op jit(solution)/shard_map/ppermute | solution.py:758
  34.5 0.0 copy-start.5
  34.5 2.1 %sines.1._.back_ref = bf16[4,128,1024]{2,1,0:T(8,128)(2,1)S(1)} custom-call(f32[3,8,8,128]{3,2,1,0:T(8,128)S(1)} %copy-done.4, f32[3,128]{1,0:T(4,128)S(1)} %copy-done.7, f32[1,128]{1,0:T(1,128)S(1)} %bitcast.11, f32[16,128]{1,0:T(8,128)S(1)} %get-tuple-element.35._.topx_ref), custom_call_target="tpu_custom_call" | custom-call | flops 1073741824 | bytes 6291456 | tf_op jit(solution)/shard_map/sines/pallas_call | solution.py:103
  36.6 0.0 collective-permute-done.2.ra_ref
  36.6 0.1 collective-permute-done.3.rb_ref
  36.7 0.1 glue_y.1
  36.8 3.1 %collective-permute-start.4 = (f32[456,128]{1,0:T(8,128)S(1)}, f32[456,128]{1,0:T(8,128)S(1)}, u32[]{:S(2)}, u32[]{:S(2)}) collective-permute-start(f32[456,128]{1,0:T(8,128)S(1)} %get-tuple-element.38), channel_id=1, source_target_pairs={{0,1},{1,0},{2,3},{3,2},{4,5},{5,4},{6,7},{7,6},{8,9},{9,8},{10,11... | collective-permute-start | bytes 700424 | tf_op jit(solution)/shard_map/ppermute | solution.py:758
  40.0 6.2 %collective-permute-start.5 = (f32[416,128]{1,0:T(8,128)S(1)}, f32[416,128]{1,0:T(8,128)S(1)}, u32[]{:S(2)}, u32[]{:S(2)}) collective-permute-start(f32[416,128]{1,0:T(8,128)S(1)} %get-tuple-element.39), channel_id=1, source_target_pairs={{0,15},{1,2},{2,1},{3,4},{4,3},{5,6},{6,5},{7,8},{8,7},{9,10},{10,... | collective-permute-start | bytes 638984 | tf_op jit(solution)/shard_map/ppermute | solution.py:758
  46.2 0.0 collective-permute-done.4.ra_ref
  46.2 3.7 %collective-permute-start.7 = (f32[72,128]{1,0:T(8,128)S(1)}, f32[72,128]{1,0:T(8,128)S(1)}, u32[]{:S(2)}, u32[]{:S(2)}) collective-permute-start(f32[72,128]{1,0:T(8,128)S(1)} %glue_z.1.pair_ref), channel_id=1, source_target_pairs={{0,3},{1,14},{2,5},{3,0},{4,7},{5,2},{6,9},{7,4},{8,11},{9,6},{10,... | collective-permute-start | bytes 110600 | tf_op jit(solution)/shard_map/ppermute | solution.py:758
  49.9 4.4 %collective-permute-start.6 = (f32[72,128]{1,0:T(8,128)S(1)}, f32[72,128]{1,0:T(8,128)S(1)}, u32[]{:S(2)}, u32[]{:S(2)}) collective-permute-start(f32[72,128]{1,0:T(8,128)S(1)} %glue_z.1.pair_ref), channel_id=1, source_target_pairs={{0,15},{1,2},{2,1},{3,4},{4,3},{5,6},{6,5},{7,8},{8,7},{9,10},{10,... | collective-permute-start | bytes 110600 | tf_op jit(solution)/shard_map/ppermute | solution.py:758
  54.3 0.0 collective-permute-done.5.rb_ref
  54.3 0.0 copy-done.5
  54.3 0.0 copy-start.3
  54.3 8.5 %far.1 = (f32[8,32,128]{2,1,0:T(8,128)S(1)}, f32[32,128]{1,0:T(8,128)S(1)}) custom-call(f32[12,4,12,128]{3,2,1,0:T(8,128)S(1)} %get-tuple-element.36.leafxy_ref, f32[8,8,2,128]{3,2,1,0:T(2,128)S(1)} %get-tuple-element.37.midxy_ref, f32[456,128]{1,0:T(8,128)S(1)} %collective-permute-done.4.ra_ref, f32[416,128]{1,0:T(8,128)S(1)} %collective-permute-done.5.rb_ref, ...), custom_call_target="tpu_custom_call" | custom-call | flops 4294967296 | bytes 4194304 | tf_op jit(solution)/shard_map/far/pallas_call | solution.py:587
  62.9 0.0 collective-permute-done.7.next_ref
  62.9 0.0 collective-permute-done.6.near_ref
  62.9 0.0 copy-done.3
  62.9 0.0 copy-done.6
  62.9 3.2 %forces.1 = (f32[3,8,8,128]{3,2,1,0:T(8,128)}, f32[512,128]{1,0:T(8,128)S(1)}) custom-call(f32[8,32,128]{2,1,0:T(8,128)S(1)} %get-tuple-element.42.far0_ref, f32[32,128]{1,0:T(8,128)S(1)} %get-tuple-element.43.far1_ref, f32[72,128]{1,0:T(8,128)S(1)} %glue_z.1.pair_ref, f32[72,128]{1,0:T(8,128)S(1)} %collective-permute-done.6.near_ref, ...), custom_call_target="tpu_custom_call" | custom-call | tf_op jit(solution)/shard_map/forces/pallas_call | solution.py:716
  66.1 31.5 %all_to_all.11 = f32[512,1,128]{2,1,0:T(1,128)S(1)} all-to-all(f32[512,1,128]{2,1,0:T(1,128)S(1)} %bitcast.8), channel_id=1, replica_groups=mesh['gx'=4,'gy'=8,'gz'=16] {'gx','gy','gz'}, dimensions={0} | all-to-all | bytes 524288 | tf_op jit(solution)/shard_map/all_to_all | solution.py:786
  97.5 0.7 virial.1
  (13 shorter events, 0.0 us)
Async XLA Ops:
  0.6 19.5 %copy-start.7 = (f32[3,128]{1,0:T(4,128)S(1)}, f32[3,128]{1,0:T(4,128)}, u32[]{:S(2)}) copy-start(f32[3,128]{1,0:T(4,128)} %wave_ref.5) | copy-start | bytes 4612
  0.6 19.5 %copy-start.4 = (f32[3,8,8,128]{3,2,1,0:T(8,128)S(1)}, f32[3,8,8,128]{3,2,1,0:T(8,128)}, u32[]{:S(2)}) copy-start(f32[3,8,8,128]{3,2,1,0:T(8,128)} %pos_ref.5) | copy-start | bytes 294916
  0.7 19.5 %copy-start.8 = (f32[128]{0:T(128)S(1)}, f32[128]{0:T(128)}, u32[]{:S(2)}) copy-start(f32[128]{0:T(128)} %param.18) | copy-start | bytes 1540
  0.7 24.5 %copy-start.1 = (f32[3,343,128]{2,1,0:T(8,128)S(1)}, f32[3,343,128]{2,1,0:T(8,128)}, u32[]{:S(2)}) copy-start(f32[3,343,128]{2,1,0:T(8,128)} %in_ref.1) | copy-start | bytes 1580548
  0.7 24.5 %copy-start.2 = (f32[3,343,128]{2,1,0:T(8,128)S(1)}, f32[3,343,128]{2,1,0:T(8,128)}, u32[]{:S(2)}) copy-start(f32[3,343,128]{2,1,0:T(8,128)} %out_ref.3) | copy-start | bytes 1580548
  8.1 17.2 %collective-permute-start.1 = (f32[88,128]{1,0:T(8,128)}, f32[88,128]{1,0:T(8,128)S(1)}, u32[]{:S(2)}, u32[]{:S(2)}) collective-permute-start(f32[88,128]{1,0:T(8,128)} %get-tuple-element.28), channel_id=1, source_target_pairs={{0,384},{128,256},{256,128},{384,0},{1,385},{129,257},{257,129},{3... | collective-permute-start | bytes 135176 | tf_op jit(solution)/shard_map/ppermute | solution.py:758
  20.2 0.9 copy-start
  23.2 3.1 %collective-permute-start = (f32[88,128]{1,0:T(8,128)S(1)}, f32[88,128]{1,0:T(8,128)S(1)}, u32[]{:S(2)}, u32[]{:S(2)}) collective-permute-start(f32[88,128]{1,0:T(8,128)S(1)} %get-tuple-element.27), channel_id=1, source_target_pairs={{0,128},{128,0},{256,384},{384,256},{1,129},{129,1},{257,385},{385... | collective-permute-start | bytes 135176 | tf_op jit(solution)/shard_map/ppermute | solution.py:758
  26.4 10.2 %collective-permute-start.2 = (f32[144,128]{1,0:T(8,128)S(1)}, f32[144,128]{1,0:T(8,128)S(1)}, u32[]{:S(2)}, u32[]{:S(2)}) collective-permute-start(f32[144,128]{1,0:T(8,128)S(1)} %get-tuple-element.31), channel_id=1, source_target_pairs={{0,16},{16,0},{32,48},{48,32},{64,80},{80,64},{96,112},{112,96},{1... | collective-permute-start | bytes 221192 | tf_op jit(solution)/shard_map/ppermute | solution.py:758
  29.6 7.1 %collective-permute-start.3 = (f32[144,128]{1,0:T(8,128)S(1)}, f32[144,128]{1,0:T(8,128)S(1)}, u32[]{:S(2)}, u32[]{:S(2)}) collective-permute-start(f32[144,128]{1,0:T(8,128)S(1)} %get-tuple-element.32), channel_id=1, source_target_pairs={{0,112},{16,32},{32,16},{48,64},{64,48},{80,96},{96,80},{112,0},{1... | collective-permute-start | bytes 221192 | tf_op jit(solution)/shard_map/ppermute | solution.py:758
  34.5 19.8 %copy-start.5 = (bf16[3,128,128]{2,1,0:T(8,128)(2,1)S(1)}, bf16[3,128,128]{2,1,0:T(8,128)(2,1)}, u32[]{:S(2)}) copy-start(bf16[3,128,128]{2,1,0:T(8,128)(2,1)} %core_ref.3) | copy-start | bytes 294916
  36.8 9.3 %collective-permute-start.4 = (f32[456,128]{1,0:T(8,128)S(1)}, f32[456,128]{1,0:T(8,128)S(1)}, u32[]{:S(2)}, u32[]{:S(2)}) collective-permute-start(f32[456,128]{1,0:T(8,128)S(1)} %get-tuple-element.38), channel_id=1, source_target_pairs={{0,1},{1,0},{2,3},{3,2},{4,5},{5,4},{6,7},{7,6},{8,9},{9,8},{10,11... | collective-permute-start | bytes 700424 | tf_op jit(solution)/shard_map/ppermute | solution.py:758
  40.0 14.3 %collective-permute-start.5 = (f32[416,128]{1,0:T(8,128)S(1)}, f32[416,128]{1,0:T(8,128)S(1)}, u32[]{:S(2)}, u32[]{:S(2)}) collective-permute-start(f32[416,128]{1,0:T(8,128)S(1)} %get-tuple-element.39), channel_id=1, source_target_pairs={{0,15},{1,2},{2,1},{3,4},{4,3},{5,6},{6,5},{7,8},{8,7},{9,10},{10,... | collective-permute-start | bytes 638984 | tf_op jit(solution)/shard_map/ppermute | solution.py:758
  46.2 16.7 %collective-permute-start.7 = (f32[72,128]{1,0:T(8,128)S(1)}, f32[72,128]{1,0:T(8,128)S(1)}, u32[]{:S(2)}, u32[]{:S(2)}) collective-permute-start(f32[72,128]{1,0:T(8,128)S(1)} %glue_z.1.pair_ref), channel_id=1, source_target_pairs={{0,3},{1,14},{2,5},{3,0},{4,7},{5,2},{6,9},{7,4},{8,11},{9,6},{10,... | collective-permute-start | bytes 110600 | tf_op jit(solution)/shard_map/ppermute | solution.py:758
  49.9 13.0 %collective-permute-start.6 = (f32[72,128]{1,0:T(8,128)S(1)}, f32[72,128]{1,0:T(8,128)S(1)}, u32[]{:S(2)}, u32[]{:S(2)}) collective-permute-start(f32[72,128]{1,0:T(8,128)S(1)} %glue_z.1.pair_ref), channel_id=1, source_target_pairs={{0,15},{1,2},{2,1},{3,4},{4,3},{5,6},{6,5},{7,8},{8,7},{9,10},{10,... | collective-permute-start | bytes 110600 | tf_op jit(solution)/shard_map/ppermute | solution.py:758
  54.3 8.6 %copy-start.3 = (bf16[2,8,128,128]{3,2,1,0:T(8,128)(2,1)S(1)}, bf16[2,8,128,128]{3,2,1,0:T(8,128)(2,1)}, u32[]{:S(2)}) copy-start(bf16[2,8,128,128]{3,2,1,0:T(8,128)(2,1)} %down_ref.1) | copy-start | bytes 1572868
  54.3 8.6 %copy-start.6 = (f32[8,8,128]{2,1,0:T(8,128)S(1)}, f32[8,8,128]{2,1,0:T(8,128)}, u32[]{:S(2)}) copy-start(f32[8,8,128]{2,1,0:T(8,128)} %get-tuple-element.47.charge_ref) | copy-start | bytes 98308

commit v6 on v5

--- a/solution.py
+++ b/solution.py
@@ -379,6 +379,7 @@
                 row = 288 + (x * 8 + y) * 2
                 ref[row : row + 2, :] = midxy_ref[x, y]
     za_ref[416:456, :] = topxy_ref[...]
+    zb_ref[416:456, :] = topxy_ref[...]
 
 
 def glue_y(ra, rb, leafx, midx, topx, back):
@@ -391,7 +392,7 @@
             jax.ShapeDtypeStruct((8, 8, 2, 128), F32),
             jax.ShapeDtypeStruct((40, 128), F32),
             jax.ShapeDtypeStruct((456, 128), F32),
-            jax.ShapeDtypeStruct((416, 128), F32),
+            jax.ShapeDtypeStruct((456, 128), F32),
         ],
         compiler_params=pltpu.CompilerParams(vmem_limit_bytes=8 << 20),
         name="glue_y",
@@ -606,24 +607,25 @@
 
 
 def force_kernel(
-    far0_ref, far1_ref, pair_ref, near_ref, next_ref, tin_ref, tout_ref, core_ref, down_ref,
+    far0_ref, far1_ref, pair_ref, side_ref, far_ref, next_ref, tin_ref, tout_ref, core_ref, down_ref,
     charge_ref, front_ref, back_ref, pos_ref, wave_ref,
     forces_ref, share_ref,
     window_ref, operand_ref, mid_ref, local_ref,
 ):
     odd = lax.axis_index("gz") % 2
+    near, beyond = side_ref[416:452, :], far_ref[0:36, :]
+    first, second = next_ref[0:36, :], next_ref[36:72, :]
+    lines = [
+        jnp.where(odd == 1, first, beyond),
+        jnp.where(odd == 1, second, near),
+        pair_ref[0:36, :],
+        pair_ref[36:72, :],
+        jnp.where(odd == 1, near, first),
+        jnp.where(odd == 1, beyond, second),
+    ]
     for xy in range(36):
-        rows = [
-            (ref[xy : xy + 1, :], ref[36 + xy : 37 + xy, :]) for ref in (near_ref, next_ref)
-        ]
-        low = [jnp.where(odd == 1, rows[1][z], rows[0][z]) for z in range(2)]
-        high = [jnp.where(odd == 1, rows[0][z], rows[1][z]) for z in range(2)]
         window_ref[xy] = jnp.concatenate(
-            low
-            + [pair_ref[xy : xy + 1, :], pair_ref[36 + xy : 37 + xy, :]]
-            + high
-            + [jnp.zeros((2, 128), F32)],
-            axis=0,
+            [line[xy : xy + 1] for line in lines] + [jnp.zeros((2, 128), F32)], axis=0
         )
     for qx in range(6):
         for qy in range(6):
@@ -712,10 +714,10 @@
     share_ref[...] = jnp.broadcast_to(row[0:1], (512, 128))
 
 
-def run_forces(far0, far1, pair, near, following, top_in, top_out, transfer, downward, charge, front, back, positions, wave):
+def run_forces(far0, far1, pair, side, beyond, following, top_in, top_out, transfer, downward, charge, front, back, positions, wave):
     return pl.pallas_call(
         force_kernel,
-        in_specs=[VMEM] * 14,
+        in_specs=[VMEM] * 15,
         out_specs=[VMEM] * 2,
         out_shape=[
             jax.ShapeDtypeStruct((3, 8, 8, 128), F32),
@@ -729,7 +731,7 @@
         ],
         compiler_params=pltpu.CompilerParams(vmem_limit_bytes=24 << 20),
         name="forces",
-    )(far0, far1, pair, near, following, top_in, top_out, transfer, downward, charge, front, back, positions, wave)
+    )(far0, far1, pair, side, beyond, following, top_in, top_out, transfer, downward, charge, front, back, positions, wave)
 
 
 def virial_kernel(scale, rows_ref, virial_ref):
@@ -776,11 +778,14 @@
     ra, rb = swapped(ya, "gy", 0), swapped(yb, "gy", 1)
     leaf, mid, top, za, zb = glue_y(ra, rb, leaf, mid, top, back)
     ra, rb = swapped(za, "gz", 0), swapped(zb, "gz", 1)
+    beyond = lax.ppermute(
+        top, "gz", [(i, (i + (-2 if i % 2 else 2)) % 16) for i in range(16)]
+    )
     pair = glue_z(ra, top)
-    near, following = swapped(pair, "gz", 1), swapped(pair, "gz", 2)
+    following = swapped(pair, "gz", 2)
     far0, far1 = run_far(leaf, mid, ra, rb, scale, tin, tout, out_scale, transfer)
     forces, share = run_forces(
-        far0, far1, pair, near, following, top_in, top_out, transfer, downward, charge, front, back,
+        far0, far1, pair, rb, beyond, following, top_in, top_out, transfer, downward, charge, front, back,
         positions, wave_numbers,
     )
     rows = lax.all_to_all(share, ("gx", "gy", "gz"), 0, 0, tiled=True)

time: 98.6 us -> 98.7 us (level)
  starting transfers between devices: 39.4 us -> 35.3 us
  waiting for transfers between devices: 1.14 us -> 4.96 us
    ppermute x8 -> x7, starting transfers between devices: 39.4 us -> 33.4 us  [swapped(): return lax.ppermute(value, axis, pairs)]
    ppermute x8 -> x7, waiting for transfers between devices: 1.14 us -> 4.96 us  [swapped(): return lax.ppermute(value, axis, pairs)]
    ppermute x0 -> x1, starting transfers between devices: none -> 1.92 us  [shards(): lax.ppermute(top, 'gz', [(i, (i + (-2 if i % 2 else 2)) % 16) for i in ra...]
  transfers between devices with their start and end apart: 8 -> 8, of which waited for: 2 -> 3; matrix products, arithmetic and copies ran while one was open for 0% -> 0% of each run, Pallas kernels for 13% -> 13%
where the time goes in v6:
time: 98.7 us; the launch traced here: 98.3 us
  starting transfers between devices  35.3 us (36%)
  blocking collectives  31.8 us (32%)
  Pallas kernels  24.4 us (25%)
  waiting for transfers between devices  4.96 us (5%)
    ppermute x7, starting transfers between devices, swapped(): return lax.ppermute(value, axis, pairs)  33.4 us
    all_to_all x1, blocking collectives, shards(): rows = lax.all_to_all(share, ('gx', 'gy', 'gz'), 0, 0, tiled=True)  31.8 us
    pallas_call x1, Pallas kernels, run_far(): pl.pallas_call(far_kernel, in_specs=[VMEM] * 9, out_specs=[VMEM] * 2, out...  8.58 us
    pallas_call x1, Pallas kernels, run_atoms(): pl.pallas_call(atoms_kernel, in_specs=[hbm] * 8, out_specs=[VMEM] * 3, ou...  7.44 us
    ppermute x7, waiting for transfers between devices, swapped(): return lax.ppermute(value, axis, pairs)  4.96 us
    pallas_call x1, Pallas kernels, run_forces(): pl.pallas_call(force_kernel, in_specs=[VMEM] * 15, out_specs=[VMEM] * 2,...  3.17 us
    pallas_call x1, Pallas kernels, run_sines(): pl.pallas_call(functools.partial(sines_kernel, start), in_specs=[VMEM] *...  2.09 us
    pallas_call x1, Pallas kernels, run_front(): pl.pallas_call(front_kernel, in_specs=[VMEM] * 4, out_specs=[VMEM] * 2, o...  2.09 us
  transfers between devices with their start and end apart: 8, of which 3 were waited for; matrix products, arithmetic and copies ran while one was open for 0% of the time, Pallas kernels for 13%

profile of v6, /device:TPU:1, one launch (start us, length us, event | category | flops | bytes accessed | tf_op | source)
XLA Modules:
  0.0 98.3 jit_solution(18279933419182321567)
XLA Ops:
  0.6 0.0 copy-start.7
  0.6 0.0 copy-start.4
  0.7 0.0 copy-start.8
  0.7 0.0 copy-start.1
  0.7 7.4 %atoms.1 = (f32[8,8,128]{2,1,0:T(8,128)}, f32[296,128]{1,0:T(8,128)}, f32[88,128]{1,0:T(8,128)}) custom-call(bf16[8,8,128,128]{3,2,1,0:T(8,128)(2,1)} %feat_hbm.1, f32[3,8,8,128]{3,2,1,0:T(8,128)} %pos_ref.5, s32[8,4,8]{2,1,0:T(4,128)} %bitcast.12, bf16[128,128]{1,0:T(8,128)(2,1)} %wh_hbm.1, bf16[1,128]{1,0:T(2,128)(2,1)} %bitcast.13, f32[3,128]{1,0:T(4,128)} %wave_ref.5, ...), custom_call_target="tpu_custom_call" | custom-call | tf_op jit(solution)/shard_map/atoms/pallas_call | solution.py:262
  8.1 12.0 %collective-permute-start.1 = (f32[88,128]{1,0:T(8,128)}, f32[88,128]{1,0:T(8,128)S(1)}, u32[]{:S(2)}, u32[]{:S(2)}) collective-permute-start(f32[88,128]{1,0:T(8,128)} %get-tuple-element.28), channel_id=1, source_target_pairs={{0,384},{128,256},{256,128},{384,0},{1,385},{129,257},{257,129},{3... | collective-permute-start | bytes 135176 | tf_op jit(solution)/shard_map/ppermute | solution.py:760
  20.2 0.9 copy-done
  21.1 2.1 %front.1 = (bf16[4,128,1024]{2,1,0:T(8,128)(2,1)S(1)}, f32[88,128]{1,0:T(8,128)S(1)}) custom-call(f32[3,8,8,128]{3,2,1,0:T(8,128)S(1)} %copy-done.4, f32[3,128]{1,0:T(4,128)S(1)} %copy-done.7, f32[1,128]{1,0:T(1,128)S(1)} %bitcast.10, f32[296,128]{1,0:T(8,128)S(1)} %copy-done), custom_call_target="tpu_custom_call" | custom-call | flops 1073741824 | bytes 6291456 | tf_op jit(solution)/shard_map/front/pallas_call | solution.py:87
  23.2 1.9 %collective-permute-start = (f32[88,128]{1,0:T(8,128)S(1)}, f32[88,128]{1,0:T(8,128)S(1)}, u32[]{:S(2)}, u32[]{:S(2)}) collective-permute-start(f32[88,128]{1,0:T(8,128)S(1)} %get-tuple-element.27), channel_id=1, source_target_pairs={{0,128},{128,0},{256,384},{384,256},{1,129},{129,1},{257,385},{385... | collective-permute-start | bytes 135176 | tf_op jit(solution)/shard_map/ppermute | solution.py:760
  25.1 0.1 tables.1
  25.3 0.0 collective-permute-done.1.rb_ref
  25.3 1.0 %collective-permute-done.ra_ref = f32[88,128]{1,0:T(8,128)S(1)} collective-permute-done((f32[88,128]{1,0:T(8,128)S(1)}, f32[88,128]{1,0:T(8,128)S(1)}, u32[]{:S(2)}, u32[]{:S(2)}) %collective-permute-start) | collective-permute-done | bytes 45088 | tf_op jit(solution)/shard_map/ppermute | solution.py:760
  26.3 0.1 glue_x.1
  26.4 3.2 %collective-permute-start.2 = (f32[144,128]{1,0:T(8,128)S(1)}, f32[144,128]{1,0:T(8,128)S(1)}, u32[]{:S(2)}, u32[]{:S(2)}) collective-permute-start(f32[144,128]{1,0:T(8,128)S(1)} %get-tuple-element.31), channel_id=1, source_target_pairs={{0,16},{16,0},{32,48},{48,32},{64,80},{80,64},{96,112},{112,96},{1... | collective-permute-start | bytes 221192 | tf_op jit(solution)/shard_map/ppermute | solution.py:760
  29.6 4.9 %collective-permute-start.3 = (f32[144,128]{1,0:T(8,128)S(1)}, f32[144,128]{1,0:T(8,128)S(1)}, u32[]{:S(2)}, u32[]{:S(2)}) collective-permute-start(f32[144,128]{1,0:T(8,128)S(1)} %get-tuple-element.32), channel_id=1, source_target_pairs={{0,112},{16,32},{32,16},{48,64},{64,48},{80,96},{96,80},{112,0},{1... | collective-permute-start | bytes 221192 | tf_op jit(solution)/shard_map/ppermute | solution.py:760
  34.5 0.0 copy-start.5
  34.5 2.1 %sines.1._.back_ref = bf16[4,128,1024]{2,1,0:T(8,128)(2,1)S(1)} custom-call(f32[3,8,8,128]{3,2,1,0:T(8,128)S(1)} %copy-done.4, f32[3,128]{1,0:T(4,128)S(1)} %copy-done.7, f32[1,128]{1,0:T(1,128)S(1)} %bitcast.11, f32[16,128]{1,0:T(8,128)S(1)} %get-tuple-element.35._.topx_ref), custom_call_target="tpu_custom_call" | custom-call | flops 1073741824 | bytes 6291456 | tf_op jit(solution)/shard_map/sines/pallas_call | solution.py:103
  36.6 0.0 collective-permute-done.2.ra_ref
  36.6 0.1 collective-permute-done.3.rb_ref
  36.7 0.1 glue_y.1
  36.8 3.1 %collective-permute-start.4 = (f32[456,128]{1,0:T(8,128)S(1)}, f32[456,128]{1,0:T(8,128)S(1)}, u32[]{:S(2)}, u32[]{:S(2)}) collective-permute-start(f32[456,128]{1,0:T(8,128)S(1)} %get-tuple-element.38), channel_id=1, source_target_pairs={{0,1},{1,0},{2,3},{3,2},{4,5},{5,4},{6,7},{7,6},{8,9},{9,8},{10,11... | collective-permute-start | bytes 700424 | tf_op jit(solution)/shard_map/ppermute | solution.py:760
  40.0 6.2 %collective-permute-start.5 = (f32[456,128]{1,0:T(8,128)S(1)}, f32[456,128]{1,0:T(8,128)S(1)}, u32[]{:S(2)}, u32[]{:S(2)}) collective-permute-start(f32[456,128]{1,0:T(8,128)S(1)} %get-tuple-element.39), channel_id=1, source_target_pairs={{0,15},{1,2},{2,1},{3,4},{4,3},{5,6},{6,5},{7,8},{8,7},{9,10},{10,... | collective-permute-start | bytes 700424 | tf_op jit(solution)/shard_map/ppermute | solution.py:760
  46.2 1.9 %collective-permute-start.6 = (f32[40,128]{1,0:T(8,128)S(1)}, f32[40,128]{1,0:T(8,128)S(1)}, u32[]{:S(2)}, u32[]{:S(2)}) collective-permute-start(f32[40,128]{1,0:T(8,128)S(1)} %get-tuple-element.44.topxy_ref), channel_id=1, source_target_pairs={{0,2},{1,15},{2,4},{3,1},{4,6},{5,3},{6,8},{7,5},{8,10},{9,7},{10,... | collective-permute-start | bytes 61448 | tf_op jit(solution)/shard_map/ppermute | solution.py:781
  48.1 0.0 collective-permute-done.4.ra_ref
  48.1 2.1 %collective-permute-start.7 = (f32[72,128]{1,0:T(8,128)S(1)}, f32[72,128]{1,0:T(8,128)S(1)}, u32[]{:S(2)}, u32[]{:S(2)}) collective-permute-start(f32[72,128]{1,0:T(8,128)S(1)} %glue_z.1.pair_ref), channel_id=1, source_target_pairs={{0,3},{1,14},{2,5},{3,0},{4,7},{5,2},{6,9},{7,4},{8,11},{9,6},{10,... | collective-permute-start | bytes 110600 | tf_op jit(solution)/shard_map/ppermute | solution.py:760
  50.2 3.8 %collective-permute-done.5.rb_ref.side_ref = f32[456,128]{1,0:T(8,128)S(1)} collective-permute-done((f32[456,128]{1,0:T(8,128)S(1)}, f32[456,128]{1,0:T(8,128)S(1)}, u32[]{:S(2)}, u32[]{:S(2)}) %collective-permute-start.5) | collective-permute-done | bytes 233504 | tf_op jit(solution)/shard_map/ppermute | solution.py:760
  54.0 8.6 %far.1 = (f32[8,32,128]{2,1,0:T(8,128)S(1)}, f32[32,128]{1,0:T(8,128)S(1)}) custom-call(f32[12,4,12,128]{3,2,1,0:T(8,128)S(1)} %get-tuple-element.36.leafxy_ref, f32[8,8,2,128]{3,2,1,0:T(2,128)S(1)} %get-tuple-element.37.midxy_ref, f32[456,128]{1,0:T(8,128)S(1)} %collective-permute-done.4.ra_ref, f32[456,128]{1,0:T(8,128)S(1)} %collective-permute-done.5.rb_ref.side_ref, ...), custom_call_target="tpu_custom_call" | custom-call | flops 4294967296 | bytes 4194304 | tf_op jit(solution)/shard_map/far/pallas_call | solution.py:588
  62.6 0.0 collective-permute-done.6.far_ref
  62.6 0.0 collective-permute-done.7.next_ref
  62.7 3.2 %forces.1 = (f32[3,8,8,128]{3,2,1,0:T(8,128)}, f32[512,128]{1,0:T(8,128)S(1)}) custom-call(f32[8,32,128]{2,1,0:T(8,128)S(1)} %get-tuple-element.42.far0_ref, f32[32,128]{1,0:T(8,128)S(1)} %get-tuple-element.43.far1_ref, f32[72,128]{1,0:T(8,128)S(1)} %glue_z.1.pair_ref, f32[456,128]{1,0:T(8,128)S(1)} %collective-permute-done.5.rb_ref.side_ref, ...), custom_call_target="tpu_custom_call" | custom-call | tf_op jit(solution)/shard_map/forces/pallas_call | solution.py:718
  65.8 31.8 %all_to_all.11 = f32[512,1,128]{2,1,0:T(1,128)S(1)} all-to-all(f32[512,1,128]{2,1,0:T(1,128)S(1)} %bitcast.8), channel_id=1, replica_groups=mesh['gx'=4,'gy'=8,'gz'=16] {'gx','gy','gz'}, dimensions={0} | all-to-all | bytes 524288 | tf_op jit(solution)/shard_map/all_to_all | solution.py:791
  97.6 0.7 virial.1
  (13 shorter events, 0.0 us)
Async XLA Ops:
  0.6 19.5 %copy-start.7 = (f32[3,128]{1,0:T(4,128)S(1)}, f32[3,128]{1,0:T(4,128)}, u32[]{:S(2)}) copy-start(f32[3,128]{1,0:T(4,128)} %wave_ref.5) | copy-start | bytes 4612
  0.6 19.5 %copy-start.4 = (f32[3,8,8,128]{3,2,1,0:T(8,128)S(1)}, f32[3,8,8,128]{3,2,1,0:T(8,128)}, u32[]{:S(2)}) copy-start(f32[3,8,8,128]{3,2,1,0:T(8,128)} %pos_ref.5) | copy-start | bytes 294916
  0.7 19.5 %copy-start.8 = (f32[128]{0:T(128)S(1)}, f32[128]{0:T(128)}, u32[]{:S(2)}) copy-start(f32[128]{0:T(128)} %param.18) | copy-start | bytes 1540
  0.7 24.5 %copy-start.1 = (f32[3,343,128]{2,1,0:T(8,128)S(1)}, f32[3,343,128]{2,1,0:T(8,128)}, u32[]{:S(2)}) copy-start(f32[3,343,128]{2,1,0:T(8,128)} %in_ref.1) | copy-start | bytes 1580548
  0.7 24.5 %copy-start.2 = (f32[3,343,128]{2,1,0:T(8,128)S(1)}, f32[3,343,128]{2,1,0:T(8,128)}, u32[]{:S(2)}) copy-start(f32[3,343,128]{2,1,0:T(8,128)} %out_ref.3) | copy-start | bytes 1580548
  8.1 17.2 %collective-permute-start.1 = (f32[88,128]{1,0:T(8,128)}, f32[88,128]{1,0:T(8,128)S(1)}, u32[]{:S(2)}, u32[]{:S(2)}) collective-permute-start(f32[88,128]{1,0:T(8,128)} %get-tuple-element.28), channel_id=1, source_target_pairs={{0,384},{128,256},{256,128},{384,0},{1,385},{129,257},{257,129},{3... | collective-permute-start | bytes 135176 | tf_op jit(solution)/shard_map/ppermute | solution.py:760
  20.2 0.9 copy-start
  23.2 3.1 %collective-permute-start = (f32[88,128]{1,0:T(8,128)S(1)}, f32[88,128]{1,0:T(8,128)S(1)}, u32[]{:S(2)}, u32[]{:S(2)}) collective-permute-start(f32[88,128]{1,0:T(8,128)S(1)} %get-tuple-element.27), channel_id=1, source_target_pairs={{0,128},{128,0},{256,384},{384,256},{1,129},{129,1},{257,385},{385... | collective-permute-start | bytes 135176 | tf_op jit(solution)/shard_map/ppermute | solution.py:760
  26.4 10.2 %collective-permute-start.2 = (f32[144,128]{1,0:T(8,128)S(1)}, f32[144,128]{1,0:T(8,128)S(1)}, u32[]{:S(2)}, u32[]{:S(2)}) collective-permute-start(f32[144,128]{1,0:T(8,128)S(1)} %get-tuple-element.31), channel_id=1, source_target_pairs={{0,16},{16,0},{32,48},{48,32},{64,80},{80,64},{96,112},{112,96},{1... | collective-permute-start | bytes 221192 | tf_op jit(solution)/shard_map/ppermute | solution.py:760
  29.6 7.1 %collective-permute-start.3 = (f32[144,128]{1,0:T(8,128)S(1)}, f32[144,128]{1,0:T(8,128)S(1)}, u32[]{:S(2)}, u32[]{:S(2)}) collective-permute-start(f32[144,128]{1,0:T(8,128)S(1)} %get-tuple-element.32), channel_id=1, source_target_pairs={{0,112},{16,32},{32,16},{48,64},{64,48},{80,96},{96,80},{112,0},{1... | collective-permute-start | bytes 221192 | tf_op jit(solution)/shard_map/ppermute | solution.py:760
  34.5 19.6 %copy-start.5 = (bf16[3,128,128]{2,1,0:T(8,128)(2,1)S(1)}, bf16[3,128,128]{2,1,0:T(8,128)(2,1)}, u32[]{:S(2)}) copy-start(bf16[3,128,128]{2,1,0:T(8,128)(2,1)} %core_ref.3) | copy-start | bytes 294916
  36.8 11.2 %collective-permute-start.4 = (f32[456,128]{1,0:T(8,128)S(1)}, f32[456,128]{1,0:T(8,128)S(1)}, u32[]{:S(2)}, u32[]{:S(2)}) collective-permute-start(f32[456,128]{1,0:T(8,128)S(1)} %get-tuple-element.38), channel_id=1, source_target_pairs={{0,1},{1,0},{2,3},{3,2},{4,5},{5,4},{6,7},{7,6},{8,9},{9,8},{10,11... | collective-permute-start | bytes 700424 | tf_op jit(solution)/shard_map/ppermute | solution.py:760
  40.0 14.1 %collective-permute-start.5 = (f32[456,128]{1,0:T(8,128)S(1)}, f32[456,128]{1,0:T(8,128)S(1)}, u32[]{:S(2)}, u32[]{:S(2)}) collective-permute-start(f32[456,128]{1,0:T(8,128)S(1)} %get-tuple-element.39), channel_id=1, source_target_pairs={{0,15},{1,2},{2,1},{3,4},{4,3},{5,6},{6,5},{7,8},{8,7},{9,10},{10,... | collective-permute-start | bytes 700424 | tf_op jit(solution)/shard_map/ppermute | solution.py:760
  46.2 16.5 %collective-permute-start.6 = (f32[40,128]{1,0:T(8,128)S(1)}, f32[40,128]{1,0:T(8,128)S(1)}, u32[]{:S(2)}, u32[]{:S(2)}) collective-permute-start(f32[40,128]{1,0:T(8,128)S(1)} %get-tuple-element.44.topxy_ref), channel_id=1, source_target_pairs={{0,2},{1,15},{2,4},{3,1},{4,6},{5,3},{6,8},{7,5},{8,10},{9,7},{10,... | collective-permute-start | bytes 61448 | tf_op jit(solution)/shard_map/ppermute | solution.py:781
  48.1 14.5 %collective-permute-start.7 = (f32[72,128]{1,0:T(8,128)S(1)}, f32[72,128]{1,0:T(8,128)S(1)}, u32[]{:S(2)}, u32[]{:S(2)}) collective-permute-start(f32[72,128]{1,0:T(8,128)S(1)} %glue_z.1.pair_ref), channel_id=1, source_target_pairs={{0,3},{1,14},{2,5},{3,0},{4,7},{5,2},{6,9},{7,4},{8,11},{9,6},{10,... | collective-permute-start | bytes 110600 | tf_op jit(solution)/shard_map/ppermute | solution.py:760
  54.0 8.6 %copy-start.3 = (bf16[2,8,128,128]{3,2,1,0:T(8,128)(2,1)S(1)}, bf16[2,8,128,128]{3,2,1,0:T(8,128)(2,1)}, u32[]{:S(2)}) copy-start(bf16[2,8,128,128]{3,2,1,0:T(8,128)(2,1)} %down_ref.1) | copy-start | bytes 1572868
  54.0 8.6 %copy-start.6 = (f32[8,8,128]{2,1,0:T(8,128)S(1)}, f32[8,8,128]{2,1,0:T(8,128)}, u32[]{:S(2)}) copy-start(f32[8,8,128]{2,1,0:T(8,128)} %get-tuple-element.47.charge_ref) | copy-start | bytes 98308

commit v7 on v6

--- a/solution.py
+++ b/solution.py
@@ -495,6 +495,10 @@
                 ],
                 axis=0,
             )
+    def products(operand_ref, core):
+        rows = 384
+        return [dot(operand_ref[i * rows : i * rows + rows, :], core) for i in range(4)]
+
     far0_ref[...] = jnp.zeros((8, 32, 128), F32)
     core0 = core_ref[0]
 
@@ -525,17 +529,17 @@
                     row = row_of(qx, qy, qz, pair, cz)
                     scale = jnp.broadcast_to(out_ref[0, pl.ds(row, 1), :], (32, 128))
                     start = ((pair * 2 + cz) * 6 + qy) * 32
-                    total = total + scale * image[start : start + 32]
+                    total = total + scale * image[start // 384][start % 384 : start % 384 + 32]
                 far0_ref[pair * 2 + cz] = total
 
     build_leaf(0, even_ref)
 
     @pl.loop(0, 18)
     def _(turn):
-        image = dot(even_ref[...], core0)
+        image = products(even_ref, core0)
         build_leaf(2 * turn + 1, odd_ref)
         apply_leaf(2 * turn, image)
-        image = dot(odd_ref[...], core0)
+        image = products(odd_ref, core0)
         build_leaf(jnp.minimum(2 * turn + 2, 35), even_ref)
         apply_leaf(2 * turn + 1, image)
 
@@ -562,17 +566,17 @@
                     scale = tout_ref[cz, (qx + 1 - pair // 2) * 7 + qy + 1 - pair % 2]
                     scale = jnp.concatenate([scale] * 4, axis=0)
                     start = ((pair * 2 + cz) * 6 + qy) * 32
-                    total = total + scale * image[start : start + 32]
+                    total = total + scale * image[start // 384][start % 384 : start % 384 + 32]
                 acc_ref[pair * 2 + cz] = total
 
     build_mid(0, even_ref)
 
     @pl.loop(0, 3)
     def _(turn):
-        image = dot(even_ref[...], core1)
+        image = products(even_ref, core1)
         build_mid(2 * turn + 1, odd_ref)
         apply_mid(2 * turn, image)
-        image = dot(odd_ref[...], core1)
+        image = products(odd_ref, core1)
         build_mid(jnp.minimum(2 * turn + 2, 5), even_ref)
         apply_mid(2 * turn + 1, image)
 

time: 98.7 us -> 98.1 us (level)
  no operation moved by 1% of the time
where the time goes in v7:
time: 98.1 us; the launch traced here: 97.7 us
  starting transfers between devices  35.3 us (36%)
  blocking collectives  31.8 us (32%)
  Pallas kernels  23.8 us (24%)
  waiting for transfers between devices  4.96 us (5%)
    ppermute x7, starting transfers between devices, swapped(): return lax.ppermute(value, axis, pairs)  33.4 us
    all_to_all x1, blocking collectives, shards(): rows = lax.all_to_all(share, ('gx', 'gy', 'gz'), 0, 0, tiled=True)  31.8 us
    pallas_call x1, Pallas kernels, run_far(): pl.pallas_call(far_kernel, in_specs=[VMEM] * 9, out_specs=[VMEM] * 2, out...  7.95 us
    pallas_call x1, Pallas kernels, run_atoms(): pl.pallas_call(atoms_kernel, in_specs=[hbm] * 8, out_specs=[VMEM] * 3, ou...  7.44 us
    ppermute x7, waiting for transfers between devices, swapped(): return lax.ppermute(value, axis, pairs)  4.96 us
    pallas_call x1, Pallas kernels, run_forces(): pl.pallas_call(force_kernel, in_specs=[VMEM] * 15, out_specs=[VMEM] * 2,...  3.16 us
    pallas_call x1, Pallas kernels, run_sines(): pl.pallas_call(functools.partial(sines_kernel, start), in_specs=[VMEM] *...  2.09 us
    pallas_call x1, Pallas kernels, run_front(): pl.pallas_call(front_kernel, in_specs=[VMEM] * 4, out_specs=[VMEM] * 2, o...  2.09 us
  transfers between devices with their start and end apart: 8, of which 3 were waited for; matrix products, arithmetic and copies ran while one was open for 0% of the time, Pallas kernels for 13%

profile of v7, /device:TPU:1, one launch (start us, length us, event | category | flops | bytes accessed | tf_op | source)
XLA Modules:
  0.0 97.7 jit_solution(2641309957869235879)
XLA Ops:
  0.6 0.0 copy-start.7
  0.6 0.0 copy-start.4
  0.7 0.0 copy-start.8
  0.7 0.0 copy-start.1
  0.7 7.4 %atoms.1 = (f32[8,8,128]{2,1,0:T(8,128)}, f32[296,128]{1,0:T(8,128)}, f32[88,128]{1,0:T(8,128)}) custom-call(bf16[8,8,128,128]{3,2,1,0:T(8,128)(2,1)} %feat_hbm.1, f32[3,8,8,128]{3,2,1,0:T(8,128)} %pos_ref.5, s32[8,4,8]{2,1,0:T(4,128)} %bitcast.12, bf16[128,128]{1,0:T(8,128)(2,1)} %wh_hbm.1, bf16[1,128]{1,0:T(2,128)(2,1)} %bitcast.13, f32[3,128]{1,0:T(4,128)} %wave_ref.5, ...), custom_call_target="tpu_custom_call" | custom-call | tf_op jit(solution)/shard_map/atoms/pallas_call | solution.py:262
  8.1 12.0 %collective-permute-start.1 = (f32[88,128]{1,0:T(8,128)}, f32[88,128]{1,0:T(8,128)S(1)}, u32[]{:S(2)}, u32[]{:S(2)}) collective-permute-start(f32[88,128]{1,0:T(8,128)} %get-tuple-element.28), channel_id=1, source_target_pairs={{0,384},{128,256},{256,128},{384,0},{1,385},{129,257},{257,129},{3... | collective-permute-start | bytes 135176 | tf_op jit(solution)/shard_map/ppermute | solution.py:764
  20.2 0.9 copy-done
  21.1 2.1 %front.1 = (bf16[4,128,1024]{2,1,0:T(8,128)(2,1)S(1)}, f32[88,128]{1,0:T(8,128)S(1)}) custom-call(f32[3,8,8,128]{3,2,1,0:T(8,128)S(1)} %copy-done.4, f32[3,128]{1,0:T(4,128)S(1)} %copy-done.7, f32[1,128]{1,0:T(1,128)S(1)} %bitcast.10, f32[296,128]{1,0:T(8,128)S(1)} %copy-done), custom_call_target="tpu_custom_call" | custom-call | flops 1073741824 | bytes 6291456 | tf_op jit(solution)/shard_map/front/pallas_call | solution.py:87
  23.2 1.9 %collective-permute-start = (f32[88,128]{1,0:T(8,128)S(1)}, f32[88,128]{1,0:T(8,128)S(1)}, u32[]{:S(2)}, u32[]{:S(2)}) collective-permute-start(f32[88,128]{1,0:T(8,128)S(1)} %get-tuple-element.27), channel_id=1, source_target_pairs={{0,128},{128,0},{256,384},{384,256},{1,129},{129,1},{257,385},{385... | collective-permute-start | bytes 135176 | tf_op jit(solution)/shard_map/ppermute | solution.py:764
  25.1 0.1 tables.1
  25.3 0.0 collective-permute-done.1.rb_ref
  25.3 1.0 %collective-permute-done.ra_ref = f32[88,128]{1,0:T(8,128)S(1)} collective-permute-done((f32[88,128]{1,0:T(8,128)S(1)}, f32[88,128]{1,0:T(8,128)S(1)}, u32[]{:S(2)}, u32[]{:S(2)}) %collective-permute-start) | collective-permute-done | bytes 45088 | tf_op jit(solution)/shard_map/ppermute | solution.py:764
  26.3 0.1 glue_x.1
  26.4 3.2 %collective-permute-start.2 = (f32[144,128]{1,0:T(8,128)S(1)}, f32[144,128]{1,0:T(8,128)S(1)}, u32[]{:S(2)}, u32[]{:S(2)}) collective-permute-start(f32[144,128]{1,0:T(8,128)S(1)} %get-tuple-element.31), channel_id=1, source_target_pairs={{0,16},{16,0},{32,48},{48,32},{64,80},{80,64},{96,112},{112,96},{1... | collective-permute-start | bytes 221192 | tf_op jit(solution)/shard_map/ppermute | solution.py:764
  29.6 4.9 %collective-permute-start.3 = (f32[144,128]{1,0:T(8,128)S(1)}, f32[144,128]{1,0:T(8,128)S(1)}, u32[]{:S(2)}, u32[]{:S(2)}) collective-permute-start(f32[144,128]{1,0:T(8,128)S(1)} %get-tuple-element.32), channel_id=1, source_target_pairs={{0,112},{16,32},{32,16},{48,64},{64,48},{80,96},{96,80},{112,0},{1... | collective-permute-start | bytes 221192 | tf_op jit(solution)/shard_map/ppermute | solution.py:764
  34.5 0.0 copy-start.5
  34.5 2.1 %sines.1._.back_ref = bf16[4,128,1024]{2,1,0:T(8,128)(2,1)S(1)} custom-call(f32[3,8,8,128]{3,2,1,0:T(8,128)S(1)} %copy-done.4, f32[3,128]{1,0:T(4,128)S(1)} %copy-done.7, f32[1,128]{1,0:T(1,128)S(1)} %bitcast.11, f32[16,128]{1,0:T(8,128)S(1)} %get-tuple-element.35._.topx_ref), custom_call_target="tpu_custom_call" | custom-call | flops 1073741824 | bytes 6291456 | tf_op jit(solution)/shard_map/sines/pallas_call | solution.py:103
  36.6 0.0 collective-permute-done.2.ra_ref
  36.6 0.1 collective-permute-done.3.rb_ref
  36.7 0.1 glue_y.1
  36.8 3.1 %collective-permute-start.4 = (f32[456,128]{1,0:T(8,128)S(1)}, f32[456,128]{1,0:T(8,128)S(1)}, u32[]{:S(2)}, u32[]{:S(2)}) collective-permute-start(f32[456,128]{1,0:T(8,128)S(1)} %get-tuple-element.38), channel_id=1, source_target_pairs={{0,1},{1,0},{2,3},{3,2},{4,5},{5,4},{6,7},{7,6},{8,9},{9,8},{10,11... | collective-permute-start | bytes 700424 | tf_op jit(solution)/shard_map/ppermute | solution.py:764
  40.0 6.2 %collective-permute-start.5 = (f32[456,128]{1,0:T(8,128)S(1)}, f32[456,128]{1,0:T(8,128)S(1)}, u32[]{:S(2)}, u32[]{:S(2)}) collective-permute-start(f32[456,128]{1,0:T(8,128)S(1)} %get-tuple-element.39), channel_id=1, source_target_pairs={{0,15},{1,2},{2,1},{3,4},{4,3},{5,6},{6,5},{7,8},{8,7},{9,10},{10,... | collective-permute-start | bytes 700424 | tf_op jit(solution)/shard_map/ppermute | solution.py:764
  46.2 1.9 %collective-permute-start.6 = (f32[40,128]{1,0:T(8,128)S(1)}, f32[40,128]{1,0:T(8,128)S(1)}, u32[]{:S(2)}, u32[]{:S(2)}) collective-permute-start(f32[40,128]{1,0:T(8,128)S(1)} %get-tuple-element.44.topxy_ref), channel_id=1, source_target_pairs={{0,2},{1,15},{2,4},{3,1},{4,6},{5,3},{6,8},{7,5},{8,10},{9,7},{10,... | collective-permute-start | bytes 61448 | tf_op jit(solution)/shard_map/ppermute | solution.py:785
  48.1 0.0 collective-permute-done.4.ra_ref
  48.1 2.1 %collective-permute-start.7 = (f32[72,128]{1,0:T(8,128)S(1)}, f32[72,128]{1,0:T(8,128)S(1)}, u32[]{:S(2)}, u32[]{:S(2)}) collective-permute-start(f32[72,128]{1,0:T(8,128)S(1)} %glue_z.1.pair_ref), channel_id=1, source_target_pairs={{0,3},{1,14},{2,5},{3,0},{4,7},{5,2},{6,9},{7,4},{8,11},{9,6},{10,... | collective-permute-start | bytes 110600 | tf_op jit(solution)/shard_map/ppermute | solution.py:764
  50.2 3.8 %collective-permute-done.5.rb_ref.side_ref = f32[456,128]{1,0:T(8,128)S(1)} collective-permute-done((f32[456,128]{1,0:T(8,128)S(1)}, f32[456,128]{1,0:T(8,128)S(1)}, u32[]{:S(2)}, u32[]{:S(2)}) %collective-permute-start.5) | collective-permute-done | bytes 233504 | tf_op jit(solution)/shard_map/ppermute | solution.py:764
  54.0 7.9 %far.1 = (f32[8,32,128]{2,1,0:T(8,128)S(1)}, f32[32,128]{1,0:T(8,128)S(1)}) custom-call(f32[12,4,12,128]{3,2,1,0:T(8,128)S(1)} %get-tuple-element.36.leafxy_ref, f32[8,8,2,128]{3,2,1,0:T(2,128)S(1)} %get-tuple-element.37.midxy_ref, f32[456,128]{1,0:T(8,128)S(1)} %collective-permute-done.4.ra_ref, f32[456,128]{1,0:T(8,128)S(1)} %collective-permute-done.5.rb_ref.side_ref, ...), custom_call_target="tpu_custom_call" | custom-call | flops 4294967296 | bytes 4194304 | tf_op jit(solution)/shard_map/far/pallas_call | solution.py:592
  62.0 0.0 collective-permute-done.6.far_ref
  62.0 0.0 collective-permute-done.7.next_ref
  62.0 3.2 %forces.1 = (f32[3,8,8,128]{3,2,1,0:T(8,128)}, f32[512,128]{1,0:T(8,128)S(1)}) custom-call(f32[8,32,128]{2,1,0:T(8,128)S(1)} %get-tuple-element.42.far0_ref, f32[32,128]{1,0:T(8,128)S(1)} %get-tuple-element.43.far1_ref, f32[72,128]{1,0:T(8,128)S(1)} %glue_z.1.pair_ref, f32[456,128]{1,0:T(8,128)S(1)} %collective-permute-done.5.rb_ref.side_ref, ...), custom_call_target="tpu_custom_call" | custom-call | tf_op jit(solution)/shard_map/forces/pallas_call | solution.py:722
  65.2 31.8 %all_to_all.11 = f32[512,1,128]{2,1,0:T(1,128)S(1)} all-to-all(f32[512,1,128]{2,1,0:T(1,128)S(1)} %bitcast.8), channel_id=1, replica_groups=mesh['gx'=4,'gy'=8,'gz'=16] {'gx','gy','gz'}, dimensions={0} | all-to-all | bytes 524288 | tf_op jit(solution)/shard_map/all_to_all | solution.py:795
  97.0 0.7 virial.1
  (13 shorter events, 0.0 us)
Async XLA Ops:
  0.6 19.5 %copy-start.7 = (f32[3,128]{1,0:T(4,128)S(1)}, f32[3,128]{1,0:T(4,128)}, u32[]{:S(2)}) copy-start(f32[3,128]{1,0:T(4,128)} %wave_ref.5) | copy-start | bytes 4612
  0.6 19.5 %copy-start.4 = (f32[3,8,8,128]{3,2,1,0:T(8,128)S(1)}, f32[3,8,8,128]{3,2,1,0:T(8,128)}, u32[]{:S(2)}) copy-start(f32[3,8,8,128]{3,2,1,0:T(8,128)} %pos_ref.5) | copy-start | bytes 294916
  0.7 19.5 %copy-start.8 = (f32[128]{0:T(128)S(1)}, f32[128]{0:T(128)}, u32[]{:S(2)}) copy-start(f32[128]{0:T(128)} %param.18) | copy-start | bytes 1540
  0.7 24.5 %copy-start.1 = (f32[3,343,128]{2,1,0:T(8,128)S(1)}, f32[3,343,128]{2,1,0:T(8,128)}, u32[]{:S(2)}) copy-start(f32[3,343,128]{2,1,0:T(8,128)} %in_ref.1) | copy-start | bytes 1580548
  0.7 24.5 %copy-start.2 = (f32[3,343,128]{2,1,0:T(8,128)S(1)}, f32[3,343,128]{2,1,0:T(8,128)}, u32[]{:S(2)}) copy-start(f32[3,343,128]{2,1,0:T(8,128)} %out_ref.3) | copy-start | bytes 1580548
  8.1 17.2 %collective-permute-start.1 = (f32[88,128]{1,0:T(8,128)}, f32[88,128]{1,0:T(8,128)S(1)}, u32[]{:S(2)}, u32[]{:S(2)}) collective-permute-start(f32[88,128]{1,0:T(8,128)} %get-tuple-element.28), channel_id=1, source_target_pairs={{0,384},{128,256},{256,128},{384,0},{1,385},{129,257},{257,129},{3... | collective-permute-start | bytes 135176 | tf_op jit(solution)/shard_map/ppermute | solution.py:764
  20.2 0.9 copy-start
  23.2 3.1 %collective-permute-start = (f32[88,128]{1,0:T(8,128)S(1)}, f32[88,128]{1,0:T(8,128)S(1)}, u32[]{:S(2)}, u32[]{:S(2)}) collective-permute-start(f32[88,128]{1,0:T(8,128)S(1)} %get-tuple-element.27), channel_id=1, source_target_pairs={{0,128},{128,0},{256,384},{384,256},{1,129},{129,1},{257,385},{385... | collective-permute-start | bytes 135176 | tf_op jit(solution)/shard_map/ppermute | solution.py:764
  26.4 10.2 %collective-permute-start.2 = (f32[144,128]{1,0:T(8,128)S(1)}, f32[144,128]{1,0:T(8,128)S(1)}, u32[]{:S(2)}, u32[]{:S(2)}) collective-permute-start(f32[144,128]{1,0:T(8,128)S(1)} %get-tuple-element.31), channel_id=1, source_target_pairs={{0,16},{16,0},{32,48},{48,32},{64,80},{80,64},{96,112},{112,96},{1... | collective-permute-start | bytes 221192 | tf_op jit(solution)/shard_map/ppermute | solution.py:764
  29.6 7.1 %collective-permute-start.3 = (f32[144,128]{1,0:T(8,128)S(1)}, f32[144,128]{1,0:T(8,128)S(1)}, u32[]{:S(2)}, u32[]{:S(2)}) collective-permute-start(f32[144,128]{1,0:T(8,128)S(1)} %get-tuple-element.32), channel_id=1, source_target_pairs={{0,112},{16,32},{32,16},{48,64},{64,48},{80,96},{96,80},{112,0},{1... | collective-permute-start | bytes 221192 | tf_op jit(solution)/shard_map/ppermute | solution.py:764
  34.5 19.6 %copy-start.5 = (bf16[3,128,128]{2,1,0:T(8,128)(2,1)S(1)}, bf16[3,128,128]{2,1,0:T(8,128)(2,1)}, u32[]{:S(2)}) copy-start(bf16[3,128,128]{2,1,0:T(8,128)(2,1)} %core_ref.3) | copy-start | bytes 294916
  36.8 11.2 %collective-permute-start.4 = (f32[456,128]{1,0:T(8,128)S(1)}, f32[456,128]{1,0:T(8,128)S(1)}, u32[]{:S(2)}, u32[]{:S(2)}) collective-permute-start(f32[456,128]{1,0:T(8,128)S(1)} %get-tuple-element.38), channel_id=1, source_target_pairs={{0,1},{1,0},{2,3},{3,2},{4,5},{5,4},{6,7},{7,6},{8,9},{9,8},{10,11... | collective-permute-start | bytes 700424 | tf_op jit(solution)/shard_map/ppermute | solution.py:764
  40.0 14.1 %collective-permute-start.5 = (f32[456,128]{1,0:T(8,128)S(1)}, f32[456,128]{1,0:T(8,128)S(1)}, u32[]{:S(2)}, u32[]{:S(2)}) collective-permute-start(f32[456,128]{1,0:T(8,128)S(1)} %get-tuple-element.39), channel_id=1, source_target_pairs={{0,15},{1,2},{2,1},{3,4},{4,3},{5,6},{6,5},{7,8},{8,7},{9,10},{10,... | collective-permute-start | bytes 700424 | tf_op jit(solution)/shard_map/ppermute | solution.py:764
  46.2 15.8 %collective-permute-start.6 = (f32[40,128]{1,0:T(8,128)S(1)}, f32[40,128]{1,0:T(8,128)S(1)}, u32[]{:S(2)}, u32[]{:S(2)}) collective-permute-start(f32[40,128]{1,0:T(8,128)S(1)} %get-tuple-element.44.topxy_ref), channel_id=1, source_target_pairs={{0,2},{1,15},{2,4},{3,1},{4,6},{5,3},{6,8},{7,5},{8,10},{9,7},{10,... | collective-permute-start | bytes 61448 | tf_op jit(solution)/shard_map/ppermute | solution.py:785
  48.1 13.9 %collective-permute-start.7 = (f32[72,128]{1,0:T(8,128)S(1)}, f32[72,128]{1,0:T(8,128)S(1)}, u32[]{:S(2)}, u32[]{:S(2)}) collective-permute-start(f32[72,128]{1,0:T(8,128)S(1)} %glue_z.1.pair_ref), channel_id=1, source_target_pairs={{0,3},{1,14},{2,5},{3,0},{4,7},{5,2},{6,9},{7,4},{8,11},{9,6},{10,... | collective-permute-start | bytes 110600 | tf_op jit(solution)/shard_map/ppermute | solution.py:764
  54.0 8.0 %copy-start.3 = (bf16[2,8,128,128]{3,2,1,0:T(8,128)(2,1)S(1)}, bf16[2,8,128,128]{3,2,1,0:T(8,128)(2,1)}, u32[]{:S(2)}) copy-start(bf16[2,8,128,128]{3,2,1,0:T(8,128)(2,1)} %down_ref.1) | copy-start | bytes 1572868
  54.0 8.0 %copy-start.6 = (f32[8,8,128]{2,1,0:T(8,128)S(1)}, f32[8,8,128]{2,1,0:T(8,128)}, u32[]{:S(2)}) copy-start(f32[8,8,128]{2,1,0:T(8,128)} %get-tuple-element.47.charge_ref) | copy-start | bytes 98308

commit v8 on v7

--- a/solution.py
+++ b/solution.py
@@ -496,8 +496,8 @@
                 axis=0,
             )
     def products(operand_ref, core):
-        rows = 384
-        return [dot(operand_ref[i * rows : i * rows + rows, :], core) for i in range(4)]
+        rows = 192
+        return [dot(operand_ref[i * rows : i * rows + rows, :], core) for i in range(8)]
 
     far0_ref[...] = jnp.zeros((8, 32, 128), F32)
     core0 = core_ref[0]
@@ -529,7 +529,7 @@
                     row = row_of(qx, qy, qz, pair, cz)
                     scale = jnp.broadcast_to(out_ref[0, pl.ds(row, 1), :], (32, 128))
                     start = ((pair * 2 + cz) * 6 + qy) * 32
-                    total = total + scale * image[start // 384][start % 384 : start % 384 + 32]
+                    total = total + scale * image[start // 192][start % 192 : start % 192 + 32]
                 far0_ref[pair * 2 + cz] = total
 
     build_leaf(0, even_ref)
@@ -566,7 +566,7 @@
                     scale = tout_ref[cz, (qx + 1 - pair // 2) * 7 + qy + 1 - pair % 2]
                     scale = jnp.concatenate([scale] * 4, axis=0)
                     start = ((pair * 2 + cz) * 6 + qy) * 32
-                    total = total + scale * image[start // 384][start % 384 : start % 384 + 32]
+                    total = total + scale * image[start // 192][start % 192 : start % 192 + 32]
                 acc_ref[pair * 2 + cz] = total
 
     build_mid(0, even_ref)

time: 98.1 us -> 98.3 us (level)
  no operation moved by 1% of the time
where the time goes in v8:
time: 98.3 us; the launch traced here: 98 us
  starting transfers between devices  35.3 us (36%)
  blocking collectives  31.8 us (32%)
  Pallas kernels  24.1 us (25%)
  waiting for transfers between devices  4.96 us (5%)
    ppermute x7, starting transfers between devices, swapped(): return lax.ppermute(value, axis, pairs)  33.4 us
    all_to_all x1, blocking collectives, shards(): rows = lax.all_to_all(share, ('gx', 'gy', 'gz'), 0, 0, tiled=True)  31.8 us
    pallas_call x1, Pallas kernels, run_far(): pl.pallas_call(far_kernel, in_specs=[VMEM] * 9, out_specs=[VMEM] * 2, out...  8.24 us
    pallas_call x1, Pallas kernels, run_atoms(): pl.pallas_call(atoms_kernel, in_specs=[hbm] * 8, out_specs=[VMEM] * 3, ou...  7.44 us
    ppermute x7, waiting for transfers between devices, swapped(): return lax.ppermute(value, axis, pairs)  4.96 us
    pallas_call x1, Pallas kernels, run_forces(): pl.pallas_call(force_kernel, in_specs=[VMEM] * 15, out_specs=[VMEM] * 2,...  3.17 us
    pallas_call x1, Pallas kernels, run_sines(): pl.pallas_call(functools.partial(sines_kernel, start), in_specs=[VMEM] *...  2.09 us
    pallas_call x1, Pallas kernels, run_front(): pl.pallas_call(front_kernel, in_specs=[VMEM] * 4, out_specs=[VMEM] * 2, o...  2.09 us
  transfers between devices with their start and end apart: 8, of which 3 were waited for; matrix products, arithmetic and copies ran while one was open for 0% of the time, Pallas kernels for 13%

profile of v8, /device:TPU:1, one launch (start us, length us, event | category | flops | bytes accessed | tf_op | source)
XLA Modules:
  0.0 98.0 jit_solution(14777135728113331351)
XLA Ops:
  0.6 0.0 copy-start.7
  0.6 0.0 copy-start.4
  0.7 0.0 copy-start.8
  0.7 0.0 copy-start.1
  0.7 7.4 %atoms.1 = (f32[8,8,128]{2,1,0:T(8,128)}, f32[296,128]{1,0:T(8,128)}, f32[88,128]{1,0:T(8,128)}) custom-call(bf16[8,8,128,128]{3,2,1,0:T(8,128)(2,1)} %feat_hbm.1, f32[3,8,8,128]{3,2,1,0:T(8,128)} %pos_ref.5, s32[8,4,8]{2,1,0:T(4,128)} %bitcast.12, bf16[128,128]{1,0:T(8,128)(2,1)} %wh_hbm.1, bf16[1,128]{1,0:T(2,128)(2,1)} %bitcast.13, f32[3,128]{1,0:T(4,128)} %wave_ref.5, ...), custom_call_target="tpu_custom_call" | custom-call | tf_op jit(solution)/shard_map/atoms/pallas_call | solution.py:262
  8.1 12.0 %collective-permute-start.1 = (f32[88,128]{1,0:T(8,128)}, f32[88,128]{1,0:T(8,128)S(1)}, u32[]{:S(2)}, u32[]{:S(2)}) collective-permute-start(f32[88,128]{1,0:T(8,128)} %get-tuple-element.28), channel_id=1, source_target_pairs={{0,384},{128,256},{256,128},{384,0},{1,385},{129,257},{257,129},{3... | collective-permute-start | bytes 135176 | tf_op jit(solution)/shard_map/ppermute | solution.py:764
  20.2 0.9 copy-done
  21.1 2.1 %front.1 = (bf16[4,128,1024]{2,1,0:T(8,128)(2,1)S(1)}, f32[88,128]{1,0:T(8,128)S(1)}) custom-call(f32[3,8,8,128]{3,2,1,0:T(8,128)S(1)} %copy-done.4, f32[3,128]{1,0:T(4,128)S(1)} %copy-done.7, f32[1,128]{1,0:T(1,128)S(1)} %bitcast.10, f32[296,128]{1,0:T(8,128)S(1)} %copy-done), custom_call_target="tpu_custom_call" | custom-call | flops 1073741824 | bytes 6291456 | tf_op jit(solution)/shard_map/front/pallas_call | solution.py:87
  23.2 1.9 %collective-permute-start = (f32[88,128]{1,0:T(8,128)S(1)}, f32[88,128]{1,0:T(8,128)S(1)}, u32[]{:S(2)}, u32[]{:S(2)}) collective-permute-start(f32[88,128]{1,0:T(8,128)S(1)} %get-tuple-element.27), channel_id=1, source_target_pairs={{0,128},{128,0},{256,384},{384,256},{1,129},{129,1},{257,385},{385... | collective-permute-start | bytes 135176 | tf_op jit(solution)/shard_map/ppermute | solution.py:764
  25.1 0.1 tables.1
  25.3 0.0 collective-permute-done.1.rb_ref
  25.3 1.0 %collective-permute-done.ra_ref = f32[88,128]{1,0:T(8,128)S(1)} collective-permute-done((f32[88,128]{1,0:T(8,128)S(1)}, f32[88,128]{1,0:T(8,128)S(1)}, u32[]{:S(2)}, u32[]{:S(2)}) %collective-permute-start) | collective-permute-done | bytes 45088 | tf_op jit(solution)/shard_map/ppermute | solution.py:764
  26.3 0.1 glue_x.1
  26.4 3.2 %collective-permute-start.2 = (f32[144,128]{1,0:T(8,128)S(1)}, f32[144,128]{1,0:T(8,128)S(1)}, u32[]{:S(2)}, u32[]{:S(2)}) collective-permute-start(f32[144,128]{1,0:T(8,128)S(1)} %get-tuple-element.31), channel_id=1, source_target_pairs={{0,16},{16,0},{32,48},{48,32},{64,80},{80,64},{96,112},{112,96},{1... | collective-permute-start | bytes 221192 | tf_op jit(solution)/shard_map/ppermute | solution.py:764
  29.6 4.9 %collective-permute-start.3 = (f32[144,128]{1,0:T(8,128)S(1)}, f32[144,128]{1,0:T(8,128)S(1)}, u32[]{:S(2)}, u32[]{:S(2)}) collective-permute-start(f32[144,128]{1,0:T(8,128)S(1)} %get-tuple-element.32), channel_id=1, source_target_pairs={{0,112},{16,32},{32,16},{48,64},{64,48},{80,96},{96,80},{112,0},{1... | collective-permute-start | bytes 221192 | tf_op jit(solution)/shard_map/ppermute | solution.py:764
  34.5 0.0 copy-start.5
  34.5 2.1 %sines.1._.back_ref = bf16[4,128,1024]{2,1,0:T(8,128)(2,1)S(1)} custom-call(f32[3,8,8,128]{3,2,1,0:T(8,128)S(1)} %copy-done.4, f32[3,128]{1,0:T(4,128)S(1)} %copy-done.7, f32[1,128]{1,0:T(1,128)S(1)} %bitcast.11, f32[16,128]{1,0:T(8,128)S(1)} %get-tuple-element.35._.topx_ref), custom_call_target="tpu_custom_call" | custom-call | flops 1073741824 | bytes 6291456 | tf_op jit(solution)/shard_map/sines/pallas_call | solution.py:103
  36.6 0.0 collective-permute-done.2.ra_ref
  36.6 0.1 collective-permute-done.3.rb_ref
  36.7 0.1 glue_y.1
  36.8 3.1 %collective-permute-start.4 = (f32[456,128]{1,0:T(8,128)S(1)}, f32[456,128]{1,0:T(8,128)S(1)}, u32[]{:S(2)}, u32[]{:S(2)}) collective-permute-start(f32[456,128]{1,0:T(8,128)S(1)} %get-tuple-element.38), channel_id=1, source_target_pairs={{0,1},{1,0},{2,3},{3,2},{4,5},{5,4},{6,7},{7,6},{8,9},{9,8},{10,11... | collective-permute-start | bytes 700424 | tf_op jit(solution)/shard_map/ppermute | solution.py:764
  40.0 6.2 %collective-permute-start.5 = (f32[456,128]{1,0:T(8,128)S(1)}, f32[456,128]{1,0:T(8,128)S(1)}, u32[]{:S(2)}, u32[]{:S(2)}) collective-permute-start(f32[456,128]{1,0:T(8,128)S(1)} %get-tuple-element.39), channel_id=1, source_target_pairs={{0,15},{1,2},{2,1},{3,4},{4,3},{5,6},{6,5},{7,8},{8,7},{9,10},{10,... | collective-permute-start | bytes 700424 | tf_op jit(solution)/shard_map/ppermute | solution.py:764
  46.2 1.9 %collective-permute-start.6 = (f32[40,128]{1,0:T(8,128)S(1)}, f32[40,128]{1,0:T(8,128)S(1)}, u32[]{:S(2)}, u32[]{:S(2)}) collective-permute-start(f32[40,128]{1,0:T(8,128)S(1)} %get-tuple-element.44.topxy_ref), channel_id=1, source_target_pairs={{0,2},{1,15},{2,4},{3,1},{4,6},{5,3},{6,8},{7,5},{8,10},{9,7},{10,... | collective-permute-start | bytes 61448 | tf_op jit(solution)/shard_map/ppermute | solution.py:785
  48.1 0.0 collective-permute-done.4.ra_ref
  48.1 2.1 %collective-permute-start.7 = (f32[72,128]{1,0:T(8,128)S(1)}, f32[72,128]{1,0:T(8,128)S(1)}, u32[]{:S(2)}, u32[]{:S(2)}) collective-permute-start(f32[72,128]{1,0:T(8,128)S(1)} %glue_z.1.pair_ref), channel_id=1, source_target_pairs={{0,3},{1,14},{2,5},{3,0},{4,7},{5,2},{6,9},{7,4},{8,11},{9,6},{10,... | collective-permute-start | bytes 110600 | tf_op jit(solution)/shard_map/ppermute | solution.py:764
  50.2 3.8 %collective-permute-done.5.rb_ref.side_ref = f32[456,128]{1,0:T(8,128)S(1)} collective-permute-done((f32[456,128]{1,0:T(8,128)S(1)}, f32[456,128]{1,0:T(8,128)S(1)}, u32[]{:S(2)}, u32[]{:S(2)}) %collective-permute-start.5) | collective-permute-done | bytes 233504 | tf_op jit(solution)/shard_map/ppermute | solution.py:764
  54.0 8.2 %far.1 = (f32[8,32,128]{2,1,0:T(8,128)S(1)}, f32[32,128]{1,0:T(8,128)S(1)}) custom-call(f32[12,4,12,128]{3,2,1,0:T(8,128)S(1)} %get-tuple-element.36.leafxy_ref, f32[8,8,2,128]{3,2,1,0:T(2,128)S(1)} %get-tuple-element.37.midxy_ref, f32[456,128]{1,0:T(8,128)S(1)} %collective-permute-done.4.ra_ref, f32[456,128]{1,0:T(8,128)S(1)} %collective-permute-done.5.rb_ref.side_ref, ...), custom_call_target="tpu_custom_call" | custom-call | flops 4294967296 | bytes 4194304 | tf_op jit(solution)/shard_map/far/pallas_call | solution.py:592
  62.3 0.0 collective-permute-done.6.far_ref
  62.3 0.0 collective-permute-done.7.next_ref
  62.3 3.2 %forces.1 = (f32[3,8,8,128]{3,2,1,0:T(8,128)}, f32[512,128]{1,0:T(8,128)S(1)}) custom-call(f32[8,32,128]{2,1,0:T(8,128)S(1)} %get-tuple-element.42.far0_ref, f32[32,128]{1,0:T(8,128)S(1)} %get-tuple-element.43.far1_ref, f32[72,128]{1,0:T(8,128)S(1)} %glue_z.1.pair_ref, f32[456,128]{1,0:T(8,128)S(1)} %collective-permute-done.5.rb_ref.side_ref, ...), custom_call_target="tpu_custom_call" | custom-call | tf_op jit(solution)/shard_map/forces/pallas_call | solution.py:722
  65.5 31.8 %all_to_all.11 = f32[512,1,128]{2,1,0:T(1,128)S(1)} all-to-all(f32[512,1,128]{2,1,0:T(1,128)S(1)} %bitcast.8), channel_id=1, replica_groups=mesh['gx'=4,'gy'=8,'gz'=16] {'gx','gy','gz'}, dimensions={0} | all-to-all | bytes 524288 | tf_op jit(solution)/shard_map/all_to_all | solution.py:795
  97.3 0.7 virial.1
  (13 shorter events, 0.0 us)
Async XLA Ops:
  0.6 19.5 %copy-start.7 = (f32[3,128]{1,0:T(4,128)S(1)}, f32[3,128]{1,0:T(4,128)}, u32[]{:S(2)}) copy-start(f32[3,128]{1,0:T(4,128)} %wave_ref.5) | copy-start | bytes 4612
  0.6 19.5 %copy-start.4 = (f32[3,8,8,128]{3,2,1,0:T(8,128)S(1)}, f32[3,8,8,128]{3,2,1,0:T(8,128)}, u32[]{:S(2)}) copy-start(f32[3,8,8,128]{3,2,1,0:T(8,128)} %pos_ref.5) | copy-start | bytes 294916
  0.7 19.5 %copy-start.8 = (f32[128]{0:T(128)S(1)}, f32[128]{0:T(128)}, u32[]{:S(2)}) copy-start(f32[128]{0:T(128)} %param.18) | copy-start | bytes 1540
  0.7 24.5 %copy-start.1 = (f32[3,343,128]{2,1,0:T(8,128)S(1)}, f32[3,343,128]{2,1,0:T(8,128)}, u32[]{:S(2)}) copy-start(f32[3,343,128]{2,1,0:T(8,128)} %in_ref.1) | copy-start | bytes 1580548
  0.7 24.5 %copy-start.2 = (f32[3,343,128]{2,1,0:T(8,128)S(1)}, f32[3,343,128]{2,1,0:T(8,128)}, u32[]{:S(2)}) copy-start(f32[3,343,128]{2,1,0:T(8,128)} %out_ref.3) | copy-start | bytes 1580548
  8.1 17.2 %collective-permute-start.1 = (f32[88,128]{1,0:T(8,128)}, f32[88,128]{1,0:T(8,128)S(1)}, u32[]{:S(2)}, u32[]{:S(2)}) collective-permute-start(f32[88,128]{1,0:T(8,128)} %get-tuple-element.28), channel_id=1, source_target_pairs={{0,384},{128,256},{256,128},{384,0},{1,385},{129,257},{257,129},{3... | collective-permute-start | bytes 135176 | tf_op jit(solution)/shard_map/ppermute | solution.py:764
  20.2 0.9 copy-start
  23.2 3.1 %collective-permute-start = (f32[88,128]{1,0:T(8,128)S(1)}, f32[88,128]{1,0:T(8,128)S(1)}, u32[]{:S(2)}, u32[]{:S(2)}) collective-permute-start(f32[88,128]{1,0:T(8,128)S(1)} %get-tuple-element.27), channel_id=1, source_target_pairs={{0,128},{128,0},{256,384},{384,256},{1,129},{129,1},{257,385},{385... | collective-permute-start | bytes 135176 | tf_op jit(solution)/shard_map/ppermute | solution.py:764
  26.4 10.2 %collective-permute-start.2 = (f32[144,128]{1,0:T(8,128)S(1)}, f32[144,128]{1,0:T(8,128)S(1)}, u32[]{:S(2)}, u32[]{:S(2)}) collective-permute-start(f32[144,128]{1,0:T(8,128)S(1)} %get-tuple-element.31), channel_id=1, source_target_pairs={{0,16},{16,0},{32,48},{48,32},{64,80},{80,64},{96,112},{112,96},{1... | collective-permute-start | bytes 221192 | tf_op jit(solution)/shard_map/ppermute | solution.py:764
  29.6 7.1 %collective-permute-start.3 = (f32[144,128]{1,0:T(8,128)S(1)}, f32[144,128]{1,0:T(8,128)S(1)}, u32[]{:S(2)}, u32[]{:S(2)}) collective-permute-start(f32[144,128]{1,0:T(8,128)S(1)} %get-tuple-element.32), channel_id=1, source_target_pairs={{0,112},{16,32},{32,16},{48,64},{64,48},{80,96},{96,80},{112,0},{1... | collective-permute-start | bytes 221192 | tf_op jit(solution)/shard_map/ppermute | solution.py:764
  34.5 19.6 %copy-start.5 = (bf16[3,128,128]{2,1,0:T(8,128)(2,1)S(1)}, bf16[3,128,128]{2,1,0:T(8,128)(2,1)}, u32[]{:S(2)}) copy-start(bf16[3,128,128]{2,1,0:T(8,128)(2,1)} %core_ref.3) | copy-start | bytes 294916
  36.8 11.2 %collective-permute-start.4 = (f32[456,128]{1,0:T(8,128)S(1)}, f32[456,128]{1,0:T(8,128)S(1)}, u32[]{:S(2)}, u32[]{:S(2)}) collective-permute-start(f32[456,128]{1,0:T(8,128)S(1)} %get-tuple-element.38), channel_id=1, source_target_pairs={{0,1},{1,0},{2,3},{3,2},{4,5},{5,4},{6,7},{7,6},{8,9},{9,8},{10,11... | collective-permute-start | bytes 700424 | tf_op jit(solution)/shard_map/ppermute | solution.py:764
  40.0 14.1 %collective-permute-start.5 = (f32[456,128]{1,0:T(8,128)S(1)}, f32[456,128]{1,0:T(8,128)S(1)}, u32[]{:S(2)}, u32[]{:S(2)}) collective-permute-start(f32[456,128]{1,0:T(8,128)S(1)} %get-tuple-element.39), channel_id=1, source_target_pairs={{0,15},{1,2},{2,1},{3,4},{4,3},{5,6},{6,5},{7,8},{8,7},{9,10},{10,... | collective-permute-start | bytes 700424 | tf_op jit(solution)/shard_map/ppermute | solution.py:764
  46.2 16.1 %collective-permute-start.6 = (f32[40,128]{1,0:T(8,128)S(1)}, f32[40,128]{1,0:T(8,128)S(1)}, u32[]{:S(2)}, u32[]{:S(2)}) collective-permute-start(f32[40,128]{1,0:T(8,128)S(1)} %get-tuple-element.44.topxy_ref), channel_id=1, source_target_pairs={{0,2},{1,15},{2,4},{3,1},{4,6},{5,3},{6,8},{7,5},{8,10},{9,7},{10,... | collective-permute-start | bytes 61448 | tf_op jit(solution)/shard_map/ppermute | solution.py:785
  48.1 14.2 %collective-permute-start.7 = (f32[72,128]{1,0:T(8,128)S(1)}, f32[72,128]{1,0:T(8,128)S(1)}, u32[]{:S(2)}, u32[]{:S(2)}) collective-permute-start(f32[72,128]{1,0:T(8,128)S(1)} %glue_z.1.pair_ref), channel_id=1, source_target_pairs={{0,3},{1,14},{2,5},{3,0},{4,7},{5,2},{6,9},{7,4},{8,11},{9,6},{10,... | collective-permute-start | bytes 110600 | tf_op jit(solution)/shard_map/ppermute | solution.py:764
  54.0 8.3 %copy-start.3 = (bf16[2,8,128,128]{3,2,1,0:T(8,128)(2,1)S(1)}, bf16[2,8,128,128]{3,2,1,0:T(8,128)(2,1)}, u32[]{:S(2)}) copy-start(bf16[2,8,128,128]{3,2,1,0:T(8,128)(2,1)} %down_ref.1) | copy-start | bytes 1572868
  54.0 8.3 %copy-start.6 = (f32[8,8,128]{2,1,0:T(8,128)S(1)}, f32[8,8,128]{2,1,0:T(8,128)}, u32[]{:S(2)}) copy-start(f32[8,8,128]{2,1,0:T(8,128)} %get-tuple-element.47.charge_ref) | copy-start | bytes 98308
